TPU v7x, 32 devices: a whole 2x2x4 slice. The times are simulated.
32 devices in a mesh: dp: 4 (over z), fsdp: 8 (over y, x, core).
Axes of the slice: x: 2, y: 2, z: 4, core: 2. Of those that a mesh axis runs over, the one named last changes fastest.
Arguments:
- tokens: bfloat16 [4096, 1280], P(('dp', 'fsdp')), may hold values from -6 to 6
- out_grad: bfloat16 [4096, 1280], P(('dp', 'fsdp')), may hold values from -6 to 6
- segment_ids: int32 [4096], P(('dp', 'fsdp')), may hold values from 0 to 15, never falling along the last dimension, each value on 1 to 1024 neighbouring positions
- expert_ids: int32 [4096, 7], P(('dp', 'fsdp')), may hold values from 0 to 15, all different within a row; in each aligned block of 128 rows (0 to 127, 128 to 255, ...) at most 80 rows name the same one
- attn_gain: bfloat16 [1280], P(('dp', 'fsdp')), may hold values from 0.5 to 1.5
- ffn_gain: bfloat16 [1280], P(('dp', 'fsdp')), may hold values from 0.5 to 1.5
- w_qkv: bfloat16 [1280, 3840], P(('dp', 'fsdp')), may hold values from -0.15625 to 0.15625
- w_out: bfloat16 [1280, 1280], P(('dp', 'fsdp')), may hold values from -1.25 to 1.25
- w_router: bfloat16 [1280, 16], P(('dp', 'fsdp')), may hold values from -0.078125 to 0.078125
- w_shared_up: bfloat16 [1280, 1792], P(('dp', 'fsdp')), may hold values from -0.15625 to 0.15625
- w_shared_down: bfloat16 [896, 1280], P(('dp', 'fsdp')), may hold values from -0.1875 to 0.1875
- w_expert_up: bfloat16 [16, 1280, 1792], P('fsdp', 'dp'), may hold values from -0.15625 to 0.15625
- w_expert_down: bfloat16 [16, 896, 1280], P('fsdp', 'dp'), may hold values from -0.375 to 0.375
Outputs:
- block_out: bfloat16 [4096, 1280], P(('dp', 'fsdp'))
- tokens_grad: bfloat16 [4096, 1280], P(('dp', 'fsdp'))
- grad_attn_gain: float32 [1280], P(('dp', 'fsdp'))
- grad_ffn_gain: float32 [1280], P(('dp', 'fsdp'))
- grad_w_qkv: float32 [1280, 3840], P(('dp', 'fsdp'))
- grad_w_out: float32 [1280, 1280], P(('dp', 'fsdp'))
- grad_w_router: float32 [1280, 16], P(('dp', 'fsdp'))
- grad_w_shared_up: float32 [1280, 1792], P(('dp', 'fsdp'))
- grad_w_shared_down: float32 [896, 1280], P(('dp', 'fsdp'))
- grad_w_expert_up: float32 [16, 1280, 1792], P('fsdp', 'dp')
- grad_w_expert_down: float32 [16, 896, 1280], P('fsdp', 'dp')
Inputs may be any that keep to these rules, and one draw needn't show every extreme that they name: `expert_ids`: each token names 7 different routed experts. Among the tokens of one device no expert is named more than 80 times, and in every draw some expert is named exactly 80 times by one device's tokens. `segment_ids`: document numbers never fall along the tokens; a document holds 1 to 1024 tokens and one holds exactly 1024.
All inputs are finite; a program needn't handle non-finite values.
Results may differ from a plain program's by a relative error of at most 0.024.
Values may be sent and summed in bfloat16 or wider, within the bound.
A program may use at most 256 MiB of HBM per device.

v0:
```python
import jax
import jax.numpy as jnp
from jax import lax
from jax.sharding import PartitionSpec as P

HEADS = 10
HEAD_DIM = 128
HIDDEN_SIZE = 896
SEQ = 1024


epsilon = 1e-06
rope_base = 10000.0


def rms_scale(values):
    return lax.rsqrt(jnp.mean(values * values, axis=-1, keepdims=True) + epsilon)


def rotary_tables(positions):
    half_dim = HEAD_DIM // 2
    freqs = rope_base ** (-jnp.arange(half_dim, dtype=jnp.float32) * 2.0 / HEAD_DIM)
    angles = positions.astype(jnp.float32)[:, None] * freqs[None, :]
    return (jnp.cos(angles)[:, None, :], jnp.sin(angles)[:, None, :])


def rotate(values, cosine_table, sine_table):
    half_dim = values.shape[-1] // 2
    front_half = values[..., :half_dim]
    back_half = values[..., half_dim:]
    return jnp.concatenate(
        [
            front_half * cosine_table - back_half * sine_table,
            back_half * cosine_table + front_half * sine_table,
        ],
        axis=-1,
    )


def unrotate(grads, cosine_table, sine_table):
    half_dim = grads.shape[-1] // 2
    front_half = grads[..., :half_dim]
    back_half = grads[..., half_dim:]
    return jnp.concatenate(
        [
            front_half * cosine_table + back_half * sine_table,
            back_half * cosine_table - front_half * sine_table,
        ],
        axis=-1,
    )


def inner_rows(left, right):
    return lax.dot_general(
        left, right, (((0,), (0,)), ((), ())), preferred_element_type=jnp.float32
    )


def times_transpose(left, right):
    return lax.dot_general(
        left, right, (((1,), (1,)), ((), ())), preferred_element_type=jnp.float32
    )


def swiglu_grad(grad_act, pre_values):
    gate_part = pre_values[..., :HIDDEN_SIZE]
    up_part = pre_values[..., HIDDEN_SIZE:]
    sigmoid_gate = jax.nn.sigmoid(gate_part)
    grad_gate = grad_act * up_part * sigmoid_gate * (1.0 + gate_part * (1.0 - sigmoid_gate))
    grad_up = grad_act * gate_part * sigmoid_gate
    return jnp.concatenate([grad_gate, grad_up], axis=-1).astype(jnp.bfloat16)


def key_allowed(query_pos, query_seg, key_pos, key_seg):
    causal = key_pos[None, :] <= query_pos[:, None]
    same_seq = key_pos[None, :] // SEQ == query_pos[:, None] // SEQ
    same_doc = key_seg[None, :] == query_seg[:, None]
    return causal & same_seq & same_doc


def norm_back(grad_normed, normal_rows, scale_rows, gain_rows):
    grad_scaled = grad_normed * gain_rows
    return scale_rows * (
        grad_scaled - normal_rows * jnp.mean(grad_scaled * normal_rows, axis=-1, keepdims=True)
    )


def local(
    tokens,
    out_grad,
    segment_ids,
    expert_ids,
    attn_gain,
    ffn_gain,
    w_qkv,
    w_out,
    w_router,
    w_shared_up,
    w_shared_down,
    w_expert_up,
    w_expert_down,
):
    row_count = tokens.shape[0]
    width = tokens.shape[1]
    top_k = expert_ids.shape[1]
    expert_count = w_router.shape[1]
    capacity = max(2, row_count * top_k * 3 // (2 * expert_count) // 8 * 8)
    score_scale = HEAD_DIM ** (-0.5)
    dense_full = (
        lax.all_gather(attn_gain, ("dp", "fsdp"), axis=0, tiled=True),
        lax.all_gather(ffn_gain, ("dp", "fsdp"), axis=0, tiled=True),
        lax.all_gather(w_qkv, ("dp", "fsdp"), axis=0, tiled=True),
        lax.all_gather(w_out, ("dp", "fsdp"), axis=0, tiled=True),
        lax.all_gather(w_router, ("dp", "fsdp"), axis=0, tiled=True),
        lax.all_gather(w_shared_up, ("dp", "fsdp"), axis=0, tiled=True),
        lax.all_gather(w_shared_down, ("dp", "fsdp"), axis=0, tiled=True),
    )
    gain_one, gain_two, full_qkv, full_out, full_router, full_sup, full_sdown = dense_full
    expert_full = (
        lax.all_gather(w_expert_up, "dp", axis=1, tiled=True),
        lax.all_gather(w_expert_down, "dp", axis=1, tiled=True),
    )
    exp_up, exp_down = expert_full
    inputs = tokens.astype(jnp.float32)
    scale_one = rms_scale(inputs)
    normal_one = inputs * scale_one
    normed_one = (normal_one * gain_one.astype(jnp.float32)).astype(jnp.bfloat16)
    qkv_proj = jnp.dot(normed_one, full_qkv, preferred_element_type=jnp.float32)
    local_pos = lax.axis_index("fsdp") * row_count + jnp.arange(row_count, dtype=jnp.int32)
    cosine_table, sine_table = rotary_tables(local_pos % SEQ)
    queries = rotate(
        qkv_proj[:, :width].reshape(row_count, HEADS, HEAD_DIM), cosine_table, sine_table
    ).astype(jnp.bfloat16)
    key_rows = (
        rotate(
            qkv_proj[:, width : 2 * width].reshape(row_count, HEADS, HEAD_DIM),
            cosine_table,
            sine_table,
        )
        .astype(jnp.bfloat16)
        .reshape(row_count, width)
    )
    value_rows = qkv_proj[:, 2 * width :].astype(jnp.bfloat16)
    row_max = jnp.full((HEADS, row_count), -1e30, jnp.float32)
    piece_keys = lax.all_gather(key_rows, "fsdp", axis=0, tiled=True)
    piece_values = lax.all_gather(value_rows, "fsdp", axis=0, tiled=True)
    piece_seg = lax.all_gather(segment_ids, "fsdp", axis=0, tiled=True)
    piece_len = piece_keys.shape[0]
    key_pos = jnp.arange(piece_len, dtype=jnp.int32)
    allowed = key_allowed(local_pos, segment_ids, key_pos, piece_seg)
    scores = (
        jnp.einsum(
            "qhd,khd->hqk",
            queries,
            piece_keys.reshape(piece_len, HEADS, HEAD_DIM),
            preferred_element_type=jnp.float32,
        )
        * score_scale
    )
    scores = jnp.where(allowed[None], scores, -1e30)
    new_max = jnp.maximum(row_max, jnp.max(scores, axis=-1))
    weights = jnp.where(allowed[None], jnp.exp(scores - new_max[..., None]), 0.0)
    row_sum = jnp.sum(weights, axis=-1)
    weighted = jnp.einsum(
        "hqk,khd->qhd",
        weights.astype(jnp.bfloat16),
        piece_values.reshape(piece_len, HEADS, HEAD_DIM),
        preferred_element_type=jnp.float32,
    )
    row_max, row_sum, weighted = (new_max, row_sum, weighted)
    attn_full = weighted / jnp.transpose(row_sum)[:, :, None]
    log_total = row_max + jnp.log(row_sum)
    attn_low = attn_full.reshape(row_count, width).astype(jnp.bfloat16)
    mixed_rows = inputs + jnp.dot(attn_low, full_out, preferred_element_type=jnp.float32)
    scale_two = rms_scale(mixed_rows)
    normal_two = mixed_rows * scale_two
    normed_two = (normal_two * gain_two.astype(jnp.float32)).astype(jnp.bfloat16)
    logits = jnp.dot(normed_two, full_router, preferred_element_type=jnp.float32)
    chosen = jnp.take_along_axis(logits, expert_ids, axis=1)
    gate_probs = jax.nn.softmax(chosen, axis=-1)
    shared_pre = jnp.dot(normed_two, full_sup, preferred_element_type=jnp.float32)
    shared_act = (jax.nn.silu(shared_pre[:, :HIDDEN_SIZE]) * shared_pre[:, HIDDEN_SIZE:]).astype(
        jnp.bfloat16
    )
    shared_res = jnp.dot(shared_act, full_sdown, preferred_element_type=jnp.float32)
    flat_ids = expert_ids.reshape(-1)
    route_marks = (flat_ids[:, None] == jnp.arange(expert_count, dtype=jnp.int32)[None, :]).astype(
        jnp.int32
    )
    slot_rank = jnp.sum((jnp.cumsum(route_marks, axis=0) - 1) * route_marks, axis=1)
    slot_index = flat_ids * capacity + slot_rank
    slot_owner = (
        jnp.zeros((expert_count * capacity,), jnp.int32)
        .at[slot_index]
        .set(jnp.arange(row_count * top_k, dtype=jnp.int32) + 1)
    )
    filled = slot_owner > 0
    pair_index = jnp.maximum(slot_owner - 1, 0)
    source_row = pair_index // top_k
    send_rows = jnp.where(filled[:, None], normed_two[source_row], 0)
    received = lax.all_to_all(
        send_rows.reshape(expert_count, capacity, width),
        "fsdp",
        split_axis=0,
        concat_axis=1,
        tiled=True,
    )
    expert_pre = jnp.einsum("erd,edf->erf", received, exp_up, preferred_element_type=jnp.float32)
    expert_act = (
        jax.nn.silu(expert_pre[..., :HIDDEN_SIZE]) * expert_pre[..., HIDDEN_SIZE:]
    ).astype(jnp.bfloat16)
    expert_out = jnp.einsum(
        "erf,efd->erd", expert_act, exp_down, preferred_element_type=jnp.float32
    ).astype(jnp.bfloat16)
    returned = lax.all_to_all(expert_out, "fsdp", split_axis=1, concat_axis=0, tiled=True).reshape(
        expert_count * capacity, width
    )
    routed_rows = returned[slot_index].reshape(row_count, top_k, width).astype(jnp.float32)
    routed = jnp.sum(gate_probs[:, :, None] * routed_rows, axis=1)
    block_out = (mixed_rows + shared_res + routed).astype(jnp.bfloat16)
    dense_full = (
        lax.all_gather(attn_gain, ("dp", "fsdp"), axis=0, tiled=True),
        lax.all_gather(ffn_gain, ("dp", "fsdp"), axis=0, tiled=True),
        lax.all_gather(w_qkv, ("dp", "fsdp"), axis=0, tiled=True),
        lax.all_gather(w_out, ("dp", "fsdp"), axis=0, tiled=True),
        lax.all_gather(w_router, ("dp", "fsdp"), axis=0, tiled=True),
        lax.all_gather(w_shared_up, ("dp", "fsdp"), axis=0, tiled=True),
        lax.all_gather(w_shared_down, ("dp", "fsdp"), axis=0, tiled=True),
    )
    gain_one, gain_two, full_qkv, full_out, full_router, full_sup, full_sdown = dense_full
    expert_full = (
        lax.all_gather(w_expert_up, "dp", axis=1, tiled=True),
        lax.all_gather(w_expert_down, "dp", axis=1, tiled=True),
    )
    exp_up, exp_down = expert_full
    grad_full = out_grad.astype(jnp.float32)
    grad_sdown = inner_rows(shared_act, out_grad)
    grad_shared_act = times_transpose(out_grad, full_sdown)
    grad_shared_pre = swiglu_grad(grad_shared_act, shared_pre)
    grad_sup = inner_rows(normed_two, grad_shared_pre)
    grad_normed = times_transpose(grad_shared_pre, full_sup)
    grad_gates = jnp.sum(grad_full[:, None, :] * routed_rows, axis=-1)
    grad_chosen = gate_probs * (
        grad_gates - jnp.sum(gate_probs * grad_gates, axis=-1, keepdims=True)
    )
    expert_marks = (
        expert_ids[:, :, None] == jnp.arange(expert_count, dtype=jnp.int32)[None, None, :]
    )
    grad_logits = jnp.sum(jnp.where(expert_marks, grad_chosen[:, :, None], 0.0), axis=1).astype(
        jnp.bfloat16
    )
    grad_router = inner_rows(normed_two, grad_logits)
    grad_normed = grad_normed + times_transpose(grad_logits, full_router)
    flat_gates = gate_probs.reshape(-1)
    grad_send = jnp.where(
        filled[:, None], flat_gates[pair_index][:, None] * grad_full[source_row], 0.0
    ).astype(jnp.bfloat16)
    grad_received = lax.all_to_all(
        grad_send.reshape(expert_count, capacity, width),
        "fsdp",
        split_axis=0,
        concat_axis=1,
        tiled=True,
    )
    expert_pre = jnp.einsum("erd,edf->erf", received, exp_up, preferred_element_type=jnp.float32)
    expert_act = (
        jax.nn.silu(expert_pre[..., :HIDDEN_SIZE]) * expert_pre[..., HIDDEN_SIZE:]
    ).astype(jnp.bfloat16)
    grad_exp_down = jnp.einsum(
        "erf,erd->efd", expert_act, grad_received, preferred_element_type=jnp.float32
    )
    grad_expert_act = jnp.einsum(
        "erd,efd->erf", grad_received, exp_down, preferred_element_type=jnp.float32
    )
    grad_expert_pre = swiglu_grad(grad_expert_act, expert_pre)
    grad_exp_up = jnp.einsum(
        "erd,erf->edf", received, grad_expert_pre, preferred_element_type=jnp.float32
    )
    grad_in_rows = jnp.einsum(
        "erf,edf->erd", grad_expert_pre, exp_up, preferred_element_type=jnp.float32
    ).astype(jnp.bfloat16)
    expert_up_grad, expert_down_grad = (
        lax.psum_scatter(
            grad_exp_up.astype(jnp.bfloat16), "dp", scatter_dimension=1, tiled=True
        ).astype(jnp.float32),
        lax.psum_scatter(
            grad_exp_down.astype(jnp.bfloat16), "dp", scatter_dimension=1, tiled=True
        ).astype(jnp.float32),
    )
    grad_back = lax.all_to_all(
        grad_in_rows, "fsdp", split_axis=1, concat_axis=0, tiled=True
    ).reshape(expert_count * capacity, width)
    grad_normed = grad_normed + jnp.sum(
        grad_back[slot_index].reshape(row_count, top_k, width).astype(jnp.float32), axis=1
    )
    grad_gain_two = jnp.sum(grad_normed * normal_two, axis=0)
    grad_mixed = grad_full + norm_back(
        grad_normed, normal_two, scale_two, gain_two.astype(jnp.float32)
    )
    grad_mixed_low = grad_mixed.astype(jnp.bfloat16)
    grad_wout = inner_rows(attn_low, grad_mixed_low)
    grad_attn = (
        times_transpose(grad_mixed_low, full_out)
        .astype(jnp.bfloat16)
        .reshape(row_count, HEADS, HEAD_DIM)
    )
    row_delta = jnp.einsum("qhd,qhd->hq", grad_attn.astype(jnp.float32), attn_full)
    piece_keys = lax.all_gather(key_rows, "fsdp", axis=0, tiled=True)
    piece_values = lax.all_gather(value_rows, "fsdp", axis=0, tiled=True)
    piece_seg = lax.all_gather(segment_ids, "fsdp", axis=0, tiled=True)
    piece_len = piece_keys.shape[0]
    keys_three = piece_keys.reshape(piece_len, HEADS, HEAD_DIM)
    values_three = piece_values.reshape(piece_len, HEADS, HEAD_DIM)
    key_pos = jnp.arange(piece_len, dtype=jnp.int32)
    allowed = key_allowed(local_pos, segment_ids, key_pos, piece_seg)
    scores = (
        jnp.einsum("qhd,khd->hqk", queries, keys_three, preferred_element_type=jnp.float32)
        * score_scale
    )
    prob_rows = jnp.where(allowed[None], jnp.exp(scores - log_total[..., None]), 0.0)
    grad_probs = jnp.einsum(
        "qhd,khd->hqk", grad_attn, values_three, preferred_element_type=jnp.float32
    )
    grad_scores = (prob_rows * (grad_probs - row_delta[..., None])).astype(jnp.bfloat16)
    grad_queries = (
        jnp.einsum("hqk,khd->qhd", grad_scores, keys_three, preferred_element_type=jnp.float32)
        * score_scale
    )
    piece_gkey = (
        jnp.einsum("hqk,qhd->khd", grad_scores, queries, preferred_element_type=jnp.float32)
        * score_scale
    )
    piece_gval = jnp.einsum(
        "hqk,qhd->khd",
        prob_rows.astype(jnp.bfloat16),
        grad_attn,
        preferred_element_type=jnp.float32,
    )
    piece_grad = jnp.concatenate(
        [piece_gkey.reshape(piece_len, width), piece_gval.reshape(piece_len, width)], axis=-1
    )
    grad_keyvals = piece_grad
    grad_queries, grad_keyvals = (grad_queries, grad_keyvals)
    grad_keyvals_own = lax.psum_scatter(
        grad_keyvals.astype(jnp.bfloat16), "fsdp", scatter_dimension=0, tiled=True
    ).astype(jnp.float32)
    grad_keys = unrotate(
        grad_keyvals_own[:, :width].reshape(row_count, HEADS, HEAD_DIM), cosine_table, sine_table
    ).reshape(row_count, width)
    grad_values = grad_keyvals_own[:, width:]
    grad_query_rows = unrotate(grad_queries, cosine_table, sine_table).reshape(row_count, width)
    grad_qkv = jnp.concatenate([grad_query_rows, grad_keys, grad_values], axis=-1).astype(
        jnp.bfloat16
    )
    grad_wqkv = inner_rows(normed_one, grad_qkv)
    grad_normed_one = times_transpose(grad_qkv, full_qkv)
    grad_gain_one = jnp.sum(grad_normed_one * normal_one, axis=0)
    tokens_grad = (
        grad_mixed + norm_back(grad_normed_one, normal_one, scale_one, gain_one.astype(jnp.float32))
    ).astype(jnp.bfloat16)
    dense_sums = (
        lax.psum_scatter(grad_gain_one, ("dp", "fsdp"), scatter_dimension=0, tiled=True),
        lax.psum_scatter(grad_gain_two, ("dp", "fsdp"), scatter_dimension=0, tiled=True),
        lax.psum_scatter(grad_wqkv, ("dp", "fsdp"), scatter_dimension=0, tiled=True),
        lax.psum_scatter(grad_wout, ("dp", "fsdp"), scatter_dimension=0, tiled=True),
        lax.psum_scatter(grad_router, ("dp", "fsdp"), scatter_dimension=0, tiled=True),
        lax.psum_scatter(grad_sup, ("dp", "fsdp"), scatter_dimension=0, tiled=True),
        lax.psum_scatter(grad_sdown, ("dp", "fsdp"), scatter_dimension=0, tiled=True),
    )
    return (
        block_out,
        tokens_grad,
        dense_sums[0],
        dense_sums[1],
        dense_sums[2],
        dense_sums[3],
        dense_sums[4],
        dense_sums[5],
        dense_sums[6],
        expert_up_grad,
        expert_down_grad,
    )


def solution(mesh):
    in_specs = (
        P(("dp", "fsdp"), None),
        P(("dp", "fsdp"), None),
        P(("dp", "fsdp")),
        P(("dp", "fsdp"), None),
        P(("dp", "fsdp")),
        P(("dp", "fsdp")),
        P(("dp", "fsdp"), None),
        P(("dp", "fsdp"), None),
        P(("dp", "fsdp"), None),
        P(("dp", "fsdp"), None),
        P(("dp", "fsdp"), None),
        P("fsdp", "dp", None),
        P("fsdp", "dp", None),
    )
    out_specs = (
        P(("dp", "fsdp"), None),
        P(("dp", "fsdp"), None),
        P(("dp", "fsdp")),
        P(("dp", "fsdp")),
        P(("dp", "fsdp"), None),
        P(("dp", "fsdp"), None),
        P(("dp", "fsdp"), None),
        P(("dp", "fsdp"), None),
        P(("dp", "fsdp"), None),
        P("fsdp", "dp", None),
        P("fsdp", "dp", None),
    )
    return jax.shard_map(local, mesh=mesh, in_specs=in_specs, out_specs=out_specs, check_vma=False)
```

profile of v0, /device:TPU:11, one launch (start us, length us, event | category | flops | bytes accessed | tf_op | source)
XLA Modules:
  0.0 1662.4 jit_solution(11114034225894690425)
XLA Ops:
  9.7 40.2 %all-reduce.8 = (bf16[1280]{0:T(1024)(128)(2,1)S(1)}, bf16[1280]{0:T(1024)(128)(2,1)S(1)}) all-reduce(bf16[1280]{0:T(1024)(128)(2,1)S(1)} %dynamic-update-slice, bf16[1280]{0:T(1024)(128)(2,1)S(1)} %dynamic-update-slice.1), channel_id=1, replica_groups=mesh['dp'=4,'fsdp'=8] {'dp','fsdp'}, use_global_device_ids=true, to_apply=%add | all-reduce | flops 2560 | bytes 10240
  51.4 45.7 %all-gather.12.cloned.1.call-done = bf16[1280,3840]{1,0:T(8,128)(2,1)} async-done(((bf16[40,3840]{1,0:T(8,128)(2,1)}), bf16[1280,3840]{1,0:T(8,128)(2,1)}) %all-gather.12.cloned.1.call-update) | async-done | bytes 9830416 | tf_op jit(solution)/shard_map/all_gather | solution.py:112
  97.1 5.4 fusion.53
  123.0 5.3 scatter_custom_fusion
  128.3 7.9 all-gather
  136.2 32.2 %all-gather.2 = bf16[32,40,16]{1,2,0:T(8,128)(2,1)S(1)} all-gather(bf16[1,40,16]{1,2,0:T(8,128)(2,1)S(1)} %bitcast.148), channel_id=1, replica_groups=mesh['dp'=4,'fsdp'=8] {'dp','fsdp'}, dimensions={0}, use_global_device_ids=true | all-gather | bytes 42240 | tf_op jit(solution)/shard_map/all_gather | solution.py:114
  169.1 5.7 gather_fusion.3
  186.7 5.9 fusion.91
  192.7 47.1 %all-gather.18.cloned.1.call-done = bf16[1280,1280]{1,0:T(8,128)(2,1)} async-done(((bf16[40,1280]{1,0:T(8,128)(2,1)}), bf16[1280,1280]{1,0:T(8,128)(2,1)}) %all-gather.18.cloned.1.call-update) | async-done | bytes 3276816 | tf_op jit(solution)/shard_map/all_gather | solution.py:113
  242.7 6.0 gather_fusion.5
  249.4 5.0 gather_fusion.2
  254.4 4.6 select_convert_fusion
  259.1 4.8 all-to-all-start.2
  263.9 5.3 gather_fusion
  273.1 28.6 %all-to-all-done.2 = bf16[16,80,1280]{2,1,0:T(8,128)(2,1)} async-done(((bf16[16,80,1280]{2,1,0:T(8,128)(2,1)}), bf16[16,80,1280]{2,1,0:T(8,128)(2,1)}, u32[]{:S(2)}, u32[]{:S(2)}) %all-to-all-start.2) | async-done | bytes 3276832 | tf_op jit(solution)/shard_map/all_to_all | solution.py:258
  301.7 6.0 all-to-all-start
  312.2 33.3 %all-to-all-done = bf16[16,80,1280]{2,1,0:T(8,128)(2,1)} async-done(((bf16[16,80,1280]{2,1,0:T(8,128)(2,1)}), bf16[16,80,1280]{2,1,0:T(8,128)(2,1)}, u32[]{:S(2)}, u32[]{:S(2)}) %all-to-all-start) | async-done | bytes 3276832 | tf_op jit(solution)/shard_map/all_to_all | solution.py:201
  349.3 50.9 %all-gather.22.cloned.1.call-done = bf16[2,1280,1792]{2,1,0:T(8,128)(2,1)} async-done(((bf16[2,320,1792]{2,1,0:T(8,128)(2,1)}), bf16[2,1280,1792]{2,1,0:T(8,128)(2,1)}) %all-gather.22.cloned.1.call-update) | async-done | bytes 9175056 | tf_op jit(solution)/shard_map/all_gather | solution.py:120
  400.2 12.7 fusion.94
  412.9 74.5 %all-gather.24.cloned.1.call-done = bf16[2,896,1280]{2,1,0:T(8,128)(2,1)} async-done(((bf16[2,224,1280]{2,1,0:T(8,128)(2,1)}), bf16[2,896,1280]{2,1,0:T(8,128)(2,1)}) %all-gather.24.cloned.1.call-update) | async-done | bytes 4587536 | tf_op jit(solution)/shard_map/all_gather | solution.py:121
  487.3 13.2 multiply_convert_fusion.3
  504.3 5.1 copy.204
  509.4 5.2 all-to-all-start.1
  514.6 10.8 convolution_convert_fusion.2
  525.4 5.1 copy.210
  530.5 27.6 %all-to-all-done.1 = bf16[2,640,1280]{2,0,1:T(2,128)(2,1)} async-done(((bf16[2,640,1280]{2,0,1:T(2,128)(2,1)}), bf16[2,640,1280]{2,0,1:T(2,128)(2,1)}, u32[]{:S(2)}, u32[]{:S(2)}) %all-to-all-start.1) | async-done | bytes 3276832 | tf_op jit(solution)/shard_map/all_to_all | solution.py:215
  558.1 7.2 all-to-all-start.3
  569.5 63.1 %all-gather.20.cloned.1.call-done = bf16[1280,1792]{1,0:T(8,128)(2,1)} async-done(((bf16[40,1792]{1,0:T(8,128)(2,1)}), bf16[1280,1792]{1,0:T(8,128)(2,1)}) %all-gather.20.cloned.1.call-update) | async-done | bytes 4587536 | tf_op jit(solution)/shard_map/all_gather | solution.py:115
  644.9 8.7 gather_fusion.1
  658.2 4.9 multiply_reduce_fusion
  667.3 8.7 gather_fusion.4
  676.0 5.0 reshape.496
  705.1 7.9 copy.238
  713.9 8.5 convolution_convert_fusion.1
  722.6 13.7 convolution_convert_fusion
  737.3 4.9 fusion.47
  750.6 17.3 %reduce-scatter.22.cloned.1.call-done = bf16[128,2560]{1,0:T(8,128)(2,1)} async-done(((bf16[1024,2560]{1,0:T(8,128)(2,1)}), bf16[128,2560]{1,0:T(8,128)(2,1)}) %reduce-scatter.22.cloned.1.call-update) | async-done | bytes 655376
  781.5 9.4 fusion.45
  793.9 65.6 %fusion = f32[32,1280]{1,0:T(8,128)S(1)} fusion(f32[896,1280]{1,0:T(8,128)} %fusion.95), kind=kCustom, calls=%all-reduce-scatter | all-reduce-scatter fusion | flops 1310721 | bytes 4751360
  873.4 6.8 collective-permute-done.3
  880.2 8.3 concatenate.43
  895.7 86.7 %reduce-scatter.20.cloned.1.call-done = bf16[2,224,1280]{2,1,0:T(8,128)(2,1)} async-done(((bf16[2,896,1280]{2,1,0:T(8,128)(2,1)}), bf16[2,224,1280]{2,1,0:T(8,128)(2,1)}) %reduce-scatter.20.cloned.1.call-update) | async-done | bytes 1146896 | tf_op jit(solution)/shard_map/reduce_scatter | solution.py:286
  985.1 7.2 fusion.40
  992.4 43.9 %all-reduce.7 = (f32[1280]{0:T(1024)S(1)}, f32[1280]{0:T(1024)S(1)}) all-reduce(f32[1280]{0:T(1024)S(1)} %get-tuple-element.15, f32[1280]{0:T(1024)S(1)} %get-tuple-element.13), channel_id=3, replica_groups=mesh['dp'=4,'fsdp'=8] {'dp','fsdp'}, use_global_device_ids=true, to_apply=%region_19.20.clone | all-reduce | flops 2560 | bytes 20480
  1038.4 104.7 %reduce-scatter.18.cloned.1.call-done = bf16[2,320,1792]{2,1,0:T(8,128)(2,1)} async-done(((bf16[2,1280,1792]{2,1,0:T(8,128)(2,1)}), bf16[2,320,1792]{2,1,0:T(8,128)(2,1)}) %reduce-scatter.18.cloned.1.call-update) | async-done | bytes 2293776 | tf_op jit(solution)/shard_map/reduce_scatter | solution.py:283
  1147.3 122.5 %reduce-scatter.16.cloned.1.call-done = f32[40,1792]{1,0:T(8,128)} async-done(((f32[1280,1792]{1,0:T(8,128)}), f32[40,1792]{1,0:T(8,128)}) %reduce-scatter.16.cloned.1.call-update) | async-done | bytes 286736 | tf_op jit(solution)/shard_map/reduce_scatter | solution.py:367
  1269.8 143.3 %reduce-scatter.14.cloned.1.call-done = f32[40,1280]{1,0:T(8,128)} async-done(((f32[1280,1280]{1,0:T(8,128)}), f32[40,1280]{1,0:T(8,128)}) %reduce-scatter.14.cloned.1.call-update) | async-done | bytes 204816 | tf_op jit(solution)/shard_map/reduce_scatter | solution.py:365
  1413.1 242.5 %reduce-scatter.12.cloned.1.call-done = f32[40,3840]{1,0:T(8,128)} async-done(((f32[1280,3840]{1,0:T(8,128)}), f32[40,3840]{1,0:T(8,128)}) %reduce-scatter.12.cloned.1.call-update) | async-done | bytes 614416 | tf_op jit(solution)/shard_map/reduce_scatter | solution.py:364
  (229 shorter events, 162.7 us)
Async XLA Ops:
  7.2 89.9 %all-gather.12.cloned.1.call-start = ((), (), s32[]{:S(2)}) async-start(), calls=%async_computation.10 | async-start | bytes 10137600 | tf_op jit(solution)/shard_map/all_gather | solution.py:112
  7.9 167.2 %all-gather.16.cloned.1.call-start = ((), (), s32[]{:S(2)}) async-start(), calls=%async_computation.12 | async-start | bytes 2949120 | tf_op jit(solution)/shard_map/all_gather | solution.py:145
  49.9 47.2 %copy-start.25 = (f32[1280]{0:T(1024)}, f32[1280]{0:T(1024)S(1)}, u32[]{:S(2)}) copy-start(f32[1280]{0:T(1024)S(1)} %convert_element_type.123) | copy-start | bytes 15364
  51.0 46.0 %copy-start.28 = (f32[128]{0:T(128)}, f32[128]{0:T(128)S(1)}, u32[]{:S(2)}) copy-start(f32[128]{0:T(128)S(1)} %add_rsqrt_fusion.1) | copy-start | bytes 1540
  51.4 61.9 %copy-start.21 = (f32[128,64]{1,0:T(8,128)}, f32[128,64]{1,0:T(8,128)S(1)}, u32[]{:S(2)}) copy-start(f32[128,64]{1,0:T(8,128)S(1)} %get-tuple-element.51) | copy-start | bytes 98308
  51.4 61.9 %copy-start.23 = (f32[128,64]{1,0:T(8,128)}, f32[128,64]{1,0:T(8,128)S(1)}, u32[]{:S(2)}) copy-start(f32[128,64]{1,0:T(8,128)S(1)} %get-tuple-element.52) | copy-start | bytes 98308
  113.3 6.4 copy-start.27
  115.1 13.2 copy-start.31
  115.1 21.1 %copy-start.30 = (bf16[40,16]{0,1:T(8,128)(2,1)S(1)}, bf16[40,16]{0,1:T(8,128)(2,1)}, u32[]{:S(2)}) copy-start(bf16[40,16]{0,1:T(8,128)(2,1)} %param.21) | copy-start | bytes 3844
  115.2 53.8 %copy-start.6 = (bf16[128,1280]{1,0:T(8,128)(2,1)S(1)}, bf16[128,1280]{1,0:T(8,128)(2,1)}, u32[]{:S(2)}) copy-start(bf16[128,1280]{1,0:T(8,128)(2,1)} %param.14) | copy-start | bytes 983044
  116.3 66.0 %all-gather.14.cloned.1.call-start = ((), (), s32[]{:S(2)}) async-start(), calls=%async_computation.11 | async-start | bytes 2949120 | tf_op jit(solution)/shard_map/all_gather | solution.py:146
  117.1 122.6 %all-gather.18.cloned.1.call-start = ((), (), s32[]{:S(2)}) async-start(), calls=%async_computation.13 | async-start | bytes 3379200 | tf_op jit(solution)/shard_map/all_gather | solution.py:113
  117.7 282.5 %all-gather.22.cloned.1.call-start = ((), (), s32[]{:S(2)}) async-start(), calls=%async_computation.15 | async-start | bytes 11468800 | tf_op jit(solution)/shard_map/all_gather | solution.py:120
  118.3 369.0 %all-gather.24.cloned.1.call-start = ((), (), s32[]{:S(2)}) async-start(), calls=%async_computation.16 | async-start | bytes 5734400 | tf_op jit(solution)/shard_map/all_gather | solution.py:121
  118.9 446.5 %all-gather.26.cloned.1.call-start = ((), (), s32[]{:S(2)}) async-start(), calls=%async_computation.22 | async-start | bytes 2703360 | tf_op jit(solution)/shard_map/all_gather | solution.py:116
  186.7 53.0 %copy-start.4 = (bf16[128,1280]{1,0:T(8,128)(2,1)S(1)}, bf16[128,1280]{1,0:T(8,128)(2,1)}, u32[]{:S(2)}) copy-start(bf16[128,1280]{1,0:T(8,128)(2,1)} %param.13) | copy-start | bytes 983044
  192.7 56.1 %copy-start.9 = (bf16[128,10,128]{0,2,1:T(8,128)(2,1)}, bf16[128,10,128]{0,2,1:T(8,128)(2,1)S(1)}, u32[]{:S(2)}) copy-start(bf16[128,10,128]{0,2,1:T(8,128)(2,1)S(1)} %get-tuple-element.55) | copy-start | bytes 983044
  259.1 42.6 %all-to-all-start.2 = ((bf16[16,80,1280]{2,1,0:T(8,128)(2,1)}), bf16[16,80,1280]{2,1,0:T(8,128)(2,1)}, u32[]{:S(2)}, u32[]{:S(2)}) async-start(bf16[16,80,1280]{2,1,0:T(8,128)(2,1)} %select_convert_fusion), calls=%async_computation.2 | async-start | bytes 6553600 | tf_op jit(solution)/shard_map/all_to_all | solution.py:258
  301.7 43.8 %all-to-all-start = ((bf16[16,80,1280]{2,1,0:T(8,128)(2,1)}), bf16[16,80,1280]{2,1,0:T(8,128)(2,1)}, u32[]{:S(2)}, u32[]{:S(2)}) async-start(bf16[16,80,1280]{2,1,0:T(8,128)(2,1)} %broadcast_select_fusion), calls=%async_computation | async-start | bytes 6553600 | tf_op jit(solution)/shard_map/all_to_all | solution.py:201
  307.7 324.9 %all-gather.20.cloned.1.call-start = ((), (), s32[]{:S(2)}) async-start(), calls=%async_computation.14 | async-start | bytes 4730880 | tf_op jit(solution)/shard_map/all_gather | solution.py:115
  487.3 13.2 copy-start.32
  509.4 48.7 %all-to-all-start.1 = ((bf16[2,640,1280]{2,0,1:T(2,128)(2,1)}), bf16[2,640,1280]{2,0,1:T(2,128)(2,1)}, u32[]{:S(2)}, u32[]{:S(2)}) async-start(bf16[2,640,1280]{2,0,1:T(2,128)(2,1)} %copy.204), calls=%async_computation.1 | async-start | bytes 6553600 | tf_op jit(solution)/shard_map/all_to_all | solution.py:215
  558.1 105.1 %all-to-all-start.3 = ((bf16[2,640,1280]{2,0,1:T(2,128)(2,1)}), bf16[2,640,1280]{2,0,1:T(2,128)(2,1)}, u32[]{:S(2)}, u32[]{:S(2)}) async-start(bf16[2,640,1280]{2,0,1:T(2,128)(2,1)} %copy.210), calls=%async_computation.3 | async-start | bytes 6553600 | tf_op jit(solution)/shard_map/all_to_all | solution.py:290
  565.4 202.5 %reduce-scatter.22.cloned.1.call-start = ((), (), s32[]{:S(2)}) async-start(), calls=%async_computation.23 | async-start | bytes 5898240
  632.5 5.8 copy-start.1
  638.3 6.6 copy-start.17
  638.4 152.6 %copy-start.16 = (bf16[128,896]{1,0:T(8,128)(2,1)}, bf16[128,896]{1,0:T(8,128)(2,1)S(1)}, u32[]{:S(2)}) copy-start(bf16[128,896]{1,0:T(8,128)(2,1)S(1)} %get-tuple-element.34) | copy-start | bytes 688132
  713.0 181.2 %all-reduce.11.cloned.1.call-start = ((), (), s32[]{:S(2)}) async-start(), calls=%async_computation.24 | async-start | bytes 163840
  713.9 268.5 %reduce-scatter.20.cloned.1.call-start = ((), (), s32[]{:S(2)}) async-start(), calls=%async_computation.21 | async-start | bytes 5734400 | tf_op jit(solution)/shard_map/reduce_scatter | solution.py:286
  722.5 420.6 %reduce-scatter.18.cloned.1.call-start = ((), (), s32[]{:S(2)}) async-start(), calls=%async_computation.20 | async-start | bytes 11468800 | tf_op jit(solution)/shard_map/reduce_scatter | solution.py:283
  736.3 533.5 %reduce-scatter.16.cloned.1.call-start = ((), (), s32[]{:S(2)}) async-start(), calls=%async_computation.19 | async-start | bytes 9461760 | tf_op jit(solution)/shard_map/reduce_scatter | solution.py:367
  742.3 670.8 %reduce-scatter.14.cloned.1.call-start = ((), (), s32[]{:S(2)}) async-start(), calls=%async_computation.18 | async-start | bytes 6758400 | tf_op jit(solution)/shard_map/reduce_scatter | solution.py:365
  747.0 28.9 %copy-start.22 = (f32[128,64]{1,0:T(8,128)S(1)}, f32[128,64]{1,0:T(8,128)}, u32[]{:S(2)}) copy-start(f32[128,64]{1,0:T(8,128)} %copy-done.21) | copy-start | bytes 98308
  747.0 28.9 %copy-start.24 = (f32[128,64]{1,0:T(8,128)S(1)}, f32[128,64]{1,0:T(8,128)}, u32[]{:S(2)}) copy-start(f32[128,64]{1,0:T(8,128)} %copy-done.23) | copy-start | bytes 98308
  747.0 908.6 %reduce-scatter.12.cloned.1.call-start = ((), (), s32[]{:S(2)}) async-start(), calls=%async_computation.17 | async-start | bytes 20275200 | tf_op jit(solution)/shard_map/reduce_scatter | solution.py:364
  773.8 7.7 copy-start.5
  773.8 7.7 copy-start.26
  773.8 7.7 copy-start.29
  779.0 11.9 copy-start.11
  781.5 9.4 copy-start.14
  793.9 96.3 %copy-start.7 = (f32[128,1280]{1,0:T(8,128)S(1)}, f32[128,1280]{1,0:T(8,128)}, u32[]{:S(2)}) copy-start(f32[128,1280]{1,0:T(8,128)} %get-tuple-element.12) | copy-start | bytes 1966084
  859.5 20.7 %collective-permute-start = (f32[32,1280]{1,0:T(8,128)S(1)}, f32[32,1280]{1,0:T(8,128)}, u32[]{:S(2)}, u32[]{:S(2)}) collective-permute-start(f32[32,1280]{1,0:T(8,128)S(1)} %fusion), channel_id=1, source_target_pairs={{0,1},{1,2},{2,3},{3,4},{4,5},{5,6},{6,7},{7,8},{8,9},{9,10},{10,1... | collective-permute-start | bytes 491528
  864.0 16.2 collective-permute-start.1
  866.0 14.3 collective-permute-start.2
  870.7 9.5 collective-permute-start.3
  873.4 111.7 %copy-start.12 = (bf16[128,10,128]{0,2,1:T(8,128)(2,1)S(1)}, bf16[128,10,128]{0,2,1:T(8,128)(2,1)}, u32[]{:S(2)}) copy-start(bf16[128,10,128]{0,2,1:T(8,128)(2,1)} %copy-done.11) | copy-start | bytes 983044
  873.4 111.7 %copy-start.13 = (bf16[128,10,128]{0,2,1:T(8,128)(2,1)S(1)}, bf16[128,10,128]{0,2,1:T(8,128)(2,1)}, u32[]{:S(2)}) copy-start(bf16[128,10,128]{0,2,1:T(8,128)(2,1)} %copy.220) | copy-start | bytes 983044
  873.4 111.7 %copy-start.15 = (bf16[128,1280]{0,1:T(8,128)(2,1)S(1)}, bf16[128,1280]{0,1:T(8,128)(2,1)}, u32[]{:S(2)}) copy-start(bf16[128,1280]{0,1:T(8,128)(2,1)} %copy-done.14) | copy-start | bytes 983044
  (9 other events, 20.7 us)
Sparse Core Ops, SparseCore 0:
  10.9 86.1 all-gather.11
  116.4 29.2 all-gather.15
  148.2 30.2 all-gather.13
  181.2 58.5 all-gather.17
  241.2 158.9 all-gather.21
  401.6 85.6 all-gather.23
  490.2 73.0 all-gather.25
  566.1 66.3 all-gather.19
  713.1 54.6 reduce-scatter.21
  774.2 120.0 all-reduce.10
  896.7 85.6 reduce-scatter.19
  984.7 158.3 reduce-scatter.17
  1146.1 123.6 reduce-scatter.15
  1272.7 140.3 reduce-scatter.13
  1421.1 234.5 reduce-scatter.11
where the time goes:
time: 1670 us; the launch traced here: 1660 us
  waiting for transfers between devices  1100 us (66%)
  blocking collectives  190 us (11%)
  local copies, waits for them, and re-layouts  143 us (9%)
  matrix products  137 us (8%)
  other arithmetic  41.9 us (3%)
  starting transfers between devices  37.3 us (2%)
    reduce_scatter x1, waiting for transfers between devices, local(): lax.psum_scatter(grad_wqkv, ('dp', 'fsdp'), scatter_dimension=0, tiled=True)  243 us
    unnamed x3, blocking collectives  150 us
    reduce_scatter x1, waiting for transfers between devices, local(): lax.psum_scatter(grad_wout, ('dp', 'fsdp'), scatter_dimension=0, tiled=True)  143 us
    reduce_scatter x1, waiting for transfers between devices, local(): lax.psum_scatter(grad_sup, ('dp', 'fsdp'), scatter_dimension=0, tiled=True)  123 us
    reduce_scatter x1, waiting for transfers between devices, local(): lax.psum_scatter(grad_exp_up.astype(jnp.bfloat16), 'dp', scatter_dimensio...  105 us
    reduce_scatter x1, waiting for transfers between devices, local(): lax.psum_scatter(grad_exp_down.astype(jnp.bfloat16), 'dp', scatter_dimens...  86.7 us
    all_gather x1, waiting for transfers between devices, local(): lax.all_gather(w_expert_down, 'dp', axis=1, tiled=True)  74.5 us
    all_gather x1, waiting for transfers between devices, local(): lax.all_gather(w_shared_up, ('dp', 'fsdp'), axis=0, tiled=True)  63.1 us
  transfers between devices with their start and end apart: 23, of which 16 were waited for; matrix products, arithmetic and copies ran while one was open for 19% of the time, Pallas kernels for 0%

commit v1 on v0

v1 whole, which is shorter than its diff:
```python
import functools

import jax
import jax.numpy as jnp
from jax import lax
from jax.experimental import pallas as pl
from jax.experimental.pallas import tpu as pltpu
from jax.sharding import PartitionSpec as P

HEADS = 10
HD = 128
SEQ = 1024
SLOTS = 2
EPS = 1e-06
ROPE = 10000.0
NEG = -1e30
TAIL = 64
F32 = jnp.float32
BF16 = jnp.bfloat16


MESH = pl.DeviceIdType.MESH
VMEM = pl.BlockSpec(memory_space=pltpu.VMEM)
ANY = pl.BlockSpec(memory_space=pl.ANY)


def up_to(value, step):
    return -(-value // step) * step


def rms_scale(values):
    return lax.rsqrt(jnp.mean(values * values, axis=-1, keepdims=True) + EPS)


def norm_back(grad_normed, normal_rows, scale_rows, gain_rows):
    scaled = grad_normed * gain_rows
    return scale_rows * (
        scaled - normal_rows * jnp.mean(scaled * normal_rows, axis=-1, keepdims=True)
    )


def head_table(group):
    heads, real = [], []
    for i in range(group):
        own = list(range(HEADS * i // group, HEADS * (i + 1) // group))
        assert len(own) <= SLOTS
        heads += own + [0] * (SLOTS - len(own))
        real += [1] * len(own) + [0] * (SLOTS - len(own))
    return heads, real


def dot(a, b):
    return jnp.dot(a, b, preferred_element_type=F32)


def dot_nt(a, b):
    return lax.dot_general(a, b, (((1,), (1,)), ((), ())), preferred_element_type=F32)


def dot_tn(a, b):
    return lax.dot_general(a, b, (((0,), (0,)), ((), ())), preferred_element_type=F32)


def attn_forward_kernel(
    tok_ref, gain_ref, w_ref, wo_ref, cos_ref, sin_ref, segq_ref, segk_ref,
    part_ref, normed_ref, qkv_ref, attn_ref, lse_ref,
    *, block,
):
    length, width = tok_ref.shape
    count = length // block
    step = 3 * HD

    def norm_step(i, _):
        rows = pl.ds(pl.multiple_of(i * block, block), block)
        x = tok_ref[rows, :].astype(F32)
        normed = (x * rms_scale(x) * gain_ref[...]).astype(BF16)
        normed_ref[rows, :] = normed
        cosine, sine = cos_ref[rows, :], sin_ref[rows, :]
        for s in range(SLOTS):
            proj = dot(normed, w_ref[s])
            for c in range(3):
                piece = proj[:, c * HD : (c + 1) * HD]
                if c < 2:
                    piece = piece * cosine + pltpu.roll(piece, HD // 2, 1) * sine
                qkv_ref[rows, s * step + c * HD : s * step + (c + 1) * HD] = piece.astype(BF16)
        return 0

    lax.fori_loop(0, count, norm_step, 0)
    scale = HD**-0.5
    for i in range(count):
        rows = slice(i * block, (i + 1) * block)
        keys = (i + 1) * block
        row_pos = i * block + lax.broadcasted_iota(jnp.int32, (block, keys), 0)
        key_pos = lax.broadcasted_iota(jnp.int32, (block, keys), 1)
        allowed = (key_pos <= row_pos) & (segq_ref[rows, :1] == segk_ref[:1, :keys])
        outs = []
        for s in range(SLOTS):
            at = s * step
            q = qkv_ref[rows, at : at + HD]
            k = qkv_ref[:keys, at + HD : at + 2 * HD]
            v = qkv_ref[:keys, at + 2 * HD : at + 3 * HD]
            scores = jnp.where(allowed, dot_nt(q, k) * scale, NEG)
            top = jnp.max(scores, axis=-1, keepdims=True)
            weights = jnp.exp(scores - top)
            total = jnp.sum(weights, axis=-1, keepdims=True)
            out = dot(weights.astype(BF16), v) / total
            lse_ref[rows, s * HD : (s + 1) * HD] = jnp.broadcast_to(
                top + jnp.log(total), (block, HD)
            )
            low = out.astype(BF16)
            attn_ref[rows, s * HD : (s + 1) * HD] = low
            outs.append(low)
        part_ref[rows, :] = dot(jnp.concatenate(outs, axis=-1), wo_ref[...]).astype(BF16)


def attn_forward(tok, gain, w, wo, cosine, sine, segq, segk):
    length, width = tok.shape
    return pl.pallas_call(
        functools.partial(attn_forward_kernel, block=256),
        out_shape=(
            jax.ShapeDtypeStruct((length, width), BF16),
            jax.ShapeDtypeStruct((length, width), BF16),
            jax.ShapeDtypeStruct((length, 3 * SLOTS * HD), BF16),
            jax.ShapeDtypeStruct((length, SLOTS * HD), BF16),
            jax.ShapeDtypeStruct((length, SLOTS * HD), F32),
        ),
        in_specs=[VMEM] * 8,
        out_specs=(VMEM,) * 5,
        compiler_params=pltpu.CompilerParams(vmem_limit_bytes=56 * 2**20),
        cost_estimate=pl.CostEstimate(
            flops=2 * length * width * 4 * SLOTS * HD + 4 * SLOTS * HD * length * length,
            bytes_accessed=10 * length * width,
            transcendentals=SLOTS * length * length,
        ),
        name="attn_forward",
    )(tok, gain, w, wo, cosine, sine, segq, segk)


def attn_backward_kernel(
    gm_ref, wo_ref, w_ref, normed_ref, qkv_ref, attn_ref, lse_ref, cos_ref, sin_ref,
    segq_ref, segk_ref,
    part_ref, gw_ref, gwo_ref,
    gkv_ref, gqkv_ref, wt_ref,
    *, block,
):
    length, width = gm_ref.shape
    count = length // block
    scale = HD**-0.5
    step = 3 * HD
    gkv_ref[...] = jnp.zeros_like(gkv_ref)
    for i in range(count):
        rows = slice(i * block, (i + 1) * block)
        keys = (i + 1) * block
        row_pos = i * block + lax.broadcasted_iota(jnp.int32, (block, keys), 0)
        key_pos = lax.broadcasted_iota(jnp.int32, (block, keys), 1)
        allowed = (key_pos <= row_pos) & (segq_ref[rows, :1] == segk_ref[:1, :keys])
        grad_attn = dot_nt(gm_ref[rows, :], wo_ref[...]).astype(BF16)
        for s in range(SLOTS):
            at = s * step
            cut = slice(s * HD, (s + 1) * HD)
            q = qkv_ref[rows, at : at + HD]
            k = qkv_ref[:keys, at + HD : at + 2 * HD]
            v = qkv_ref[:keys, at + 2 * HD : at + 3 * HD]
            ga = grad_attn[:, cut]
            delta = jnp.sum(ga.astype(F32) * attn_ref[rows, cut].astype(F32), axis=-1, keepdims=True)
            scores = dot_nt(q, k) * scale
            probs = jnp.where(allowed, jnp.exp(scores - lse_ref[rows, s * HD : s * HD + 1]), 0.0)
            gs = (probs * (dot_nt(ga, v) - delta)).astype(BF16)
            gq = dot(gs, k) * scale
            gq = gq * cos_ref[rows, :] - pltpu.roll(gq, HD // 2, 1) * sin_ref[rows, :]
            gqkv_ref[rows, at : at + HD] = gq.astype(BF16)
            gkv_ref[:keys, 2 * s * HD : (2 * s + 1) * HD] += dot_tn(gs, q)
            gkv_ref[:keys, (2 * s + 1) * HD : (2 * s + 2) * HD] += dot_tn(probs.astype(BF16), ga)
    for s in range(SLOTS):
        at = s * step
        gk = gkv_ref[:, 2 * s * HD : (2 * s + 1) * HD] * scale
        gk = gk * cos_ref[...] - pltpu.roll(gk, HD // 2, 1) * sin_ref[...]
        gqkv_ref[:, at + HD : at + 2 * HD] = gk.astype(BF16)
        gqkv_ref[:, at + 2 * HD : at + 3 * HD] = gkv_ref[:, (2 * s + 1) * HD : (2 * s + 2) * HD].astype(BF16)
        wt_ref[s * step : (s + 1) * step, :] = w_ref[s].T
    for i in range(count):
        rows = slice(i * block, (i + 1) * block)
        part_ref[rows, :] = dot(gqkv_ref[rows, :], wt_ref[...]).astype(BF16)
    for s in range(SLOTS):
        gw_ref[s] = dot_tn(normed_ref[...], gqkv_ref[:, s * step : (s + 1) * step]).astype(BF16)
    gwo_ref[...] = dot_tn(attn_ref[...], gm_ref[...]).astype(BF16)


def attn_backward(gm, wo, w, normed, qkv, attn, lse, cosine, sine, segq, segk):
    length, width = gm.shape
    return pl.pallas_call(
        functools.partial(attn_backward_kernel, block=256),
        out_shape=(
            jax.ShapeDtypeStruct((length, width), BF16),
            jax.ShapeDtypeStruct((SLOTS, width, 3 * HD), BF16),
            jax.ShapeDtypeStruct((SLOTS * HD, width), BF16),
        ),
        in_specs=[VMEM] * 11,
        out_specs=(VMEM,) * 3,
        scratch_shapes=[
            pltpu.VMEM((length, 2 * SLOTS * HD), F32),
            pltpu.VMEM((length, 3 * SLOTS * HD), BF16),
            pltpu.VMEM((3 * SLOTS * HD, width), BF16),
        ],
        compiler_params=pltpu.CompilerParams(vmem_limit_bytes=56 * 2**20),
        cost_estimate=pl.CostEstimate(
            flops=4 * length * width * 4 * SLOTS * HD + 10 * SLOTS * HD * length * length,
            bytes_accessed=10 * length * width,
            transcendentals=SLOTS * length * length,
        ),
        name="attn_backward",
    )(gm, wo, w, normed, qkv, attn, lse, cosine, sine, segq, segk)


def ffn_kernel(
    x_ref, g_ref, mark_ref, own_ref, eup_ref, tail_ref, edown_ref, sdown_ref,
    out_ref, gx_ref, geup_ref, gtail_ref, gedown_ref, gsdown_ref,
    up_ref, upt_ref, down_ref, downt_ref, gup_ref, gdown_ref,
    *, hidden, shared,
):
    step = pl.program_id(0)
    half = down_ref.shape[0]
    width = x_ref.shape[1]
    pair = 2 * hidden
    gap = half - pair - TAIL

    @pl.when(step == 0)
    def _():
        gup_ref[...] = jnp.zeros_like(gup_ref)
        gdown_ref[...] = jnp.zeros_like(gdown_ref)
        between = [jnp.zeros((width, gap), BF16)] if gap else []
        up_ref[...] = jnp.concatenate(
            [eup_ref[:, :pair], *between, tail_ref[:, :TAIL], eup_ref[:, pair:], *between, tail_ref[:, TAIL:]], axis=1
        )
        between = [jnp.zeros((gap, width), BF16)] if gap else []
        down_ref[...] = jnp.concatenate(
            [edown_ref[...], *between, sdown_ref[...], jnp.zeros((TAIL - shared, width), BF16)], axis=0
        )
        upt_ref[...] = up_ref[...].T
        downt_ref[...] = down_ref[...].T

    x, g = x_ref[...], g_ref[...]
    pre = dot(x, up_ref[...])
    gate, up = pre[:, :half], pre[:, half:]
    marks = mark_ref[...].astype(F32) > 0.5
    logits = jnp.where(marks, gate[:, half - HD :], NEG)
    weights = jnp.exp(logits - jnp.max(logits, axis=-1, keepdims=True))
    probs = weights / jnp.sum(weights, axis=-1, keepdims=True)
    p0 = jnp.sum(probs * own_ref[0:1, :], axis=-1, keepdims=True)
    p1 = jnp.sum(probs * own_ref[1:2, :], axis=-1, keepdims=True)
    lane = lax.broadcasted_iota(jnp.int32, (1, half), 1)
    in0 = lane < hidden
    in1 = (lane >= hidden) & (lane < pair)
    rest = jnp.where((lane >= half - TAIL) & (lane < half - TAIL + shared), 1.0, 0.0)
    weight = jnp.where(in0, p0, jnp.where(in1, p1, rest))
    sig = jax.nn.sigmoid(gate)
    silu = gate * sig
    act = silu * up
    acts = (act * weight).astype(BF16)
    out_ref[...] = dot(acts, down_ref[...]).astype(BF16)
    grad = dot(g, downt_ref[...])
    both = act * grad
    d0 = jnp.sum(jnp.where(in0, both, 0.0), axis=-1, keepdims=True)
    d1 = jnp.sum(jnp.where(in1, both, 0.0), axis=-1, keepdims=True)
    grad = grad * weight
    grad_gate = grad * up * sig * (1.0 + gate * (1.0 - sig))
    grad_up = grad * silu
    grad_pre = jnp.concatenate([grad_gate, grad_up], axis=-1).astype(BF16)
    gx_ref[:, :width] = dot(grad_pre, upt_ref[...]).astype(BF16)
    gx_ref[:, width:] = (d0 * own_ref[0:1, :] + d1 * own_ref[1:2, :]).astype(BF16)
    gup_ref[...] += dot_tn(x, grad_pre)
    gdown_ref[...] += dot_tn(acts, g)

    @pl.when(step == pl.num_programs(0) - 1)
    def _():
        geup_ref[...] = jnp.concatenate([gup_ref[:, :pair], gup_ref[:, half : half + pair]], axis=1).astype(BF16)
        gtail_ref[...] = jnp.concatenate([gup_ref[:, half - TAIL : half], gup_ref[:, 2 * half - TAIL :]], axis=1)
        gedown_ref[...] = gdown_ref[:pair, :]
        gsdown_ref[...] = gdown_ref[half - TAIL : half - TAIL + shared, :]


def ffn(x, g, marks, own, eup, tail, edown, sdown):
    total, width = x.shape
    pair, shared = edown.shape[0], sdown.shape[0]
    half = up_to(pair + TAIL, HD)
    tile = 512
    row = lambda n: pl.BlockSpec((tile, n), lambda i: (i, 0))
    return pl.pallas_call(
        functools.partial(ffn_kernel, hidden=pair // 2, shared=shared),
        out_shape=(
            jax.ShapeDtypeStruct((total, width), BF16),
            jax.ShapeDtypeStruct((total, width + HD), BF16),
            jax.ShapeDtypeStruct((width, 2 * pair), BF16),
            jax.ShapeDtypeStruct((width, HD), F32),
            jax.ShapeDtypeStruct((pair, width), F32),
            jax.ShapeDtypeStruct((shared, width), F32),
        ),
        grid=(total // tile,),
        in_specs=[row(width), row(width), row(HD)] + [VMEM] * 5,
        out_specs=(row(width), row(width + HD), VMEM, VMEM, VMEM, VMEM),
        scratch_shapes=[
            pltpu.VMEM((width, 2 * half), BF16),
            pltpu.VMEM((2 * half, width), BF16),
            pltpu.VMEM((half, width), BF16),
            pltpu.VMEM((width, half), BF16),
            pltpu.VMEM((width, 2 * half), F32),
            pltpu.VMEM((half, width), F32),
        ],
        compiler_params=pltpu.CompilerParams(vmem_limit_bytes=60 * 2**20),
        cost_estimate=pl.CostEstimate(
            flops=2 * total * width * 9 * half,
            bytes_accessed=8 * total * width,
            transcendentals=total * half,
        ),
        name="ffn",
    )(x, g, marks, own, eup, tail, edown, sdown)


def flip(f, bits):
    for b in (1, 2, 4):
        if bits & b:
            f = f + b - 2 * b * (f // b % 2)
    return f


def place():
    return lax.axis_index("dp"), lax.axis_index("fsdp")


def greet(devices):
    barrier = pltpu.get_barrier_semaphore()
    for device in devices:
        pl.semaphore_signal(barrier, inc=1, device_id=device, device_id_type=MESH)
    pl.semaphore_wait(barrier, len(devices))


def greet_all(nz, nf):
    barrier = pltpu.get_barrier_semaphore()
    z, f = place()
    me, count = z * nf + f, nz * nf

    def hail(i, _):
        d = (me + i) % count
        pl.semaphore_signal(barrier, inc=1, device_id=(d // nf, d % nf), device_id_type=MESH)
        return 0

    lax.fori_loop(1, count, hail, 0)
    pl.semaphore_wait(barrier, count - 1)


def send(src, dst, sems, index, device):
    return pltpu.make_async_remote_copy(
        src, dst, sems[0].at[index], sems[1].at[index], device_id=device, device_id_type=MESH
    )


ORDER = ((2, 4), (4, 2))


def halves(width):
    cut = (width // HD + 1) // 2 * HD
    return ((0, cut), (cut, width - cut))


class Gather:
    @staticmethod
    def copies(nz):
        return 11 * nz

    def __init__(self, own, buf, sems, nz, z, f, pieces=None):
        self.own, self.buf, self.sems, self.nz = own, buf, sems, nz
        self.z, self.f = z, f
        self.width = buf.shape[-1]
        self.sent = {}

    def piece(self, zr):
        return lax.rem(self.z - zr + self.nz, self.nz) if zr else self.z

    def source(self, zr, r, h=None):
        ref = self.own if zr == 0 and r == 0 else self.buf.at[self.piece(zr), flip(self.f, r)]
        return ref if h is None else ref.at[:, pl.ds(*halves(self.width)[h])]

    def slot(self, zr, r, h=None):
        ref = self.buf.at[self.piece(zr), flip(self.f, r)]
        return ref if h is None else ref.at[:, pl.ds(*halves(self.width)[h])]

    def go(self, src, dst, index, device):
        copy = send(src, dst, self.sems, index, device)
        copy.start()
        self.sent[index] = copy

    def along_z(self):
        for zr in range(1, self.nz):
            there = lax.rem(self.z + zr, self.nz)
            self.go(self.own, self.buf.at[self.z, self.f], zr, (there, self.f))

    def first(self, zr):
        nz = self.nz
        if zr:
            self.sent[zr].wait_recv()
        for h in range(2):
            near = (self.z, flip(self.f, ORDER[h][0]))
            self.go(self.source(zr, 0, h), self.slot(zr, 0, h), nz + 2 * zr + h, near)
        self.core(zr, 0)

    def core(self, zr, i):
        other = (self.z, flip(self.f, 1))
        self.go(self.source(zr, 2 * i), self.slot(zr, 2 * i), 7 * self.nz + 4 * zr + i, other)

    def second(self, zr):
        nz = self.nz
        for h in range(2):
            self.sent[nz + 2 * zr + h].wait_recv()
            near = (self.z, flip(self.f, ORDER[h][1]))
            for i, r in enumerate((0, ORDER[h][0])):
                self.go(self.source(zr, r, h), self.slot(zr, r, h), 3 * nz + 4 * zr + 2 * h + i, near)

    def third(self, zr):
        for k in range(4):
            self.sent[3 * self.nz + 4 * zr + k].wait_recv()
        for i in range(1, 4):
            self.core(zr, i)

    def fourth(self, zr):
        for i in range(4):
            self.sent[7 * self.nz + 4 * zr + i].wait_recv()

    def end(self):
        for copy in self.sent.values():
            copy.wait_send()


class Reduce:
    @staticmethod
    def copies(nz):
        return 11 * nz

    @staticmethod
    def scratch(nz, rows, width):
        return [
            pltpu.VMEM((nz, 4, rows, width), BF16),
            pltpu.VMEM((nz, 2, rows, width), BF16),
            pltpu.VMEM((nz, rows, width), BF16),
            pltpu.VMEM((nz, rows, width), BF16),
        ]

    def __init__(self, terms, bufs, sems, nz, z, f):
        self.terms, self.sems, self.nz, self.z, self.f = terms, sems, nz, z, f
        self.by_core, self.by_near, self.by_far, self.by_z = bufs
        self.width = terms.shape[-1]
        self.sent = {}

    def piece(self, zr):
        return lax.rem(self.z + zr, self.nz) if zr else self.z

    def go(self, src, dst, index, device):
        copy = send(src, dst, self.sems, index, device)
        copy.start()
        self.sent[index] = copy

    def core(self, zr):
        other = flip(self.f, 1)
        for i in range(4):
            self.go(
                self.terms.at[self.piece(zr), flip(self.f, 1 | 2 * i)], self.by_core.at[zr, i], 4 * zr + i, (self.z, other)
            )

    def near(self, zr):
        for i in range(4):
            self.sent[4 * zr + i].wait_recv()
            self.by_core[zr, i] = self.by_core[zr, i] + self.terms[self.piece(zr), flip(self.f, 2 * i)]
        for h in range(2):
            first, last = ORDER[1 - h]
            cols = pl.ds(*halves(self.width)[h])
            for i, r in enumerate((last, 6)):
                self.go(
                    self.by_core.at[zr, (last if i == 0 else 6) // 2, :, cols],
                    self.by_near.at[zr, i, :, cols],
                    4 * self.nz + 4 * zr + 2 * h + i,
                    (self.z, flip(self.f, last)),
                )

    def far(self, zr):
        for h in range(2):
            first, last = ORDER[1 - h]
            at, size = halves(self.width)[h]
            cols = slice(at, at + size)
            for i, r in enumerate((0, first)):
                self.sent[4 * self.nz + 4 * zr + 2 * h + i].wait_recv()
                self.by_near[zr, i, :, cols] = self.by_near[zr, i, :, cols] + self.by_core[zr, r // 2, :, cols]
            cols = pl.ds(at, size)
            self.go(
                self.by_near.at[zr, 1, :, cols], self.by_far.at[zr, :, cols], 8 * self.nz + 2 * zr + h,
                (self.z, flip(self.f, first)),
            )

    def along_z(self, zr):
        for h in range(2):
            at, size = halves(self.width)[h]
            cols = slice(at, at + size)
            self.sent[8 * self.nz + 2 * zr + h].wait_recv()
            self.by_far[zr, :, cols] = self.by_far[zr, :, cols] + self.by_near[zr, 0, :, cols]
        if zr:
            self.go(self.by_far.at[zr], self.by_z.at[zr], 10 * self.nz + zr, (self.piece(zr), self.f))

    def total(self):
        result = self.by_far[0].astype(F32)
        for zr in range(1, self.nz):
            self.sent[10 * self.nz + zr].wait_recv()
            result = result + self.by_z[zr].astype(F32)
        return result

    def end(self):
        for copy in self.sent.values():
            copy.wait_send()


def near_devices(z, f):
    return [(z, flip(f, 1)), (z, flip(f, 2)), (z, flip(f, 4))]


def z_devices(z, f, nz):
    return [(lax.rem(z + zr, nz), f) for zr in range(1, nz)]


def pair_of(count):
    return [pltpu.SemaphoreType.DMA((count,))] * 2


def first_head(member):
    return HEADS * member // 8


def out_blocks(member, dense):
    return first_head(member) * HD // dense, (first_head(member + 1) * HD - 1) // dense


def head_owner(head):
    return (8 * head + 7) // HEADS


def prologue_kernel(
    tok_ref, wqkv_ref, wout_ref, router_ref, sup_ref, gains_ref, ids_ref,
    seq_ref, wq_ref, wo_ref, tail_ref, all_ids_ref,
    qpack, tpack, tok_sems_s, tok_sems_r, all_s, all_r, wo_s, wo_r, own_sems,
    *, nz, nf, shared, heads, real,
):
    z, f = place()
    me, count = z * nf + f, nz * nf
    dense = wqkv_ref.shape[0]
    width = wqkv_ref.shape[1] // 3
    experts = router_ref.shape[1]
    hidden = shared * count
    greet_all(nz, nf)

    toks = (tok_sems_s, tok_sems_r)
    to_near = []
    for i, r in enumerate((2, 4, 6)):
        copy = send(tok_ref, seq_ref.at[f], toks, i, (z, flip(f, r)))
        copy.start()
        to_near.append(copy)
    to_core = [send(tok_ref, seq_ref.at[f], toks, 3, (z, flip(f, 1)))]
    to_core[0].start()
    own = [pltpu.make_async_copy(tok_ref, seq_ref.at[f], own_sems.at[0])]

    for m in range(8):
        for s in range(SLOTS):
            h = heads[m * SLOTS + s]
            if real[m * SLOTS + s]:
                qpack[m, s] = jnp.concatenate(
                    [wqkv_ref[:, c * width + h * HD : c * width + (h + 1) * HD] for c in range(3)], axis=1
                )
    pad = jnp.zeros((dense, TAIL - shared - experts), BF16)
    pad_two = jnp.zeros((dense, TAIL - shared - 2), BF16)
    for d in range(count):
        tpack[d] = jnp.concatenate(
            [
                sup_ref[:, d * shared : (d + 1) * shared], router_ref[...], pad,
                sup_ref[:, hidden + d * shared : hidden + (d + 1) * shared], gains_ref[...], pad_two,
            ],
            axis=1,
        )

    def two(m):
        return first_head(m + 1) - first_head(m) == 2

    def copies(d):
        device = (d // nf, d % nf)
        at = lambda k: (all_s.at[k, d], all_r.at[k, me])
        make = lambda src, dst, k: pltpu.make_async_remote_copy(
            src, dst, *at(k), device_id=device, device_id_type=MESH
        )
        return (
            make(qpack.at[d % nf, 0], wq_ref.at[0, me], 0),
            make(qpack.at[d % nf, 1], wq_ref.at[1, me], 1),
            make(tpack.at[d], tail_ref.at[me], 2),
            make(ids_ref, all_ids_ref.at[me], 3),
        )

    def out_copy(d):
        low, _ = out_blocks(d % nf, dense)
        return pltpu.make_async_remote_copy(
            wout_ref, wo_ref.at[me - low], wo_s.at[d], wo_r.at[me - low],
            device_id=(d // nf, d % nf), device_id_type=MESH,
        )

    def wanted(d, block):
        low, high = out_blocks(d % nf, dense)
        return (low <= block) & (block <= high)

    def start(i, _):
        d = (me + i) % count
        q0, q1, tail, ids = copies(d)
        q0.start()

        @pl.when(two(d % nf))
        def _():
            q1.start()

        tail.start()
        ids.start()

        @pl.when(wanted(d, me))
        def _():
            out_copy(d).start()

        return 0

    lax.fori_loop(1, count, start, 0)

    own += [
        pltpu.make_async_copy(qpack.at[f, 0], wq_ref.at[0, me], own_sems.at[1]),
        pltpu.make_async_copy(tpack.at[me], tail_ref.at[me], own_sems.at[2]),
        pltpu.make_async_copy(ids_ref, all_ids_ref.at[me], own_sems.at[3]),
    ]
    for copy in own:
        copy.start()
    own_two = pltpu.make_async_copy(qpack.at[f, 1], wq_ref.at[1, me], own_sems.at[4])
    low, high = out_blocks(f, dense)
    own_out = pltpu.make_async_copy(wout_ref, wo_ref.at[me - low], own_sems.at[5])

    @pl.when(two(f))
    def _():
        own_two.start()

    @pl.when(wanted(me, me))
    def _():
        own_out.start()

    for i, r in enumerate((2, 4, 6)):
        to_near[i].wait_recv()
        slot = seq_ref.at[flip(f, r)]
        copy = send(slot, slot, toks, 4 + i, (z, flip(f, 1)))
        copy.start()
        to_core.append(copy)
    for copy in to_core:
        copy.wait()
    for copy in to_near:
        copy.wait_send()

    def came(src, dst, k, d):
        return pltpu.make_async_remote_copy(
            src, dst, all_s.at[k, d], all_r.at[k, d], device_id=(d // nf, d % nf), device_id_type=MESH
        )

    def finish(i, _):
        d = (me + i) % count
        came(qpack.at[f, 0], wq_ref.at[0, d], 0, d).wait_recv()

        @pl.when(two(f))
        def _():
            came(qpack.at[f, 1], wq_ref.at[1, d], 1, d).wait_recv()

        came(tpack.at[d], tail_ref.at[d], 2, d).wait_recv()
        came(ids_ref, all_ids_ref.at[d], 3, d).wait_recv()
        q0, q1, tail, ids = copies(d)
        q0.wait_send()

        @pl.when(two(d % nf))
        def _():
            q1.wait_send()

        tail.wait_send()
        ids.wait_send()

        @pl.when(wanted(d, me))
        def _():
            out_copy(d).wait_send()

        return 0

    lax.fori_loop(1, count, finish, 0)
    for j in range(wo_ref.shape[0]):

        @pl.when((low + j <= high) & (low + j != me))
        def _():
            pltpu.make_async_remote_copy(
                wout_ref, wo_ref.at[j], wo_s.at[j], wo_r.at[j], device_id=(z, flip(f, 1)), device_id_type=MESH
            ).wait_recv()

    for copy in own:
        copy.wait()

    @pl.when(two(f))
    def _():
        own_two.wait()

    @pl.when(wanted(me, me))
    def _():
        own_out.wait()


def prologue(tok, wqkv, wout, router, sup, gains, ids, nz, nf, shared):
    rows, width = tok.shape
    dense, count = wqkv.shape[0], nz * nf
    heads, real = head_table(8)
    return pl.pallas_call(
        functools.partial(prologue_kernel, nz=nz, nf=nf, shared=shared, heads=heads, real=real),
        out_shape=(
            jax.ShapeDtypeStruct((8, rows, width), BF16),
            jax.ShapeDtypeStruct((SLOTS, count, dense, 3 * HD), BF16),
            jax.ShapeDtypeStruct((8, dense, width), BF16),
            jax.ShapeDtypeStruct((count, dense, 2 * TAIL), BF16),
            jax.ShapeDtypeStruct((count, *ids.shape), jnp.int32),
        ),
        in_specs=[ANY, VMEM, ANY, VMEM, VMEM, VMEM, ANY],
        out_specs=(ANY,) * 5,
        scratch_shapes=[
            pltpu.VMEM((8, SLOTS, dense, 3 * HD), BF16),
            pltpu.VMEM((count, dense, 2 * TAIL), BF16),
            *pair_of(7),
            pltpu.SemaphoreType.DMA((4, count)),
            pltpu.SemaphoreType.DMA((4, count)),
            pltpu.SemaphoreType.DMA((count,)),
            pltpu.SemaphoreType.DMA((8,)),
            pltpu.SemaphoreType.DMA((6,)),
        ],
        compiler_params=pltpu.CompilerParams(
            collective_id=1, has_side_effects=True, vmem_limit_bytes=16 * 2**20
        ),
        name="prologue",
    )(tok, wqkv, wout, router, sup, gains, ids)


def spread_kernel(
    part_ref, tok_ref, gain_ref, og_ref, eup_ref,
    all_normed_ref, all_grad_ref, pieces_ref, mixed_ref, normed_ref,
    pack, *refs, nz, hidden,
):
    bufs, (rs, rr, xs, xr, gs, gr, es, er, own_sems) = refs[:4], refs[4:]
    z, f = place()
    up_rows = eup_ref.shape[1]
    greet(near_devices(z, f) + z_devices(z, f, nz))
    reduce = Reduce(part_ref, bufs, (rs, rr), 1, 0, f)
    reduce.z = z
    reduce.piece = lambda zr: 0
    reduce.core(0)
    grads = Gather(og_ref, all_grad_ref, (gs, gr), nz, z, f)
    grads.along_z()
    own = [pltpu.make_async_copy(og_ref, all_grad_ref.at[z, f], own_sems.at[0])]
    own[0].start()
    grads.first(0)
    full = nz * hidden
    for t in range(nz):
        pack[t] = jnp.concatenate(
            [
                eup_ref[e, :, g * full + t * hidden : g * full + (t + 1) * hidden]
                for g in range(2)
                for e in range(2)
            ],
            axis=1,
        )
    ups = []
    for zr in range(1, nz):
        there = lax.rem(z + zr, nz)
        copy = send(pack.at[there], pieces_ref.at[z], (es, er), zr, (there, f))
        copy.start()
        ups.append(copy)
    own.append(pltpu.make_async_copy(pack.at[z], pieces_ref.at[z], own_sems.at[1]))
    own[1].start()

    reduce.near(0)
    grads.second(0)
    reduce.far(0)
    reduce.along_z(0)
    mixed = tok_ref[...].astype(F32) + reduce.by_far[0].astype(F32)
    mixed_ref[...] = mixed
    normed_ref[...] = (mixed * rms_scale(mixed) * gain_ref[...]).astype(BF16)
    rows = Gather(normed_ref, all_normed_ref, (xs, xr), nz, z, f)
    rows.along_z()
    own.append(pltpu.make_async_copy(normed_ref, all_normed_ref.at[z, f], own_sems.at[2]))
    own[2].start()
    rows.first(0)
    rows.second(0)
    for zr in range(1, nz):
        for part in (grads, rows):
            part.first(zr)
        for part in (grads, rows):
            part.second(zr)
    for zr in range(nz):
        for part in (grads, rows):
            part.third(zr)
    for zr in range(nz):
        for part in (grads, rows):
            part.fourth(zr)
    for part in (reduce, grads, rows):
        part.end()
    for copy in ups + own:
        copy.wait()


def spread(part, tok, gain, og, eup, nz, nf):
    rows, width = tok.shape
    hidden = eup.shape[2] // (2 * nz)
    up_rows = eup.shape[1]
    return pl.pallas_call(
        functools.partial(spread_kernel, nz=nz, hidden=hidden),
        out_shape=(
            jax.ShapeDtypeStruct((nz, 8, rows, width), BF16),
            jax.ShapeDtypeStruct((nz, 8, rows, width), BF16),
            jax.ShapeDtypeStruct((nz, up_rows, 4 * hidden), BF16),
            jax.ShapeDtypeStruct((rows, width), F32),
            jax.ShapeDtypeStruct((rows, width), BF16),
        ),
        in_specs=[VMEM, VMEM, VMEM, ANY, VMEM],
        out_specs=(ANY, ANY, ANY, VMEM, VMEM),
        scratch_shapes=[
            pltpu.VMEM((nz, up_rows, 4 * hidden), BF16),
            *Reduce.scratch(1, rows, width),
            *pair_of(Reduce.copies(1)),
            *pair_of(Gather.copies(nz)),
            *pair_of(Gather.copies(nz)),
            *pair_of(nz),
            pltpu.SemaphoreType.DMA((3,)),
        ],
        compiler_params=pltpu.CompilerParams(
            collective_id=2, has_side_effects=True, vmem_limit_bytes=40 * 2**20
        ),
        name="spread",
    )(part.reshape(1, 8, rows, width), tok, gain, og, eup)


def route_grads(gx, og, mixed, normed, router, marks, gain):
    width = mixed.shape[1]
    scale = rms_scale(mixed)
    normal = mixed * scale
    logits = jnp.where(marks > 0.5, dot(normed, router), NEG)
    weights = jnp.exp(logits - jnp.max(logits, axis=-1, keepdims=True))
    probs = weights / jnp.sum(weights, axis=-1, keepdims=True)
    grad_gates = gx[:, width:]
    grad_logits = (probs * (grad_gates - jnp.sum(probs * grad_gates, axis=-1, keepdims=True))).astype(BF16)
    grad_router = dot_tn(normed, grad_logits)
    grad_normed = gx[:, :width] + dot_nt(grad_logits, router)
    ones = jnp.where(lax.broadcasted_iota(jnp.int32, (mixed.shape[0], HD), 1) == TAIL - 1, 1.0, 0.0)
    grad_gain = lax.dot_general(
        grad_normed * normal, ones, (((0,), (0,)), ((), ())),
        precision=lax.Precision.HIGHEST, preferred_element_type=F32,
    )
    grad_mixed = og.astype(F32) + norm_back(grad_normed, normal, scale, gain)
    return grad_mixed, pltpu.roll(grad_router + grad_gain, TAIL, 1)


def turn_kernel(
    gx_ref, og_ref, mixed_ref, normed_ref, router_ref, mark_ref, gain_ref,
    seq_ref, gm_ref, small_ref,
    low, *refs, nz,
):
    bufs, (rs, rr, gs, gr, own_sem) = refs[:4], refs[4:]
    z, f = place()
    greet(near_devices(z, f) + z_devices(z, f, nz))
    reduce = Reduce(gx_ref, bufs, (rs, rr), nz, z, f)
    order = list(range(1, nz)) + [0]
    for step in (reduce.core, reduce.near, reduce.far, reduce.along_z):
        for zr in order:
            step(zr)
    grad_mixed, small = route_grads(
        reduce.total(), og_ref[...], mixed_ref[...], normed_ref[...], router_ref[...], mark_ref[...], gain_ref[...]
    )
    gm_ref[...] = grad_mixed
    low[...] = grad_mixed.astype(BF16)
    rows = Gather(low, seq_ref, (gs, gr), 1, 0, f)
    rows.z = z
    rows.piece = lambda zr: 0
    own = pltpu.make_async_copy(low, seq_ref.at[0, f], own_sem.at[0])
    own.start()
    rows.first(0)
    small_ref[...] = small
    rows.second(0)
    rows.third(0)
    rows.fourth(0)
    own.wait()
    rows.end()
    reduce.end()


def turn(gx, og, mixed, normed, router, marks, gain, nz, nf):
    rows, width = mixed.shape
    return pl.pallas_call(
        functools.partial(turn_kernel, nz=nz),
        out_shape=(
            jax.ShapeDtypeStruct((1, 8, rows, width), BF16),
            jax.ShapeDtypeStruct((rows, width), F32),
            jax.ShapeDtypeStruct((width, HD), F32),
        ),
        in_specs=[VMEM] * 7,
        out_specs=(ANY, VMEM, VMEM),
        scratch_shapes=[
            pltpu.VMEM((rows, width), BF16),
            *Reduce.scratch(nz, rows, width + HD),
            *pair_of(Reduce.copies(nz)),
            *pair_of(Gather.copies(1)),
            pltpu.SemaphoreType.DMA((1,)),
        ],
        compiler_params=pltpu.CompilerParams(
            collective_id=3, has_side_effects=True, vmem_limit_bytes=48 * 2**20
        ),
        name="turn",
    )(gx.reshape(nz, 8, rows, width + HD), og, mixed, normed, router, marks, gain)


def finish_kernel(
    part_ref, out_ref, gw_ref, gwo_ref, small_ref, eup_ref, tok_ref, mixed_ref, gm_ref, gain_ref,
    block_ref, gtok_ref, gwqkv_ref, gwout_ref, all_small_ref, pieces_ref,
    gws, gwos, smalls, *refs, nz, nf, heads, real,
):
    bufs, refs = refs[:8], refs[8:]
    rs, rr, os_, or_, all_s, all_r, wo_s, wo_r, es, er, own_sems = refs
    z, f = place()
    me, count = z * nf + f, nz * nf
    dense = gw_ref.shape[2]
    greet_all(nz, nf)
    reduce = Reduce(part_ref, bufs[:4], (rs, rr), 1, 0, f)
    reduce.z = z
    reduce.piece = lambda zr: 0
    reduce.core(0)

    def two(m):
        return first_head(m + 1) - first_head(m) == 2

    def copies(d):
        device = (d // nf, d % nf)
        make = lambda src, dst, k: pltpu.make_async_remote_copy(
            src, dst, all_s.at[k, d], all_r.at[k, me], device_id=device, device_id_type=MESH
        )
        return (
            make(gw_ref.at[0, d], gws.at[0, me], 0),
            make(gw_ref.at[1, d], gws.at[1, me], 1),
            make(small_ref.at[d], smalls.at[me], 2),
        )

    def wanted(m, block):
        low, high = out_blocks(m, dense)
        return (low <= block) & (block <= high)

    def owner_of(block):
        return head_owner(block * dense // HD)

    def out_copy(d):
        low, _ = out_blocks(f, dense)
        k = 2 * z + f - owner_of(d)
        return pltpu.make_async_remote_copy(
            gwo_ref.at[d - low], gwos.at[k], wo_s.at[d - low], wo_r.at[k],
            device_id=(d // nf, d % nf), device_id_type=MESH,
        )

    def start(i, _):
        d = (me + i) % count
        q0, q1, small = copies(d)
        q0.start()

        @pl.when(two(f))
        def _():
            q1.start()

        small.start()

        @pl.when(wanted(f, d))
        def _():
            out_copy(d).start()

        return 0

    lax.fori_loop(1, count, start, 0)
    own = [
        pltpu.make_async_copy(gw_ref.at[0, me], gws.at[0, me], own_sems.at[0]),
        pltpu.make_async_copy(small_ref.at[me], smalls.at[me], own_sems.at[1]),
        pltpu.make_async_copy(eup_ref.at[z], pieces_ref.at[z], own_sems.at[2]),
    ]
    for copy in own:
        copy.start()
    own_two = pltpu.make_async_copy(gw_ref.at[1, me], gws.at[1, me], own_sems.at[3])
    low, _ = out_blocks(f, dense)
    own_slot = 2 * z + f - owner_of(me)
    own_out = pltpu.make_async_copy(gwo_ref.at[me - low], gwos.at[own_slot], own_sems.at[4])

    @pl.when(two(f))
    def _():
        own_two.start()

    @pl.when(wanted(f, me))
    def _():
        own_out.start()

    ups = []
    for zr in range(1, nz):
        there = lax.rem(z + zr, nz)
        copy = send(eup_ref.at[there], pieces_ref.at[z], (es, er), zr, (there, f))
        copy.start()
        ups.append(copy)

    outs = Reduce(out_ref, bufs[4:], (os_, or_), nz, z, f)
    order = list(range(1, nz)) + [0]
    for zr in order:
        outs.core(zr)
    reduce.near(0)
    reduce.far(0)
    for zr in order:
        outs.near(zr)
    reduce.along_z(0)
    x = tok_ref[...].astype(F32)
    scale = rms_scale(x)
    gtok_ref[...] = (
        gm_ref[...] + norm_back(reduce.by_far[0].astype(F32), x * scale, scale, gain_ref[...])
    ).astype(BF16)
    for step in (outs.far, outs.along_z):
        for zr in order:
            step(zr)
    block_ref[...] = (mixed_ref[...] + outs.total()).astype(BF16)

    def came(src, dst, k, d):
        return pltpu.make_async_remote_copy(
            src, dst, all_s.at[k, d], all_r.at[k, d], device_id=(d // nf, d % nf), device_id_type=MESH
        )

    def finish(i, _):
        d = (me + i) % count
        came(gw_ref.at[0, d], gws.at[0, d], 0, d).wait_recv()

        @pl.when(two(d % nf))
        def _():
            came(gw_ref.at[1, d], gws.at[1, d], 1, d).wait_recv()

        came(small_ref.at[d], smalls.at[d], 2, d).wait_recv()
        q0, q1, small = copies(d)
        q0.wait_send()

        @pl.when(two(f))
        def _():
            q1.wait_send()

        small.wait_send()

        @pl.when(wanted(f, d))
        def _():
            out_copy(d).wait_send()

        return 0

    lax.fori_loop(1, count, finish, 0)
    for copy in own:
        copy.wait()

    @pl.when(two(f))
    def _():
        own_two.wait()

    @pl.when(wanted(f, me))
    def _():
        own_out.wait()

    owner = owner_of(me)
    next_owner = head_owner((me * dense + dense - 1) // HD)
    for k in range(2 * nz):
        other = k % 2 == 1
        there = ((next_owner != owner) if other else True) & ((k // 2 != z) | (f != owner + k % 2))

        @pl.when(there)
        def _():
            pltpu.make_async_remote_copy(
                gwo_ref.at[0], gwos.at[k], wo_s.at[0], wo_r.at[k], device_id=(z, flip(f, 1)), device_id_type=MESH
            ).wait_recv()

    gwout_ref[...] = sum(gwos[2 * t].astype(F32) for t in range(nz))

    @pl.when(next_owner != owner)
    def _():
        gwout_ref[...] += sum(gwos[2 * t + 1].astype(F32) for t in range(nz))

    width = part_ref.shape[-1]
    for m in range(8):
        for s in range(SLOTS):
            if real[m * SLOTS + s]:
                h = heads[m * SLOTS + s]
                both = sum(gws[s, t * nf + m].astype(F32) for t in range(nz))
                for c in range(3):
                    gwqkv_ref[:, c * width + h * HD : c * width + (h + 1) * HD] = both[:, c * HD : (c + 1) * HD]
    all_small_ref[...] = smalls[...]
    for copy in ups:
        copy.wait()
    reduce.end()
    outs.end()


def finish(part, out_part, gw, gwo, small, geup, tok, mixed, gm, gain, nz, nf):
    rows, width = tok.shape
    count = nz * nf
    dense = width // count
    pieces = geup.reshape(nz, width // nz, geup.shape[1])
    heads, real = head_table(8)
    return pl.pallas_call(
        functools.partial(finish_kernel, nz=nz, nf=nf, heads=heads, real=real),
        out_shape=(
            jax.ShapeDtypeStruct((rows, width), BF16),
            jax.ShapeDtypeStruct((rows, width), BF16),
            jax.ShapeDtypeStruct((dense, 3 * width), F32),
            jax.ShapeDtypeStruct((dense, width), F32),
            jax.ShapeDtypeStruct((count, dense, HD), F32),
            jax.ShapeDtypeStruct(pieces.shape, BF16),
        ),
        in_specs=[VMEM, VMEM, ANY, ANY, ANY, ANY, VMEM, VMEM, VMEM, VMEM],
        out_specs=(VMEM, VMEM, VMEM, VMEM, VMEM, ANY),
        scratch_shapes=[
            pltpu.VMEM((SLOTS, count, dense, 3 * HD), BF16),
            pltpu.VMEM((2 * nz, dense, width), BF16),
            pltpu.VMEM((count, dense, HD), F32),
            *Reduce.scratch(1, rows, width),
            *Reduce.scratch(nz, rows, width),
            *pair_of(Reduce.copies(1)),
            *pair_of(Reduce.copies(nz)),
            pltpu.SemaphoreType.DMA((3, count)),
            pltpu.SemaphoreType.DMA((3, count)),
            pltpu.SemaphoreType.DMA((8,)),
            pltpu.SemaphoreType.DMA((2 * nz,)),
            *pair_of(nz),
            pltpu.SemaphoreType.DMA((5,)),
        ],
        compiler_params=pltpu.CompilerParams(
            collective_id=4, has_side_effects=True, vmem_limit_bytes=56 * 2**20
        ),
        name="finish",
    )(
        part.reshape(1, 8, rows, width), out_part.reshape(nz, 8, rows, width), gw.reshape(SLOTS, count, dense, 3 * HD),
        gwo, small.reshape(count, dense, HD), pieces, tok, mixed, gm, gain,
    )


def unpack_kernel(
    pieces_ref, small_ref, wqkv_ref, gwqkv_ref, gain_ref,
    geup_ref, gsup_ref, grouter_ref, ggain_ref,
    *, shared, experts,
):
    nz = pieces_ref.shape[0]
    hidden = pieces_ref.shape[2] // 4
    for t in range(nz):
        for g in range(2):
            for e in range(2):
                at = (2 * g + e) * hidden
                to = (g * nz + t) * hidden
                geup_ref[e, :, to : to + hidden] = pieces_ref[t, :, at : at + hidden].astype(F32)
    count = small_ref.shape[0]
    total = small_ref[0]
    for d in range(count):
        if d:
            total = total + small_ref[d]
        for g in range(2):
            to = (g * count + d) * shared
            gsup_ref[:, to : to + shared] = small_ref[d, :, g * TAIL : g * TAIL + shared]
    grouter_ref[...] = total[:, shared : shared + experts]
    one = jnp.sum(wqkv_ref[...].astype(F32) * gwqkv_ref[...], axis=-1, keepdims=True) / gain_ref[:, :1].astype(F32)
    ggain_ref[...] = jnp.concatenate([one, total[:, HD - 1 :]], axis=1)


def unpack(pieces, small, wqkv, gwqkv, gains, shared, experts):
    nz, up_rows, packed = pieces.shape
    count, dense, _ = small.shape
    return pl.pallas_call(
        functools.partial(unpack_kernel, shared=shared, experts=experts),
        out_shape=(
            jax.ShapeDtypeStruct((2, up_rows, nz * packed // 2), F32),
            jax.ShapeDtypeStruct((dense, 2 * count * shared), F32),
            jax.ShapeDtypeStruct((dense, experts), F32),
            jax.ShapeDtypeStruct((dense, 2), F32),
        ),
        in_specs=[VMEM] * 5,
        out_specs=(VMEM,) * 4,
        compiler_params=pltpu.CompilerParams(vmem_limit_bytes=32 * 2**20),
        name="unpack",
    )(pieces, small, wqkv, gwqkv, gains)


def tables():
    pos = jnp.arange(SEQ, dtype=F32)
    freqs = ROPE ** (-jnp.arange(HD // 2, dtype=F32) * 2.0 / HD)
    angles = pos[:, None] * freqs[None, :]
    cosine = jnp.concatenate([jnp.cos(angles)] * 2, axis=1)
    sine = jnp.concatenate([-jnp.sin(angles), jnp.sin(angles)], axis=1)
    return cosine, sine


def local_near(
    mesh, tokens, out_grad, segment_ids, expert_ids, attn_gain, ffn_gain, w_qkv, w_out,
    w_router, w_shared_up, w_shared_down, w_expert_up, w_expert_down,
):
    nz, nf = mesh.shape["dp"], mesh.shape["fsdp"]
    rows, width = tokens.shape
    total = rows * nz * nf
    top_k, experts = expert_ids.shape[1], w_router.shape[1]
    dense = w_qkv.shape[0]
    hidden, shared = w_expert_down.shape[1], w_shared_down.shape[0]
    z, f = lax.axis_index("dp"), lax.axis_index("fsdp")
    first, last = first_head(f), first_head(f + 1)
    low, _ = out_blocks(f, dense)

    gains = jnp.stack([attn_gain, ffn_gain], axis=1)
    ids = jnp.concatenate([expert_ids.T, segment_ids[None]], axis=0)
    seq_tok, wq, wo, tail, all_ids = prologue(
        tokens, w_qkv, w_out, w_router, w_shared_up, gains, ids, nz, nf, shared
    )
    real = first + jnp.arange(SLOTS) < last
    w = jnp.where(real[:, None, None], wq.reshape(SLOTS, width, 3 * HD), 0)
    wo = lax.dynamic_slice(wo.reshape(8 * dense, width), (first * HD - low * dense, 0), (SLOTS * HD, width))
    wo = jnp.where(jnp.repeat(real, HD)[:, None], wo, 0)
    tail = tail.reshape(width, 2 * TAIL)
    all_gains = tail[:, TAIL + shared : TAIL + shared + 2].T.astype(F32)
    gain_one, gain_two = all_gains[:1], all_gains[1:]
    router = jnp.pad(tail[:, shared : shared + experts], ((0, 0), (TAIL + shared, TAIL - shared - experts)))
    lane = jnp.arange(HD, dtype=jnp.int32) - TAIL - shared
    chosen = all_ids[:, 0, :, None] == lane
    for k in range(1, top_k):
        chosen = chosen | (all_ids[:, k, :, None] == lane)
    marks = chosen.astype(BF16).reshape(total, HD)
    own_marks = lax.dynamic_slice(marks, ((z * nf + f) * rows, 0), (rows, HD)).astype(F32)
    own = (lane[None, :] == (2 * f + jnp.arange(2, dtype=jnp.int32))[:, None]).astype(F32)
    seg = lax.dynamic_slice(all_ids[:, top_k], (z * nf, 0), (nf, rows)).reshape(SEQ)
    cosine, sine = tables()
    segq = jnp.broadcast_to(seg[:, None], (SEQ, HD))
    segk = jnp.broadcast_to(seg[None, :], (8, SEQ))

    part, normed_one, qkv, attn, lse = attn_forward(
        seq_tok.reshape(SEQ, width), gain_one, w, wo, cosine, sine, segq, segk
    )
    all_normed, all_grad, pieces, mixed, normed = spread(part, tokens, gain_two, out_grad, w_expert_up, nz, nf)
    out_part, gx, geup, gtail, gedown, gsdown = ffn(
        all_normed.reshape(total, width), all_grad.reshape(total, width), marks, own, pieces.reshape(width, 4 * hidden),
        tail, w_expert_down.reshape(2 * hidden, width), w_shared_down,
    )
    seq_gm, grad_mixed, small = turn(gx, out_grad, mixed, normed, router, own_marks, gain_two, nz, nf)
    part_back, gw, gwo = attn_backward(
        seq_gm.reshape(SEQ, width), wo, w, normed_one, qkv, attn, lse, cosine, sine, segq, segk
    )
    gwo = lax.dynamic_update_slice(jnp.zeros((8 * dense, width), BF16), gwo, (first * HD - low * dense, 0))
    block_out, tokens_grad, grad_wqkv, grad_wout, smalls, gpieces = finish(
        part_back, out_part, gw, gwo.reshape(8, dense, width), small + gtail, geup, tokens, mixed, grad_mixed, gain_one,
        nz, nf,
    )
    grad_eup, grad_sup, grad_router, grad_gains = unpack(gpieces, smalls, w_qkv, grad_wqkv, gains, shared, experts)
    return (
        block_out, tokens_grad, grad_gains[:, 0], grad_gains[:, 1], grad_wqkv, grad_wout, grad_router, grad_sup,
        gsdown, grad_eup, gedown.reshape(2, hidden, width),
    )


def local_far(
    mesh, tokens, out_grad, segment_ids, expert_ids, attn_gain, ffn_gain, w_qkv, w_out,
    w_router, w_shared_up, w_shared_down, w_expert_up, w_expert_down,
):
    nz, nf = mesh.shape["dp"], mesh.shape["fsdp"]
    nd = nz * nf
    rows, width = tokens.shape
    group = SEQ // rows
    experts = w_router.shape[1]
    dense = w_qkv.shape[0]
    hidden, shared = w_expert_down.shape[1], w_shared_down.shape[0]
    up_rows = w_expert_up.shape[1]
    both = ("dp", "fsdp")
    groups = None if nf == group else [[a + i for i in range(group)] for a in range(0, nf, group)]
    f = lax.axis_index("fsdp")
    member = lax.rem(f, group)
    heads, real = head_table(group)

    by_head = w_qkv.reshape(dense, 3, HEADS, HD)
    empty = jnp.zeros((dense, 3, HD), BF16)
    cols = jnp.stack([by_head[:, :, h] if r else empty for h, r in zip(heads, real)], axis=0)
    cols = cols.reshape(group, SLOTS, dense, 3 * HD)
    cols = jnp.tile(cols, (nf // group, 1, 1, 1))
    cols = lax.all_to_all(cols, "fsdp", 0, 0, tiled=True)
    w = lax.all_gather(cols, "dp", axis=0, tiled=True).transpose(1, 0, 2, 3).reshape(SLOTS, width, 3 * HD)
    full_out = lax.all_gather(w_out, both, axis=0, tiled=True)
    first = HEADS * member // group
    own_real = (first + jnp.arange(SLOTS) < HEADS * (member + 1) // group).astype(BF16)
    padded = jnp.pad(full_out, ((0, (SLOTS - 1) * HD), (0, 0)))
    wo = lax.dynamic_slice(padded, (first * HD, 0), (SLOTS * HD, width))
    wo = wo * jnp.repeat(own_real, HD)[:, None]
    gains = lax.all_gather(jnp.stack([attn_gain, ffn_gain], axis=1).astype(F32), both, axis=0, tiled=True)
    gain_one, gain_two = gains[:, 0], gains[:, 1]
    router = lax.all_gather(w_router, both, axis=0, tiled=True)
    sup = w_shared_up.reshape(dense, 2, nd, shared).transpose(2, 0, 1, 3).reshape(nd, dense, 2 * shared)
    sup = lax.all_to_all(sup, both, 0, 0, tiled=True).reshape(width, 2, shared)
    eup = w_expert_up.reshape(2, up_rows, 2, nz, hidden).transpose(3, 1, 2, 0, 4)
    eup = lax.all_to_all(eup, "dp", 0, 0, tiled=True).reshape(width, 4 * hidden)
    rest = jnp.zeros((width, TAIL - shared), BF16)
    tail = jnp.concatenate([sup[:, 0], router, rest[:, experts:], sup[:, 1], rest], axis=1)
    chosen = jnp.any(expert_ids[:, :, None] == jnp.arange(experts, dtype=jnp.int32), axis=1)
    at = TAIL + shared
    marks = jnp.pad(chosen.astype(BF16), ((0, 0), (at, HD - experts - at)))
    marks = lax.all_gather(marks, both, axis=0, tiled=True)
    lane = jnp.arange(HD, dtype=jnp.int32)
    own = (lane[None, :] == (at + 2 * f + jnp.arange(2, dtype=jnp.int32))[:, None]).astype(F32)
    cosine, sine = tables()
    seg = lax.all_gather(segment_ids, "fsdp", axis=0, tiled=True, axis_index_groups=groups)
    segq = jnp.broadcast_to(seg[:, None], (SEQ, HD))
    segk = jnp.broadcast_to(seg[None, :], (8, SEQ))

    seq_tokens = lax.all_gather(tokens, "fsdp", axis=0, tiled=True, axis_index_groups=groups)
    part, normed_one, qkv, attn, lse = attn_forward(
        seq_tokens, gain_one[None, :], w, wo, cosine, sine, segq, segk
    )
    projected = lax.psum_scatter(part, "fsdp", scatter_dimension=0, tiled=True, axis_index_groups=groups)
    inputs = tokens.astype(F32)
    mixed = inputs + projected.astype(F32)
    scale_two = rms_scale(mixed)
    normal_two = mixed * scale_two
    normed_two = (normal_two * gain_two).astype(BF16)
    all_normed = lax.all_gather(normed_two, both, axis=0, tiled=True)
    all_grad = lax.all_gather(out_grad, both, axis=0, tiled=True)
    out_part, gx_part, geup, gtail, gedown, gsdown = ffn(
        all_normed, all_grad, marks, own, eup, tail, w_expert_down.reshape(2 * hidden, width), w_shared_down
    )
    gx = lax.psum_scatter(gx_part, both, scatter_dimension=0, tiled=True).astype(F32)
    ffn_out = lax.psum_scatter(out_part, both, scatter_dimension=0, tiled=True).astype(F32)
    block_out = (mixed + ffn_out).astype(BF16)

    logits = jnp.where(chosen, dot(normed_two, router), NEG)
    probs = jax.nn.softmax(logits, axis=-1)
    grad_gates = gx[:, width + at : width + at + experts]
    grad_logits = (
        probs * (grad_gates - jnp.sum(probs * grad_gates, axis=-1, keepdims=True))
    ).astype(BF16)
    grad_router = dot_tn(normed_two, grad_logits)
    grad_normed = gx[:, :width] + dot_nt(grad_logits, router)
    grad_gain_two = jnp.sum(grad_normed * normal_two, axis=0)
    grad_mixed = out_grad.astype(F32) + norm_back(grad_normed, normal_two, scale_two, gain_two)

    seq_gm = lax.all_gather(grad_mixed.astype(BF16), "fsdp", axis=0, tiled=True, axis_index_groups=groups)
    part_back, gw, gwo = attn_backward(
        seq_gm, wo, w, normed_one, qkv, attn, lse, cosine, sine, segq, segk
    )
    grad_normed_one = lax.psum_scatter(
        part_back, "fsdp", scatter_dimension=0, tiled=True, axis_index_groups=groups
    ).astype(F32)
    scale_one = rms_scale(inputs)
    normal_one = inputs * scale_one
    grad_gain_one = jnp.sum(grad_normed_one * normal_one, axis=0)
    tokens_grad = (grad_mixed + norm_back(grad_normed_one, normal_one, scale_one, gain_one)).astype(BF16)

    gw = lax.psum_scatter(gw, "dp", scatter_dimension=1, tiled=True)
    gw = lax.all_to_all(gw.reshape(SLOTS, nf, dense, 3 * HD), "fsdp", 1, 1, tiled=True).astype(F32)
    gw = jnp.sum(gw.reshape(SLOTS, nf // group, group, dense, 3, HD), axis=1)
    picked = [gw[i % SLOTS, i // SLOTS] for i in range(group * SLOTS) if real[i]]
    grad_wqkv = jnp.stack(picked, axis=2).reshape(dense, 3 * width)
    gwo = gwo * jnp.repeat(own_real, HD)[:, None]
    all_gwo = jnp.zeros(((HEADS + SLOTS - 1) * HD, width), BF16)
    all_gwo = lax.dynamic_update_slice(all_gwo, gwo, (first * HD, 0))[: HEADS * HD]
    grad_wout = lax.psum_scatter(all_gwo, both, scatter_dimension=0, tiled=True).astype(F32)
    small = jnp.concatenate([grad_router, grad_gain_one[:, None], grad_gain_two[:, None]], axis=1)
    small = lax.psum_scatter(small, both, scatter_dimension=0, tiled=True)
    gsup = jnp.stack([gtail[:, :shared], gtail[:, TAIL : TAIL + shared]], axis=1)
    gsup = lax.all_to_all(gsup.reshape(nd, dense, 2 * shared).astype(BF16), both, 0, 0, tiled=True)
    grad_sup = gsup.reshape(nd, dense, 2, shared).transpose(1, 2, 0, 3).reshape(dense, 2 * nd * shared).astype(F32)
    geup = lax.all_to_all(geup.reshape(nz, up_rows, 2, 2, hidden), "dp", 0, 0, tiled=True)
    grad_eup = geup.transpose(3, 1, 2, 0, 4).reshape(2, up_rows, 2 * nz * hidden).astype(F32)
    return (
        block_out, tokens_grad, small[:, experts], small[:, experts + 1], grad_wqkv, grad_wout,
        small[:, :experts], grad_sup, gsdown, grad_eup, gedown.reshape(2, hidden, width),
    )


def solution(mesh):
    one, two = P(("dp", "fsdp")), P(("dp", "fsdp"), None)
    three = P("fsdp", "dp", None)

    def local(tokens, *rest):
        near = mesh.shape["fsdp"] == 8 == SEQ // tokens.shape[0] and mesh.shape["dp"] <= 4
        return (local_near if near else local_far)(mesh, tokens, *rest)

    return jax.shard_map(
        local,
        mesh=mesh,
        in_specs=(two, two, one, two, one, one, two, two, two, two, two, three, three),
        out_specs=(two, two, one, one, two, two, two, two, two, three, three),
        check_vma=False,
    )
```

time: 1670 us -> 644 us (0.39)
  waiting for transfers between devices: 1100 us -> 0 us
  Pallas kernels: 0 us -> 593 us
  blocking collectives: 190 us -> 0 us
  matrix products: 137 us -> 0 us
  local copies, waits for them, and re-layouts: 143 us -> 24.7 us
  starting transfers between devices: 37.3 us -> 0 us
  other arithmetic: 41.9 us -> 15.5 us
    reduce_scatter x5 -> x0, waiting for transfers between devices: 700 us -> none  [the longest x1 243 us: local(): lax.psum_scatter(grad_wqkv, ('dp', 'fsdp'), scatter_dimension=0, tiled=True)]
    pallas_call x0 -> x8, Pallas kernels: none -> 593 us  [the longest x1 163 us: finish(): pl.pallas_call(functools.partial(finish_kernel, nz=nz, nf=nf, heads=heads...]
    all_gather x8 -> x0, waiting for transfers between devices: 281 us -> none  [the longest x1 74.5 us: local(): lax.all_gather(w_expert_down, 'dp', axis=1, tiled=True)]
    unnamed x3 -> x0, blocking collectives: 150 us -> none
    dot_general x27 -> x0, matrix products: 137 us -> none  [the longest x5 21.8 us: inner_rows(): lax.dot_general(left, right, (((0,), (0,)), ((), ())), preferred_element_...]
    all_to_all x4 -> x0, waiting for transfers between devices: 89.5 us -> none  [the longest x1 33.3 us: local(): lax.all_to_all(send_rows.reshape(expert_count, capacity, width), 'fsdp',...]
    all_gather x2 -> x0, blocking collectives: 40.1 us -> none  [the longest x1 32.2 us: local(): lax.all_gather(w_router, ('dp', 'fsdp'), axis=0, tiled=True)]
    gather x10 -> x0, local copies, waits for them, and re-layouts: 39.9 us -> none  [the longest x1 8.68 us: local(): grad_back[slot_index].reshape(row_count, top_k, width).astype(jnp.float32)]
  transfers between devices with their start and end apart: 23 -> 0, of which waited for: 16 -> 0; matrix products, arithmetic and copies ran while one was open for 19% -> 0% of each run, Pallas kernels for 0% -> 0%
where the time goes in v1:
time: 644 us; the launch traced here: 634 us
  Pallas kernels  593 us (92%)
  local copies, waits for them, and re-layouts  24.7 us (4%)
  other arithmetic  15.5 us (2%)
    pallas_call x1, Pallas kernels, finish(): pl.pallas_call(functools.partial(finish_kernel, nz=nz, nf=nf, heads=heads...  163 us
    pallas_call x1, Pallas kernels, spread(): pl.pallas_call(functools.partial(spread_kernel, nz=nz, hidden=hidden), ou...  143 us
    pallas_call x1, Pallas kernels, turn(): pl.pallas_call(functools.partial(turn_kernel, nz=nz), out_shape=(jax.Shap...  133 us
    pallas_call x1, Pallas kernels, ffn(): pl.pallas_call(functools.partial(ffn_kernel, hidden=pair // 2, shared=sha...  64.1 us
    pallas_call x1, Pallas kernels, prologue(): pl.pallas_call(functools.partial(prologue_kernel, nz=nz, nf=nf, shared=sh...  56.2 us
    unnamed x57, local copies, waits for them, and re-layouts  20 us
    pallas_call x1, Pallas kernels, attn_backward(): pl.pallas_call(functools.partial(attn_backward_kernel, block=256), out_sh...  17 us
    pallas_call x1, Pallas kernels, attn_forward(): pl.pallas_call(functools.partial(attn_forward_kernel, block=256), out_sha...  13.6 us

profile of v1, /device:TPU:11, one launch (start us, length us, event | category | flops | bytes accessed | tf_op | source)
XLA Modules:
  0.0 634.1 jit_solution(7356037316148278143)
XLA Ops:
  0.7 0.7 pad_maximum_fusion.2
  1.4 0.1 copy.37.gains_ref.gain_ref
  1.5 0.8 copy.36.router_ref
  2.2 0.7 pad_add_fusion.ids_ref
  3.0 1.0 copy-done
  3.9 1.0 copy-done.11
  4.9 0.9 copy-done.15
  5.8 0.9 copy-done.16
  6.7 56.2 %prologue.1 = (bf16[8,128,1280]{2,1,0:T(8,128)(2,1)S(1)}, bf16[2,32,40,384]{3,2,1,0:T(8,128)(2,1)S(1)}, bf16[8,40,1280]{2,1,0:T(8,128)(2,1)S(1)}, bf16[32,40,128]{2,1,0:T(8,128)(2,1)S(1)}, s32[32,8,128]{2,1,0:T(8,128)S(1)}) custom-call(bf16[128,1280]{1,0:T(8,128)(2,1)S(1)} %copy-done, bf16[40,3840]{1,0:T(8,128)(2,1)S(1)} %copy-done.11, ...), custom_call_target="tpu_custom_call" | custom-call | tf_op jit(solution)/shard_map/prologue/pallas_call | solution.py:717
  62.9 1.5 copy-done.17
  64.4 1.7 bitcast_select_fusion.w_ref
  66.1 1.0 dynamic-slice_select_fusion.wo_ref
  67.1 0.1 fusion.3
  67.2 1.0 broadcast_in_dim.67.segq_ref
  68.2 0.6 broadcast_in_dim.68.segk_ref
  68.9 0.2 slice_convert_fusion
  69.0 0.2 copy.42
  69.2 0.6 fusion.4
  69.9 2.0 fusion.2
  71.8 1.3 pad_maximum_fusion
  73.2 13.6 %attn_forward.1 = (bf16[1024,1280]{1,0:T(8,128)(2,1)}, bf16[1024,1280]{1,0:T(8,128)(2,1)}, bf16[1024,768]{1,0:T(8,128)(2,1)}, bf16[1024,256]{1,0:T(8,128)(2,1)}, f32[1024,256]{1,0:T(8,128)}) custom-call(bf16[1024,1280]{1,0:T(8,128)(2,1)} %bitcast.39, f32[1,1280]{1,0:T(1,128)} %get-tuple-element.129.gain_ref, bf16[2,1280,384]{2,1,0:T(8,128)(2,1)} %bitcast_select_fusion.w_ref, ...), custom_call_target="tpu_custom_call" | custom-call | flops 3758096384 | bytes 13107200 | tf_op jit(solution)/shard_map/attn_forward/pallas_call | solution.py:118
  86.7 1.7 copy-done.3
  88.5 143.0 %spread.1 = (bf16[4,8,128,1280]{3,2,1,0:T(8,128)(2,1)}, bf16[4,8,128,1280]{3,2,1,0:T(8,128)(2,1)}, bf16[4,320,896]{2,1,0:T(8,128)(2,1)S(1)}, f32[128,1280]{1,0:T(8,128)S(1)}, bf16[128,1280]{1,0:T(8,128)(2,1)S(1)}) custom-call(bf16[1,8,128,1280]{3,2,1,0:T(8,128)(2,1)S(1)} %bitcast.34, bf16[128,1280]{1,0:T(8,128)(2,1)S(1)} %copy-done.1, ...), custom_call_target="tpu_custom_call" | custom-call | tf_op jit(solution)/shard_map/spread/pallas_call | solution.py:816
  231.5 1.4 copy-done.19
  232.8 5.7 or_convert_fusion.mark_ref
  238.5 0.6 compare_convert_fusion.own_ref
  239.2 64.1 %ffn.1 = (bf16[4096,1280]{1,0:T(8,128)(2,1)}, bf16[4096,1408]{1,0:T(8,128)(2,1)}, bf16[1280,896]{1,0:T(8,128)(2,1)}, f32[1280,128]{1,0:T(8,128)}, f32[448,1280]{1,0:T(8,128)}, /*index=5*/f32[28,1280]{1,0:T(8,128)}) custom-call(bf16[4096,1280]{1,0:T(8,128)(2,1)} %bitcast.61, bf16[4096,1280]{1,0:T(8,128)(2,1)} %bitcast.62, ...), custom_call_target="tpu_custom_call" | custom-call | flops 48318382080 | bytes 41943040 | tf_op jit(solution)/shard_map/ffn/pallas_call | solution.py:288
  303.3 0.8 dynamic-slice_convert_fusion.mark_ref
  304.1 0.2 slice.59
  304.2 0.2 pad.4.router_ref
  304.4 133.0 %turn.1 = (bf16[1,8,128,1280]{3,2,1,0:T(8,128)(2,1)S(1)}, f32[128,1280]{1,0:T(8,128)S(1)}, f32[1280,128]{1,0:T(8,128)S(1)}) custom-call(bf16[4,8,128,1408]{3,2,1,0:T(8,128)(2,1)} %bitcast.42, bf16[128,1280]{1,0:T(8,128)(2,1)S(1)} %copy-done.8, f32[128,1280]{1,0:T(8,128)S(1)} %get-tuple-element.58.mixed_ref, ...), custom_call_target="tpu_custom_call" | custom-call | tf_op jit(solution)/shard_map/turn/pallas_call | solution.py:898
  437.4 0.8 copy-done.13
  438.2 1.5 copy-done.18
  439.7 0.9 add.69
  440.6 17.0 %attn_backward.1 = (bf16[1024,1280]{1,0:T(8,128)(2,1)}, bf16[2,1280,384]{2,1,0:T(8,128)(2,1)}, bf16[256,1280]{1,0:T(8,128)(2,1)}) custom-call(bf16[1024,1280]{1,0:T(8,128)(2,1)} %bitcast.40, bf16[256,1280]{1,0:T(8,128)(2,1)} %dynamic-slice_select_fusion.wo_ref, bf16[2,1280,384]{2,1,0:T(8,128)(2,1)} %bitcast_select_fusion.w_ref, ...), custom_call_target="tpu_custom_call" | custom-call | flops 8053063680 | bytes 13107200 | tf_op jit(solution)/shard_map/attn_backward/pallas_call | solution.py:191
  457.7 1.1 constant_dynamic-update-slice_fusion
  458.8 0.9 copy-done.20
  459.7 162.8 %finish.1 = (bf16[128,1280]{1,0:T(8,128)(2,1)}, bf16[128,1280]{1,0:T(8,128)(2,1)}, f32[40,3840]{1,0:T(8,128)}, f32[40,1280]{1,0:T(8,128)}, f32[32,40,128]{2,1,0:T(8,128)}, /*index=5*/bf16[4,320,896]{2,1,0:T(8,128)(2,1)}) custom-call(bf16[1,8,128,1280]{3,2,1,0:T(8,128)(2,1)} %bitcast.46, bf16[4,8,128,1280]{3,2,1,0:T(8,128)(2,1)} %bitcast.43, ...), custom_call_target="tpu_custom_call" | custom-call | tf_op jit(solution)/shard_map/finish/pallas_call | solution.py:1110
  622.5 1.1 copy-done.4
  623.6 1.6 copy-done.7
  625.3 1.1 copy-done.14
  626.3 3.2 unpack.1
  629.6 0.7 copy.40
  630.2 0.7 slice_reduce_fusion
  630.9 0.7 copy.48
  631.7 0.7 copy.49
  632.4 0.8 copy.50
  633.2 0.7 copy.51
  (44 shorter events, 0.2 us)
Async XLA Ops:
  3.0 1.0 copy-start
  3.9 1.0 copy-start.11
  4.9 0.9 copy-start.15
  5.8 0.9 copy-start.16
  62.9 1.5 copy-start.17
  64.4 4.5 copy-start.9
  73.1 13.6 %copy-start.1 = (bf16[128,1280]{1,0:T(8,128)(2,1)S(1)}, bf16[128,1280]{1,0:T(8,128)(2,1)}, u32[]{:S(2)}) copy-start(bf16[128,1280]{1,0:T(8,128)(2,1)} %tok_ref.5) | copy-start | bytes 983044
  73.1 13.6 %copy-start.6 = (bf16[2,320,1792]{2,1,0:T(8,128)(2,1)S(1)}, bf16[2,320,1792]{2,1,0:T(8,128)(2,1)}, u32[]{:S(2)}) copy-start(bf16[2,320,1792]{2,1,0:T(8,128)(2,1)} %eup_ref.1) | copy-start | bytes 6881284
  73.2 13.6 %copy-start.8 = (bf16[128,1280]{1,0:T(8,128)(2,1)S(1)}, bf16[128,1280]{1,0:T(8,128)(2,1)}, u32[]{:S(2)}) copy-start(bf16[128,1280]{1,0:T(8,128)(2,1)} %og_ref.3) | copy-start | bytes 983044
  86.7 1.7 copy-start.3
  231.4 1.4 copy-start.19
  232.8 71.6 %copy-start.2 = (f32[128,1280]{1,0:T(8,128)}, f32[128,1280]{1,0:T(8,128)S(1)}, u32[]{:S(2)}) copy-start(f32[128,1280]{1,0:T(8,128)S(1)} %get-tuple-element.58.mixed_ref) | copy-start | bytes 1966084
  239.2 64.9 %copy-start.10 = (bf16[32,40,128]{2,1,0:T(8,128)(2,1)S(1)}, bf16[32,40,128]{2,1,0:T(8,128)(2,1)}, u32[]{:S(2)}) copy-start(bf16[32,40,128]{2,1,0:T(8,128)(2,1)} %copy-done.9) | copy-start | bytes 983044
  304.4 135.3 %copy-start.21 = (f32[1280,128]{1,0:T(8,128)S(1)}, f32[1280,128]{1,0:T(8,128)}, u32[]{:S(2)}) copy-start(f32[1280,128]{1,0:T(8,128)} %get-tuple-element.70) | copy-start | bytes 1966084
  437.4 0.8 copy-start.13
  438.2 1.5 copy-start.18
  458.8 0.9 copy-start.20
  459.7 162.8 %copy-start.12 = (bf16[40,3840]{1,0:T(8,128)(2,1)S(1)}, bf16[40,3840]{1,0:T(8,128)(2,1)}, u32[]{:S(2)}) copy-start(bf16[40,3840]{1,0:T(8,128)(2,1)} %wqkv_ref.3) | copy-start | bytes 921604
  622.5 1.1 copy-start.4
  623.6 1.6 copy-start.7
  625.3 1.1 copy-start.14
  626.3 4.6 copy-start.23
  626.3 5.3 copy-start.22
  626.3 6.1 copy-start.5
  629.6 3.7 copy-start.24

commit v2 on v1

v2 whole, which is shorter than its diff:
```python
import functools

import jax
import jax.numpy as jnp
import numpy as np
from jax import lax
from jax.experimental import pallas as pl
from jax.experimental.pallas import tpu as pltpu
from jax.sharding import PartitionSpec as P

HEADS = 10
HD = 128
SEQ = 1024
SLOTS = 2
EPS = 1e-06
ROPE = 10000.0
NEG = -1e30
TAIL = 64
F32 = jnp.float32
BF16 = jnp.bfloat16


MESH = pl.DeviceIdType.MESH
VMEM = pl.BlockSpec(memory_space=pltpu.VMEM)
ANY = pl.BlockSpec(memory_space=pl.ANY)


def up_to(value, step):
    return -(-value // step) * step


def rms_scale(values):
    return lax.rsqrt(jnp.mean(values * values, axis=-1, keepdims=True) + EPS)


def norm_back(grad_normed, normal_rows, scale_rows, gain_rows):
    scaled = grad_normed * gain_rows
    return scale_rows * (
        scaled - normal_rows * jnp.mean(scaled * normal_rows, axis=-1, keepdims=True)
    )


def head_table(group):
    heads, real = [], []
    for i in range(group):
        own = list(range(HEADS * i // group, HEADS * (i + 1) // group))
        assert len(own) <= SLOTS
        heads += own + [0] * (SLOTS - len(own))
        real += [1] * len(own) + [0] * (SLOTS - len(own))
    return heads, real


def dot(a, b):
    return jnp.dot(a, b, preferred_element_type=F32)


def dot_nt(a, b):
    return lax.dot_general(a, b, (((1,), (1,)), ((), ())), preferred_element_type=F32)


def dot_tn(a, b):
    return lax.dot_general(a, b, (((0,), (0,)), ((), ())), preferred_element_type=F32)


def attn_project(i, block, x, gain, w_ref, cos_ref, sin_ref, normed_ref, qkv_ref):
    rows = pl.ds(pl.multiple_of(i * block, block), block)
    x = x.astype(F32)
    normed = (x * rms_scale(x) * gain).astype(BF16)
    normed_ref[rows, :] = normed
    cosine, sine = cos_ref[rows, :], sin_ref[rows, :]
    for s in range(SLOTS):
        proj = dot(normed, w_ref[s])
        for c in range(3):
            piece = proj[:, c * HD : (c + 1) * HD]
            if c < 2:
                piece = piece * cosine + pltpu.roll(piece, HD // 2, 1) * sine
            at = (3 * s + c) * HD
            qkv_ref[rows, at : at + HD] = piece.astype(BF16)


def attn_block(i, block, segq_ref, segk_ref, qkv_ref, attn_ref, lse_ref):
    scale = HD**-0.5
    rows = slice(i * block, (i + 1) * block)
    keys = (i + 1) * block
    row_pos = i * block + lax.broadcasted_iota(jnp.int32, (block, keys), 0)
    key_pos = lax.broadcasted_iota(jnp.int32, (block, keys), 1)
    allowed = (key_pos <= row_pos) & (segq_ref[rows, :1] == segk_ref[:1, :keys])
    outs = []
    for s in range(SLOTS):
        at = 3 * s * HD
        q = qkv_ref[rows, at : at + HD]
        k = qkv_ref[:keys, at + HD : at + 2 * HD]
        v = qkv_ref[:keys, at + 2 * HD : at + 3 * HD]
        scores = jnp.where(allowed, dot_nt(q, k) * scale, NEG)
        top = jnp.max(scores, axis=-1, keepdims=True)
        weights = jnp.exp(scores - top)
        total = jnp.sum(weights, axis=-1, keepdims=True)
        out = dot(weights.astype(BF16), v) / total
        lse_ref[rows, s * HD : (s + 1) * HD] = jnp.broadcast_to(top + jnp.log(total), (block, HD))
        low = out.astype(BF16)
        attn_ref[rows, s * HD : (s + 1) * HD] = low
        outs.append(low)
    return jnp.concatenate(outs, axis=-1)


def attn_forward_kernel(
    tok_ref, gain_ref, w_ref, wo_ref, cos_ref, sin_ref, segq_ref, segk_ref,
    part_ref, normed_ref, qkv_ref, attn_ref, lse_ref,
    *, block,
):
    count = tok_ref.shape[0] // block

    def project(i, _):
        x = tok_ref[pl.ds(pl.multiple_of(i * block, block), block), :]
        attn_project(i, block, x, gain_ref[...], w_ref, cos_ref, sin_ref, normed_ref, qkv_ref)
        return 0

    lax.fori_loop(0, count, project, 0)
    for i in range(count):
        outs = attn_block(i, block, segq_ref, segk_ref, qkv_ref, attn_ref, lse_ref)
        part_ref[i * block : (i + 1) * block, :] = dot(outs, wo_ref[...]).astype(BF16)


def attn_forward(tok, gain, w, wo, cosine, sine, segq, segk):
    length, width = tok.shape
    return pl.pallas_call(
        functools.partial(attn_forward_kernel, block=256),
        out_shape=(
            jax.ShapeDtypeStruct((length, width), BF16),
            jax.ShapeDtypeStruct((length, width), BF16),
            jax.ShapeDtypeStruct((length, 3 * SLOTS * HD), BF16),
            jax.ShapeDtypeStruct((length, SLOTS * HD), BF16),
            jax.ShapeDtypeStruct((length, SLOTS * HD), F32),
        ),
        in_specs=[VMEM] * 8,
        out_specs=(VMEM,) * 5,
        compiler_params=pltpu.CompilerParams(vmem_limit_bytes=56 * 2**20),
        cost_estimate=pl.CostEstimate(
            flops=2 * length * width * 4 * SLOTS * HD + 4 * SLOTS * HD * length * length,
            bytes_accessed=10 * length * width,
            transcendentals=SLOTS * length * length,
        ),
        name="attn_forward",
    )(tok, gain, w, wo, cosine, sine, segq, segk)


def attn_back_block(
    i, block, gm_ref, wo_ref, qkv_ref, attn_ref, lse_ref, cos_ref, sin_ref, segq_ref, segk_ref, gkv_ref, gqkv_ref
):
    scale = HD**-0.5
    rows = slice(i * block, (i + 1) * block)
    keys = (i + 1) * block
    row_pos = i * block + lax.broadcasted_iota(jnp.int32, (block, keys), 0)
    key_pos = lax.broadcasted_iota(jnp.int32, (block, keys), 1)
    allowed = (key_pos <= row_pos) & (segq_ref[rows, :1] == segk_ref[:1, :keys])
    grad_attn = dot_nt(gm_ref[rows, :], wo_ref[...]).astype(BF16)
    for s in range(SLOTS):
        at = 3 * s * HD
        cut = slice(s * HD, (s + 1) * HD)
        q = qkv_ref[rows, at : at + HD]
        k = qkv_ref[:keys, at + HD : at + 2 * HD]
        v = qkv_ref[:keys, at + 2 * HD : at + 3 * HD]
        ga = grad_attn[:, cut]
        delta = jnp.sum(ga.astype(F32) * attn_ref[rows, cut].astype(F32), axis=-1, keepdims=True)
        scores = dot_nt(q, k) * scale
        probs = jnp.where(allowed, jnp.exp(scores - lse_ref[rows, s * HD : s * HD + 1]), 0.0)
        gs = (probs * (dot_nt(ga, v) - delta)).astype(BF16)
        gq = dot(gs, k) * scale
        gq = gq * cos_ref[rows, :] - pltpu.roll(gq, HD // 2, 1) * sin_ref[rows, :]
        gqkv_ref[rows, at : at + HD] = gq.astype(BF16)
        gkv_ref[:keys, 2 * s * HD : (2 * s + 1) * HD] += dot_tn(gs, q)
        gkv_ref[:keys, (2 * s + 1) * HD : (2 * s + 2) * HD] += dot_tn(probs.astype(BF16), ga)


def attn_back_keys(w_ref, cos_ref, sin_ref, gkv_ref, gqkv_ref, wt_ref):
    step = 3 * HD
    for s in range(SLOTS):
        at = s * step
        gk = gkv_ref[:, 2 * s * HD : (2 * s + 1) * HD] * HD**-0.5
        gk = gk * cos_ref[...] - pltpu.roll(gk, HD // 2, 1) * sin_ref[...]
        gqkv_ref[:, at + HD : at + 2 * HD] = gk.astype(BF16)
        gqkv_ref[:, at + 2 * HD : at + 3 * HD] = gkv_ref[:, (2 * s + 1) * HD : (2 * s + 2) * HD].astype(BF16)
        wt_ref[s * step : (s + 1) * step, :] = w_ref[s].T


def attn_backward_kernel(
    gm_ref, wo_ref, w_ref, normed_ref, qkv_ref, attn_ref, lse_ref, cos_ref, sin_ref,
    segq_ref, segk_ref,
    part_ref, gw_ref, gwo_ref,
    gkv_ref, gqkv_ref, wt_ref,
    *, block,
):
    count = gm_ref.shape[0] // block
    step = 3 * HD
    gkv_ref[...] = jnp.zeros_like(gkv_ref)
    for i in range(count):
        attn_back_block(
            i, block, gm_ref, wo_ref, qkv_ref, attn_ref, lse_ref, cos_ref, sin_ref, segq_ref, segk_ref, gkv_ref, gqkv_ref
        )
    attn_back_keys(w_ref, cos_ref, sin_ref, gkv_ref, gqkv_ref, wt_ref)
    for i in range(count):
        rows = slice(i * block, (i + 1) * block)
        part_ref[rows, :] = dot(gqkv_ref[rows, :], wt_ref[...]).astype(BF16)
    for s in range(SLOTS):
        gw_ref[s] = dot_tn(normed_ref[...], gqkv_ref[:, s * step : (s + 1) * step]).astype(BF16)
    gwo_ref[...] = dot_tn(attn_ref[...], gm_ref[...]).astype(BF16)


def attn_backward(gm, wo, w, normed, qkv, attn, lse, cosine, sine, segq, segk):
    length, width = gm.shape
    return pl.pallas_call(
        functools.partial(attn_backward_kernel, block=256),
        out_shape=(
            jax.ShapeDtypeStruct((length, width), BF16),
            jax.ShapeDtypeStruct((SLOTS, width, 3 * HD), BF16),
            jax.ShapeDtypeStruct((SLOTS * HD, width), BF16),
        ),
        in_specs=[VMEM] * 11,
        out_specs=(VMEM,) * 3,
        scratch_shapes=[
            pltpu.VMEM((length, 2 * SLOTS * HD), F32),
            pltpu.VMEM((length, 3 * SLOTS * HD), BF16),
            pltpu.VMEM((3 * SLOTS * HD, width), BF16),
        ],
        compiler_params=pltpu.CompilerParams(vmem_limit_bytes=56 * 2**20),
        cost_estimate=pl.CostEstimate(
            flops=4 * length * width * 4 * SLOTS * HD + 10 * SLOTS * HD * length * length,
            bytes_accessed=10 * length * width,
            transcendentals=SLOTS * length * length,
        ),
        name="attn_backward",
    )(gm, wo, w, normed, qkv, attn, lse, cosine, sine, segq, segk)


def ffn_weights(eup_ref, tail_ref, edown_ref, sdown_ref, up_ref, upt_ref, down_ref, downt_ref):
    width, half = downt_ref.shape
    pair, shared = edown_ref.shape[0], sdown_ref.shape[0]
    gap = half - pair - TAIL
    between = [jnp.zeros((width, gap), BF16)] if gap else []
    up_ref[...] = jnp.concatenate(
        [eup_ref[:, :pair], *between, tail_ref[:, :TAIL], eup_ref[:, pair:], *between, tail_ref[:, TAIL:]], axis=1
    )
    between = [jnp.zeros((gap, width), BF16)] if gap else []
    down_ref[...] = jnp.concatenate(
        [edown_ref[...], *between, sdown_ref[...], jnp.zeros((TAIL - shared, width), BF16)], axis=0
    )
    upt_ref[...] = up_ref[...].T
    downt_ref[...] = down_ref[...].T


def ffn_rows(x, g, marks, own, up_ref, upt_ref, down_ref, downt_ref, hidden, shared):
    half = down_ref.shape[0]
    pair = 2 * hidden
    pre = dot(x, up_ref[...])
    gate, up = pre[:, :half], pre[:, half:]
    logits = jnp.where(marks.astype(F32) > 0.5, gate[:, half - HD :], NEG)
    weights = jnp.exp(logits - jnp.max(logits, axis=-1, keepdims=True))
    probs = weights / jnp.sum(weights, axis=-1, keepdims=True)
    p0 = jnp.sum(probs * own[0:1, :], axis=-1, keepdims=True)
    p1 = jnp.sum(probs * own[1:2, :], axis=-1, keepdims=True)
    lane = lax.broadcasted_iota(jnp.int32, (1, half), 1)
    in0 = lane < hidden
    in1 = (lane >= hidden) & (lane < pair)
    rest = jnp.where((lane >= half - TAIL) & (lane < half - TAIL + shared), 1.0, 0.0)
    weight = jnp.where(in0, p0, jnp.where(in1, p1, rest))
    sig = jax.nn.sigmoid(gate)
    silu = gate * sig
    act = silu * up
    acts = (act * weight).astype(BF16)
    out = dot(acts, down_ref[...]).astype(BF16)
    grad = dot(g, downt_ref[...])
    both = act * grad
    d0 = jnp.sum(jnp.where(in0, both, 0.0), axis=-1, keepdims=True)
    d1 = jnp.sum(jnp.where(in1, both, 0.0), axis=-1, keepdims=True)
    grad = grad * weight
    grad_gate = grad * up * sig * (1.0 + gate * (1.0 - sig))
    grad_up = grad * silu
    grad_pre = jnp.concatenate([grad_gate, grad_up], axis=-1).astype(BF16)
    gates = (d0 * own[0:1, :] + d1 * own[1:2, :]).astype(BF16)
    gx = jnp.concatenate([dot(grad_pre, upt_ref[...]).astype(BF16), gates], axis=-1)
    return out, gx, grad_pre, acts


def ffn_kernel(
    x_ref, g_ref, mark_ref, own_ref, eup_ref, tail_ref, edown_ref, sdown_ref,
    out_ref, gx_ref, geup_ref, gtail_ref, gedown_ref, gsdown_ref,
    up_ref, upt_ref, down_ref, downt_ref, gup_ref, gdown_ref,
    *, hidden, shared,
):
    step = pl.program_id(0)
    half = down_ref.shape[0]
    pair = 2 * hidden

    @pl.when(step == 0)
    def _():
        gup_ref[...] = jnp.zeros_like(gup_ref)
        gdown_ref[...] = jnp.zeros_like(gdown_ref)
        ffn_weights(eup_ref, tail_ref, edown_ref, sdown_ref, up_ref, upt_ref, down_ref, downt_ref)

    out, gx, grad_pre, acts = ffn_rows(
        x_ref[...], g_ref[...], mark_ref[...], own_ref[...], up_ref, upt_ref, down_ref, downt_ref, hidden, shared
    )
    out_ref[...] = out
    gx_ref[...] = gx
    gup_ref[...] += dot_tn(x_ref[...], grad_pre)
    gdown_ref[...] += dot_tn(acts, g_ref[...])

    @pl.when(step == pl.num_programs(0) - 1)
    def _():
        geup_ref[...] = jnp.concatenate([gup_ref[:, :pair], gup_ref[:, half : half + pair]], axis=1).astype(BF16)
        gtail_ref[...] = jnp.concatenate([gup_ref[:, half - TAIL : half], gup_ref[:, 2 * half - TAIL :]], axis=1)
        gedown_ref[...] = gdown_ref[:pair, :]
        gsdown_ref[...] = gdown_ref[half - TAIL : half - TAIL + shared, :]


def ffn(x, g, marks, own, eup, tail, edown, sdown):
    total, width = x.shape
    pair, shared = edown.shape[0], sdown.shape[0]
    half = up_to(pair + TAIL, HD)
    tile = 512
    row = lambda n: pl.BlockSpec((tile, n), lambda i: (i, 0))
    return pl.pallas_call(
        functools.partial(ffn_kernel, hidden=pair // 2, shared=shared),
        out_shape=(
            jax.ShapeDtypeStruct((total, width), BF16),
            jax.ShapeDtypeStruct((total, width + HD), BF16),
            jax.ShapeDtypeStruct((width, 2 * pair), BF16),
            jax.ShapeDtypeStruct((width, HD), F32),
            jax.ShapeDtypeStruct((pair, width), F32),
            jax.ShapeDtypeStruct((shared, width), F32),
        ),
        grid=(total // tile,),
        in_specs=[row(width), row(width), row(HD)] + [VMEM] * 5,
        out_specs=(row(width), row(width + HD), VMEM, VMEM, VMEM, VMEM),
        scratch_shapes=[
            pltpu.VMEM((width, 2 * half), BF16),
            pltpu.VMEM((2 * half, width), BF16),
            pltpu.VMEM((half, width), BF16),
            pltpu.VMEM((width, half), BF16),
            pltpu.VMEM((width, 2 * half), F32),
            pltpu.VMEM((half, width), F32),
        ],
        compiler_params=pltpu.CompilerParams(vmem_limit_bytes=60 * 2**20),
        cost_estimate=pl.CostEstimate(
            flops=2 * total * width * 9 * half,
            bytes_accessed=8 * total * width,
            transcendentals=total * half,
        ),
        name="ffn",
    )(x, g, marks, own, eup, tail, edown, sdown)


def flip(f, bits):
    for b in (1, 2, 4):
        if bits & b:
            f = f + b - 2 * b * (f // b % 2)
    return f


def place():
    return lax.axis_index("dp"), lax.axis_index("fsdp")


def greet(devices):
    barrier = pltpu.get_barrier_semaphore()
    for device in devices:
        pl.semaphore_signal(barrier, inc=1, device_id=device, device_id_type=MESH)
    pl.semaphore_wait(barrier, len(devices))


def greet_all(nz, nf):
    barrier = pltpu.get_barrier_semaphore()
    z, f = place()
    me, count = z * nf + f, nz * nf

    def hail(i, _):
        d = (me + i) % count
        pl.semaphore_signal(barrier, inc=1, device_id=(d // nf, d % nf), device_id_type=MESH)
        return 0

    lax.fori_loop(1, count, hail, 0)
    pl.semaphore_wait(barrier, count - 1)


def send(src, dst, sems, index, device):
    return pltpu.make_async_remote_copy(
        src, dst, sems[0].at[index], sems[1].at[index], device_id=device, device_id_type=MESH
    )


ORDER = ((2, 4), (4, 2))


def halves(rows):
    return ((0, rows // 2), (rows // 2, rows - rows // 2))


def away(j, nz):
    if nz < 3:
        return j
    if isinstance(j, int):
        return j if j < 2 else nz - 1 if j == 2 else j - 1
    return jnp.where(j < 2, j, jnp.where(j == 2, nz - 1, j - 1))


class Gather:
    @staticmethod
    def copies(nz):
        return 11 * nz

    def __init__(self, buf, sems, nz, z, f):
        self.buf, self.sems, self.nz, self.z, self.f = buf, sems, nz, z, f

    def slot(self, j, r, h=None):
        piece = lax.rem(self.z - away(j, self.nz) + self.nz, self.nz) if self.nz > 1 else 0
        ref = self.buf.at[piece, flip(self.f, r)]
        return ref if h is None else ref.at[pl.ds(*halves(self.buf.shape[-2])[h])]

    def here(self, j, r, h, index, device):
        ref = self.slot(j, r, h)
        return send(ref, ref, self.sems, index, device)

    def by_z(self, j):
        own = self.slot(0, 0)
        return send(own, own, self.sems, j, (lax.rem(self.z + away(j, self.nz), self.nz), self.f))

    def near(self, j, h):
        return self.here(j, 0, h, self.nz + 2 * j + h, (self.z, flip(self.f, ORDER[h][0])))

    def far(self, j, h, i):
        r = ORDER[h][0] if i else 0
        return self.here(j, r, h, 3 * self.nz + 4 * j + 2 * h + i, (self.z, flip(self.f, ORDER[h][1])))

    def core(self, j, i):
        return self.here(j, 2 * i, None, 7 * self.nz + 4 * j + i, (self.z, flip(self.f, 1)))

    def along_z(self, j):
        if 1 < j <= self.nz:
            self.by_z(j - 1).wait_send()
        if j < self.nz:
            self.by_z(j).start()

    def first(self, j, own=False):
        if not own:
            self.by_z(j).wait_recv()
        for h in range(2):
            self.near(j, h).start()
        self.core(j, 0).start()

    def second(self, j):
        for h in range(2):
            self.near(j, h).wait_recv()
            for i in range(2):
                self.far(j, h, i).start()

    def third(self, j):
        for h in range(2):
            for i in range(2):
                self.far(j, h, i).wait_recv()
        for i in range(1, 4):
            self.core(j, i).start()

    def fourth(self, j):
        for i in range(4):
            self.core(j, i).wait_recv()

    def end(self, first=0):
        for j in range(first, self.nz):
            for h in range(2):
                self.near(j, h).wait_send()
                for i in range(2):
                    self.far(j, h, i).wait_send()
            for i in range(4):
                self.core(j, i).wait_send()


class Reduce:
    @staticmethod
    def copies(nz):
        return 11 * nz

    @staticmethod
    def scratch(nz, rows, width):
        return [
            pltpu.VMEM((nz, 4, rows, width), BF16),
            pltpu.VMEM((nz, 2, rows, width), BF16),
            pltpu.VMEM((nz, rows, width), BF16),
            pltpu.VMEM((nz, rows, width), BF16),
        ]

    def __init__(self, bufs, sems, nz, z, f):
        self.by_core, self.by_near, self.by_far, self.by_z = bufs
        self.sems, self.nz, self.z, self.f = sems, nz, z, f
        self.parts = halves(self.by_core.shape[-2])

    def core(self, j, i, src):
        to = self.by_core.at[j, i]
        return send(to if src is None else src, to, self.sems, 4 * j + i, (self.z, flip(self.f, 1)))

    def near(self, j, h, i):
        last = ORDER[1 - h][1]
        rows = pl.ds(*self.parts[h])
        return send(
            self.by_core.at[j, 3 if i else last // 2, rows], self.by_near.at[j, i, rows], self.sems,
            4 * self.nz + 4 * j + 2 * h + i, (self.z, flip(self.f, last)),
        )

    def far_copy(self, j, h):
        rows = pl.ds(*self.parts[h])
        return send(
            self.by_near.at[j, 1, rows], self.by_far.at[j, rows], self.sems,
            8 * self.nz + 2 * j + h, (self.z, flip(self.f, ORDER[1 - h][0])),
        )

    def z_copy(self, j):
        there = lax.rem(self.z - away(j, self.nz) + self.nz, self.nz)
        return send(self.by_far.at[j], self.by_z.at[j], self.sems, 10 * self.nz + j, (there, self.f))

    def send_near(self, j):
        for h in range(2):
            for i in range(2):
                self.near(j, h, i).start()

    def far(self, j):
        for h in range(2):
            at, size = self.parts[h]
            rows = slice(at, at + size)
            for i, r in enumerate((0, ORDER[1 - h][0])):
                self.near(j, h, i).wait_recv()
                self.by_near[j, i, rows] = self.by_near[j, i, rows] + self.by_core[j, r // 2, rows]
            self.far_copy(j, h).start()

    def along_z(self, j):
        for h in range(2):
            at, size = self.parts[h]
            rows = slice(at, at + size)
            self.far_copy(j, h).wait_recv()
            self.by_far[j, rows] = self.by_far[j, rows] + self.by_near[j, 0, rows]
        if isinstance(j, int):
            if j:
                self.z_copy(j).start()
        else:

            @pl.when(j > 0)
            def _():
                self.z_copy(j).start()

    def total(self):
        result = self.by_far[0].astype(F32)
        for j in range(1, self.nz):
            self.z_copy(j).wait_recv()
            result = result + self.by_z[j].astype(F32)
        return result

    def end(self):
        for j in range(self.nz):
            for h in range(2):
                for i in range(2):
                    self.near(j, h, i).wait_send()
                self.far_copy(j, h).wait_send()
            if j:
                self.z_copy(j).wait_send()


def near_devices(z, f):
    return [(z, flip(f, 1)), (z, flip(f, 2)), (z, flip(f, 4))]


def z_devices(z, f, nz):
    return [(lax.rem(z + zr, nz), f) for zr in range(1, nz)]


def pair_of(count):
    return [pltpu.SemaphoreType.DMA((count,))] * 2


def first_head(member):
    return HEADS * member // 8


def out_blocks(member, dense):
    return first_head(member) * HD // dense, (first_head(member + 1) * HD - 1) // dense


def head_owner(head):
    return (8 * head + 7) // HEADS


def front_kernel(
    tok_ref, wqkv_ref, wout_ref, router_ref, sup_ref, gains_ref, ids_ref, cos_ref, sin_ref, og_ref, eup_ref,
    w_ref, wo_ref, tail_ref, gain_ref, mark_ref, own_mark_ref, segq_ref, segk_ref,
    normed_ref, qkv_ref, attn_ref, lse_ref, mixed_ref, low_ref, plane_ref, all_grad_ref, pieces_ref,
    seq, wq, wo_in, all_ids, qpack, tpack, part, wide, pack, *refs, nz, nf, hidden, shared, heads, real,
):
    bufs, refs = refs[:4], refs[4:]
    tok_s, tok_r, all_s, all_r, wo_s, wo_r, rs, rr, gs, gr, xs, xr, es, er, own_sems = refs
    z, f = place()
    me, count = z * nf + f, nz * nf
    rows, width = tok_ref.shape
    dense = wqkv_ref.shape[0]
    experts = router_ref.shape[1]
    full = shared * count
    greet_all(nz, nf)

    toks = (tok_s, tok_r)
    to_near = [send(tok_ref, seq.at[f], toks, i, (z, flip(f, r))) for i, r in enumerate((2, 4, 6))]
    to_core = [send(tok_ref, seq.at[f], toks, 3, (z, flip(f, 1)))]
    own = [
        pltpu.make_async_copy(tok_ref, seq.at[f], own_sems.at[0]),
        pltpu.make_async_copy(ids_ref, all_ids.at[me], own_sems.at[1]),
        pltpu.make_async_copy(og_ref, all_grad_ref.at[z, f], own_sems.at[2]),
    ]
    for copy in to_near + to_core + own:
        copy.start()

    for m in range(8):
        for s in range(SLOTS):
            h = heads[m * SLOTS + s]
            if real[m * SLOTS + s]:
                qpack[m, s] = jnp.concatenate(
                    [wqkv_ref[:, c * width + h * HD : c * width + (h + 1) * HD] for c in range(3)], axis=1
                )
    pad = jnp.zeros((dense, TAIL - shared - experts), BF16)
    pad_two = jnp.zeros((dense, TAIL - shared - 2), BF16)
    for d in range(count):
        tpack[d] = jnp.concatenate(
            [
                sup_ref[:, d * shared : (d + 1) * shared], router_ref[...], pad,
                sup_ref[:, full + d * shared : full + (d + 1) * shared], gains_ref[...], pad_two,
            ],
            axis=1,
        )

    def two(m):
        return first_head(m + 1) - first_head(m) == 2

    def copies(d, k):
        src, dst = (
            (qpack.at[d % nf, 0], wq.at[0, me]),
            (qpack.at[d % nf, 1], wq.at[1, me]),
            (tpack.at[d], tail_ref.at[me]),
            (ids_ref, all_ids.at[me]),
        )[k]
        return pltpu.make_async_remote_copy(
            src, dst, all_s.at[k, d], all_r.at[k, me], device_id=(d // nf, d % nf), device_id_type=MESH
        )

    def came(d, k):
        dst = (wq.at[0, d], wq.at[1, d], tail_ref.at[d], all_ids.at[d])[k]
        return pltpu.make_async_remote_copy(
            dst, dst, all_s.at[k, d], all_r.at[k, d], device_id=(d // nf, d % nf), device_id_type=MESH
        )

    def out_copy(d):
        first, _ = out_blocks(d % nf, dense)
        return pltpu.make_async_remote_copy(
            wout_ref, wo_in.at[me - first], wo_s.at[d], wo_r.at[me - first],
            device_id=(d // nf, d % nf), device_id_type=MESH,
        )

    def wanted(d, block):
        low, high = out_blocks(d % nf, dense)
        return (low <= block) & (block <= high)

    def start(i, _):
        d = (me + i) % count
        copies(d, 0).start()

        @pl.when(two(d % nf))
        def _():
            copies(d, 1).start()

        copies(d, 2).start()
        copies(d, 3).start()
        return 0

    lax.fori_loop(1, count, start, 0)

    def start_out(i, _):
        d = (me + i) % count

        @pl.when(wanted(d, me))
        def _():
            out_copy(d).start()

        return 0

    lax.fori_loop(1, count, start_out, 0)
    own_packs = [
        pltpu.make_async_copy(qpack.at[f, 0], wq.at[0, me], own_sems.at[3]),
        pltpu.make_async_copy(tpack.at[me], tail_ref.at[me], own_sems.at[4]),
    ]
    for copy in own_packs:
        copy.start()
    own_two = pltpu.make_async_copy(qpack.at[f, 1], wq.at[1, me], own_sems.at[5])
    low, high = out_blocks(f, dense)
    own_out = pltpu.make_async_copy(wout_ref, wo_in.at[me - low], own_sems.at[6])

    @pl.when(two(f))
    def _():
        own_two.start()

    @pl.when(wanted(me, me))
    def _():
        own_out.start()

    whole = nz * hidden
    for t in range(nz):
        pack[t] = jnp.concatenate(
            [
                eup_ref[e, :, g * whole + t * hidden : g * whole + (t + 1) * hidden]
                for g in range(2)
                for e in range(2)
            ],
            axis=1,
        )
    for i, r in enumerate((2, 4, 6)):
        to_near[i].wait_recv()
        slot = seq.at[flip(f, r)]
        copy = send(slot, slot, toks, 4 + i, (z, flip(f, 1)))
        copy.start()
        to_core.append(copy)

    def arrive(i, _):
        d = (me + i) % count
        came(d, 0).wait_recv()

        @pl.when(two(f))
        def _():
            came(d, 1).wait_recv()

        came(d, 2).wait_recv()
        came(d, 3).wait_recv()
        return 0

    lax.fori_loop(1, count, arrive, 0)
    for copy in own + own_packs:
        copy.wait()

    @pl.when(two(f))
    def _():
        own_two.wait()

    for copy in to_core:
        copy.wait_recv()

    grads = Gather(all_grad_ref, (gs, gr), nz, z, f)
    grads.along_z(1)
    grads.first(0, own=True)

    w_ref[0] = wq[0].reshape(width, 3 * HD)
    w_ref[1] = jnp.where(two(f), wq[1].astype(F32), 0.0).reshape(width, 3 * HD).astype(BF16)
    gain_ref[...] = tail_ref[...].reshape(width, 2 * TAIL)[:, TAIL + shared : TAIL + shared + 2].astype(F32).T
    for m in range(8):
        ids = all_ids[z * nf + m]
        segk_ref[:, m * rows : (m + 1) * rows] = jnp.broadcast_to(ids[-1:], (8, rows))
        segq_ref[m * rows : (m + 1) * rows, :] = jnp.broadcast_to(ids.T[:, -1:], (rows, HD))
    block = 256
    gain_one = gain_ref[0:1, :]

    def project(i, _):
        x = seq[pl.ds(i * (block // rows), block // rows)].reshape(block, width)
        attn_project(i, block, x, gain_one, w_ref, cos_ref, sin_ref, normed_ref, qkv_ref)
        return 0

    lax.fori_loop(0, 8 * rows // block, project, 0)
    grads.second(0)
    grads.along_z(2)

    def arrive_out(j, _):
        @pl.when((low + j <= high) & (low + j != me))
        def _():
            pltpu.make_async_remote_copy(
                wo_in.at[j], wo_in.at[j], wo_s.at[j], wo_r.at[j], device_id=(z, flip(f, 1)), device_id_type=MESH
            ).wait_recv()

        return 0

    lax.fori_loop(0, wo_in.shape[0], arrive_out, 0)

    @pl.when(wanted(me, me))
    def _():
        own_out.wait()

    wide[...] = wo_in[...].astype(F32).reshape(wide.shape)
    offset = pl.multiple_of(first_head(f) * HD - low * dense, 8)
    wo_ref[:HD, :] = wide[pl.ds(offset, HD), :].astype(BF16)
    wo_ref[HD:, :] = jnp.where(two(f), wide[pl.ds(offset + HD, HD), :], 0.0).astype(BF16)
    reduce = Reduce(bufs, (rs, rr), 1, z, f)
    for i in range(8 * rows // block):
        outs = attn_block(i, block, segq_ref, segk_ref, qkv_ref, attn_ref, lse_ref)
        at = i * (block // rows)
        part[at : at + block // rows] = dot(outs, wo_ref[...]).astype(BF16).reshape(block // rows, rows, width)
        if i == 1:
            grads.third(0)
    for i in range(4):
        reduce.core(0, i, part.at[flip(f, 1 | 2 * i)]).start()
    for i in range(4):
        reduce.core(0, i, None).wait_recv()
        reduce.by_core[0, i] = reduce.by_core[0, i] + part[flip(f, 2 * i)]
    reduce.send_near(0)
    grads.along_z(3)
    reduce.far(0)
    reduce.along_z(0)
    mixed = tok_ref[...].astype(F32) + reduce.by_far[0].astype(F32)
    mixed_ref[...] = mixed
    low_ref[...] = (mixed * rms_scale(mixed) * gain_ref[1:2, :]).astype(BF16)
    near_own = pltpu.make_async_copy(low_ref, plane_ref.at[0, f], own_sems.at[7])
    near_own.start()
    near = Gather(plane_ref, (xs, xr), 1, z, f)
    near_own.wait()
    near.first(0, own=True)

    ups = []
    for j in range(1, nz):
        there = lax.rem(z + j, nz)
        copy = send(pack.at[there], pieces_ref.at[z], (es, er), j, (there, f))
        copy.start()
        ups.append(copy)
    ups.append(pltpu.make_async_copy(pack.at[z], pieces_ref.at[z], own_sems.at[8]))
    ups[-1].start()

    near.second(0)
    lane = lax.broadcasted_iota(jnp.int32, (rows, HD), 1) - TAIL - shared

    def mark(d, _):
        ids = all_ids[d].T
        found = ids[:, 0:1] == lane
        for k in range(1, ids.shape[1] - 1):
            found = found | (ids[:, k : k + 1] == lane)
        value = jnp.where(found, 1.0, 0.0)
        mark_ref[d] = value.astype(BF16)

        @pl.when(d == me)
        def _():
            own_mark_ref[...] = value

        return 0

    lax.fori_loop(0, count, mark, 0)
    near.third(0)
    for j in range(1, nz):
        grads.first(j)
        grads.second(j)
        if j + 3 <= nz:
            grads.along_z(j + 3)
        grads.third(j)
    for j in range(nz):
        grads.fourth(j)
    near.fourth(0)

    def left(i, _):
        d = (me + i) % count
        copies(d, 0).wait_send()

        @pl.when(two(d % nf))
        def _():
            copies(d, 1).wait_send()

        copies(d, 2).wait_send()
        copies(d, 3).wait_send()

        @pl.when(wanted(d, me))
        def _():
            out_copy(d).wait_send()

        return 0

    lax.fori_loop(1, count, left, 0)
    for copy in to_near + to_core:
        copy.wait_send()
    for i in range(4):
        reduce.core(0, i, part.at[0]).wait_send()
    reduce.end()
    grads.end()
    near.end()
    for copy in ups:
        copy.wait()


def front(tok, wqkv, wout, router, sup, gains, ids, cosine, sine, og, eup, nz, nf, shared):
    rows, width = tok.shape
    dense, count = wqkv.shape[0], nz * nf
    length = 8 * rows
    hidden, up_rows = eup.shape[2] // (2 * nz), eup.shape[1]
    heads, real = head_table(8)
    shape = jax.ShapeDtypeStruct
    return pl.pallas_call(
        functools.partial(front_kernel, nz=nz, nf=nf, hidden=hidden, shared=shared, heads=heads, real=real),
        out_shape=(
            shape((SLOTS, width, 3 * HD), BF16),
            shape((SLOTS * HD, width), BF16),
            shape((count, dense, 2 * TAIL), BF16),
            shape((2, width), F32),
            shape((count, rows, HD), BF16),
            shape((rows, HD), F32),
            shape((length, HD), jnp.int32),
            shape((8, length), jnp.int32),
            shape((length, width), BF16),
            shape((length, 3 * SLOTS * HD), BF16),
            shape((length, SLOTS * HD), BF16),
            shape((length, SLOTS * HD), F32),
            shape((rows, width), F32),
            shape((rows, width), BF16),
            shape((1, 8, rows, width), BF16),
            shape((nz, 8, rows, width), BF16),
            shape((nz, up_rows, 4 * hidden), BF16),
        ),
        in_specs=[VMEM] * 9 + [ANY, VMEM],
        out_specs=(VMEM,) * 14 + (ANY,) * 3,
        scratch_shapes=[
            pltpu.VMEM((8, rows, width), BF16),
            pltpu.VMEM((SLOTS, count, dense, 3 * HD), BF16),
            pltpu.VMEM((8, dense, width), BF16),
            pltpu.VMEM((count, *ids.shape), jnp.int32),
            pltpu.VMEM((8, SLOTS, dense, 3 * HD), BF16),
            pltpu.VMEM((count, dense, 2 * TAIL), BF16),
            pltpu.VMEM((8, rows, width), BF16),
            pltpu.VMEM((8 * dense, width), F32),
            pltpu.VMEM((nz, up_rows, 4 * hidden), BF16),
            *Reduce.scratch(1, rows, width),
            *pair_of(7),
            pltpu.SemaphoreType.DMA((4, count)),
            pltpu.SemaphoreType.DMA((4, count)),
            pltpu.SemaphoreType.DMA((count,)),
            pltpu.SemaphoreType.DMA((8,)),
            *pair_of(Reduce.copies(1)),
            *pair_of(Gather.copies(nz)),
            *pair_of(Gather.copies(1)),
            *pair_of(nz),
            pltpu.SemaphoreType.DMA((9,)),
        ],
        compiler_params=pltpu.CompilerParams(
            collective_id=1, has_side_effects=True, vmem_limit_bytes=58 * 2**20
        ),
        name="front",
    )(tok, wqkv, wout, router, sup, gains, ids, cosine, sine, og, eup)


def route_grads(gx, og, mixed, normed, router, marks, gain):
    width = mixed.shape[1]
    scale = rms_scale(mixed)
    normal = mixed * scale
    logits = jnp.where(marks > 0.5, dot(normed, router), NEG)
    weights = jnp.exp(logits - jnp.max(logits, axis=-1, keepdims=True))
    probs = weights / jnp.sum(weights, axis=-1, keepdims=True)
    grad_gates = gx[:, width:]
    grad_logits = (probs * (grad_gates - jnp.sum(probs * grad_gates, axis=-1, keepdims=True))).astype(BF16)
    grad_router = dot_tn(normed, grad_logits)
    grad_normed = gx[:, :width] + dot_nt(grad_logits, router)
    ones = jnp.where(lax.broadcasted_iota(jnp.int32, (mixed.shape[0], HD), 1) == TAIL - 1, 1.0, 0.0)
    grad_gain = lax.dot_general(
        grad_normed * normal, ones, (((0,), (0,)), ((), ())),
        precision=lax.Precision.HIGHEST, preferred_element_type=F32,
    )
    grad_mixed = og.astype(F32) + norm_back(grad_normed, normal, scale, gain)
    return grad_mixed, pltpu.roll(grad_router + grad_gain, TAIL, 1)


def experts_kernel(
    normed_ref, plane_ref, all_grad_ref, mark_ref, own_ref, eup_ref, tail_ref, edown_ref, sdown_ref,
    og_ref, mixed_ref, router_ref, own_mark_ref, gain_ref,
    out_ref, seq_ref, gm_ref, small_ref, pieces_ref, gedown_ref, gsdown_ref, all_normed_ref,
    up_ref, upt_ref, down_ref, downt_ref, gup_ref, gdown_ref,
    xt, gt, mt, px, po, low, *refs, nz, hidden, shared,
):
    bufs, (tile_sems, rs, rr, os_, or_, xs, xr, gs, gr, es, er, own_sems) = refs[:4], refs[4:]
    z, f = place()
    rows, width = mixed_ref.shape
    half = down_ref.shape[0]
    pair = 2 * hidden
    greet(near_devices(z, f) + z_devices(z, f, nz))
    own = pltpu.make_async_copy(normed_ref, all_normed_ref.at[z, f], own_sems.at[0])
    own.start()
    gather = Gather(all_normed_ref, (xs, xr), nz, z, f)
    reduce = Reduce(bufs, (rs, rr), nz, z, f)
    outs = Reduce([out_ref, out_ref, out_ref, out_ref], (os_, or_), nz, z, f)
    own.wait()
    gather.along_z(1)
    ffn_weights(eup_ref, tail_ref, edown_ref, sdown_ref, up_ref, upt_ref, down_ref, downt_ref)
    gup_ref[...] = jnp.zeros_like(gup_ref)
    gdown_ref[...] = jnp.zeros_like(gdown_ref)
    gather.along_z(2)
    if nz > 1:
        gather.first(1)

    def loads(i, rows_ref=all_normed_ref):
        j, t, slot = i // 4, i % 4, i % 2
        piece = lax.rem(z - away(j, nz) + nz, nz)
        base = f + (1 - 2 * (f % 2)) * (1 - t // 2) + (4 - 8 * (f // 4 % 2)) * (t % 2)
        copies = []
        for b in range(2):
            block = flip(base, 2 * b)
            there = piece if rows_ref is all_normed_ref else 0
            copies += [
                pltpu.make_async_copy(rows_ref.at[there, block], xt.at[slot, b], tile_sems.at[slot, b]),
                pltpu.make_async_copy(all_grad_ref.at[piece, block], gt.at[slot, b], tile_sems.at[slot, 2 + b]),
                pltpu.make_async_copy(mark_ref.at[piece, block], mt.at[slot, b], tile_sems.at[slot, 4 + b]),
            ]
        return copies

    for copy in loads(0, plane_ref):
        copy.start()
    last = 4 * nz - 1

    def tile(i, _):
        j, t, slot = i // 4, i % 4, i % 2
        more = j < nz - 1

        @pl.when((t == 0) & more)
        def _():
            gather.second(j + 1)

        @pl.when(i == 1)
        def _():
            gather.along_z(3)

        @pl.when((t == 2) & more)
        def _():
            gather.third(j + 1)

        @pl.when((t == 2) & (j < nz - 2))
        def _():
            gather.first(j + 2)

        @pl.when((t == 3) & more)
        def _():
            gather.fourth(j + 1)

        @pl.when((t == 0) & (j > 0))
        def _():
            for k in range(4):
                reduce.core(j - 1, k, px.at[k]).wait_send()
                outs.core(j - 1, k, po.at[k]).wait_send()

        for copy in loads(i):
            copy.wait()

        @pl.when(i < 3)
        def _():
            for copy in loads(i + 1, plane_ref):
                copy.start()

        @pl.when((i >= 3) & (i < last))
        def _():
            for copy in loads(i + 1):
                copy.start()

        x = xt[slot].reshape(2 * rows, width)
        g = gt[slot].reshape(2 * rows, width)
        out, gx, grad_pre, acts = ffn_rows(
            x, g, mt[slot].reshape(2 * rows, HD), own_ref[...], up_ref, upt_ref, down_ref, downt_ref, hidden, shared
        )
        at = pl.ds(2 * t, 2)
        po[at] = out.reshape(2, rows, width)
        px[at] = gx.reshape(2, rows, width + HD)
        gup_ref[...] += dot_tn(x, grad_pre)
        gdown_ref[...] += dot_tn(acts, g)

        @pl.when(t == 1)
        def _():
            for k in range(4):
                reduce.core(j, k, px.at[k]).start()
            for k in range(4):
                outs.core(j, k, po.at[k]).start()

        @pl.when((t == 1) & (j > 0))
        def _():
            reduce.far(j - 1)

        @pl.when((t == 2) & (j > 0))
        def _():
            reduce.along_z(j - 1)

        @pl.when(t == 3)
        def _():
            for k in range(4):
                reduce.core(j, k, None).wait_recv()
                reduce.by_core[j, k] = reduce.by_core[j, k] + px[4 + k]
            reduce.send_near(j)
            for k in range(4):
                outs.core(j, k, None).wait_recv()
                out_ref[j, k] = out_ref[j, k] + po[4 + k]

        return 0

    lax.fori_loop(0, 4 * nz, tile, 0)
    up_ref[:, : 2 * pair] = jnp.concatenate([gup_ref[:, :pair], gup_ref[:, half : half + pair]], axis=1).astype(BF16)
    up_rows = width // nz

    def ups(j):
        there = lax.rem(z + j, nz)
        src = up_ref.at[pl.ds(pl.multiple_of(there * up_rows, up_rows), up_rows), pl.ds(0, 2 * pair)]
        if j == 0:
            return pltpu.make_async_copy(src, pieces_ref.at[z], own_sems.at[1])
        return send(src, pieces_ref.at[z], (es, er), j, (there, f))

    for j in (1, nz - 1):
        ups(j).start()
    own_down = pltpu.make_async_copy(gdown_ref.at[pl.ds(0, pair)], gedown_ref, own_sems.at[2])
    own_down.start()
    ups(0).start()
    reduce.far(nz - 1)
    gtail = jnp.concatenate([gup_ref[:, half - TAIL : half], gup_ref[:, 2 * half - TAIL :]], axis=1)
    gsdown_ref[...] = gdown_ref[half - TAIL : half - TAIL + shared, :]
    reduce.along_z(nz - 1)
    for j in range(2, nz - 1):
        ups(j).start()
    grad_mixed, small = route_grads(
        reduce.total(), og_ref[...], mixed_ref[...], normed_ref[...], router_ref[...], own_mark_ref[...], gain_ref[...]
    )
    gm_ref[...] = grad_mixed
    low[...] = grad_mixed.astype(BF16)
    own = pltpu.make_async_copy(low, seq_ref.at[0, f], own_sems.at[3])
    own.start()
    turned = Gather(seq_ref, (gs, gr), 1, z, f)
    own.wait()
    turned.first(0, own=True)
    small_ref[...] = small + gtail
    turned.second(0)
    turned.third(0)
    turned.fourth(0)
    for k in range(4):
        reduce.core(nz - 1, k, px.at[k]).wait_send()
        outs.core(nz - 1, k, po.at[k]).wait_send()
    own_down.wait()
    for j in range(nz):
        ups(j).wait()
    for j in range(4, nz + 1):
        gather.along_z(j)
    gather.end(1)
    reduce.end()
    turned.end()


def experts_turn(
    normed, plane, all_grad, marks, own, eup, tail, edown, sdown, og, mixed, router, own_marks, gain, nz, nf
):
    rows, width = mixed.shape
    pair, shared = edown.shape[0], sdown.shape[0]
    half = up_to(pair + TAIL, HD)
    wide = width + HD
    return pl.pallas_call(
        functools.partial(experts_kernel, nz=nz, hidden=pair // 2, shared=shared),
        out_shape=(
            jax.ShapeDtypeStruct((nz, 4, rows, width), BF16),
            jax.ShapeDtypeStruct((1, 8, rows, width), BF16),
            jax.ShapeDtypeStruct((rows, width), F32),
            jax.ShapeDtypeStruct((width, HD), F32),
            jax.ShapeDtypeStruct((nz, width // nz, 2 * pair), BF16),
            jax.ShapeDtypeStruct((pair, width), F32),
            jax.ShapeDtypeStruct((shared, width), F32),
            jax.ShapeDtypeStruct((nz, 8, rows, width), BF16),
        ),
        in_specs=[VMEM, ANY, ANY, ANY] + [VMEM] * 10,
        out_specs=(VMEM, ANY, VMEM, VMEM, ANY, ANY, VMEM, ANY),
        scratch_shapes=[
            pltpu.VMEM((width, 2 * half), BF16),
            pltpu.VMEM((2 * half, width), BF16),
            pltpu.VMEM((half, width), BF16),
            pltpu.VMEM((width, half), BF16),
            pltpu.VMEM((width, 2 * half), F32),
            pltpu.VMEM((half, width), F32),
            pltpu.VMEM((2, 2, rows, width), BF16),
            pltpu.VMEM((2, 2, rows, width), BF16),
            pltpu.VMEM((2, 2, rows, HD), BF16),
            pltpu.VMEM((8, rows, wide), BF16),
            pltpu.VMEM((8, rows, width), BF16),
            pltpu.VMEM((rows, width), BF16),
            *Reduce.scratch(nz, rows, wide),
            pltpu.SemaphoreType.DMA((2, 6)),
            *pair_of(Reduce.copies(nz)),
            *pair_of(Reduce.copies(nz)),
            *pair_of(Gather.copies(nz)),
            *pair_of(Gather.copies(1)),
            *pair_of(nz),
            pltpu.SemaphoreType.DMA((4,)),
        ],
        compiler_params=pltpu.CompilerParams(
            collective_id=3, has_side_effects=True, vmem_limit_bytes=60 * 2**20
        ),
        name="experts_turn",
    )(
        normed, plane, all_grad, marks.reshape(nz, 8, rows, HD), own, eup, tail, edown, sdown, og, mixed, router, own_marks, gain
    )[:7]


def back_kernel(
    gm_ref, wo_ref, w_ref, normed_ref, qkv_ref, attn_ref, lse_ref, cos_ref, sin_ref, segq_ref, segk_ref,
    out_ref, small_ref, tok_ref, mixed_ref, own_gm_ref, gain_ref,
    block_ref, gtok_ref, gwqkv_ref, gwout_ref, all_small_ref,
    gkv_ref, gqkv_ref, wt_ref, part_ref, gw_ref, gwo_ref, gws, gwos, smalls, *refs, nz, nf, heads, real,
):
    bufs, refs = refs[:7], refs[7:]
    rs, rr, os_, or_, all_s, all_r, wo_s, wo_r, own_sems = refs
    z, f = place()
    me, count = z * nf + f, nz * nf
    dense = gw_ref.shape[2]
    rows, width = tok_ref.shape
    length = gm_ref.shape[0]
    greet_all(nz, nf)
    outs = Reduce([out_ref, *bufs[4:]], (os_, or_), nz, z, f)
    order = list(range(1, nz)) + [0]
    outs.send_near(order[0])

    def two(m):
        return first_head(m + 1) - first_head(m) == 2

    def copies(d, k):
        device = (d // nf, d % nf)
        src, dst = ((gw_ref.at[0, d], gws.at[0, me]), (gw_ref.at[1, d], gws.at[1, me]), (small_ref.at[d], smalls.at[me]))[k]
        return pltpu.make_async_remote_copy(
            src, dst, all_s.at[k, d], all_r.at[k, me], device_id=device, device_id_type=MESH
        )

    def wanted(m, block):
        low, high = out_blocks(m, dense)
        return (low <= block) & (block <= high)

    def owner_of(block):
        return head_owner(block * dense // HD)

    low, _ = out_blocks(f, dense)

    def out_copy(d):
        k = 2 * z + f - owner_of(d)
        return pltpu.make_async_remote_copy(
            gwo_ref.at[d - low], gwos.at[k], wo_s.at[d - low], wo_r.at[k],
            device_id=(d // nf, d % nf), device_id_type=MESH,
        )

    spare = gwo_ref.shape[0] * dense
    wide = up_to(spare, HD)
    shift = first_head(f) * HD - low * dense
    moved = jnp.concatenate([attn_ref[...].astype(F32), jnp.zeros((length, wide - SLOTS * HD), F32)], axis=1)
    moved = pltpu.roll(moved, shift, 1).astype(BF16)
    gwo_ref[...] = dot_tn(moved, gm_ref[...])[:spare].reshape(gwo_ref.shape).astype(BF16)

    def start_small(i, _):
        d = (me + i) % count
        copies(d, 2).start()

        @pl.when(wanted(f, d))
        def _():
            out_copy(d).start()

        return 0

    lax.fori_loop(1, count, start_small, 0)
    own_slot = 2 * z + f - owner_of(me)
    own_out = pltpu.make_async_copy(gwo_ref.at[me - low], gwos.at[own_slot], own_sems.at[0])
    own_small = pltpu.make_async_copy(small_ref.at[me], smalls.at[me], own_sems.at[1])
    own_small.start()

    @pl.when(wanted(f, me))
    def _():
        own_out.start()

    gkv_ref[...] = jnp.zeros_like(gkv_ref)
    block = 256
    for i in range(length // block):
        attn_back_block(
            i, block, gm_ref, wo_ref, qkv_ref, attn_ref, lse_ref, cos_ref, sin_ref, segq_ref, segk_ref, gkv_ref, gqkv_ref
        )
        if i + 1 < nz:
            outs.send_near(order[i + 1])
        if i < nz:
            outs.far(order[i])
        if 0 < i <= nz:
            outs.along_z(order[i - 1])
    attn_back_keys(w_ref, cos_ref, sin_ref, gkv_ref, gqkv_ref, wt_ref)
    step = 3 * HD
    reduce = Reduce(bufs[:4], (rs, rr), 1, z, f)
    for i in range(length // block):
        mine = slice(i * block, (i + 1) * block)
        at = i * block // rows
        part_ref[at : at + block // rows] = (
            dot(gqkv_ref[mine, :], wt_ref[...]).astype(BF16).reshape(block // rows, rows, width)
        )
    for i in range(4):
        reduce.core(0, i, part_ref.at[flip(f, 1 | 2 * i)]).start()

    own_gw = [pltpu.make_async_copy(gw_ref.at[s, me], gws.at[s, me], own_sems.at[2 + s]) for s in range(SLOTS)]

    def weights(s):
        value = dot_tn(normed_ref[...], gqkv_ref[:, s * step : (s + 1) * step])
        gw_ref[s] = value.reshape(count, dense, step).astype(BF16)

        def start(i, _):
            copies((me + i) % count, s).start()
            return 0

        lax.fori_loop(1, count, start, 0)
        own_gw[s].start()

    weights(0)
    for i in range(4):
        reduce.core(0, i, None).wait_recv()
        reduce.by_core[0, i] = reduce.by_core[0, i] + part_ref[flip(f, 2 * i)]
    reduce.send_near(0)

    @pl.when(two(f))
    def _():
        weights(1)

    for k in range(length // block, nz):
        outs.far(order[k])
    for k in range(length // block - 1, nz):
        outs.along_z(order[k])
    reduce.far(0)
    reduce.along_z(0)
    x = tok_ref[...].astype(F32)
    scale = rms_scale(x)
    gtok_ref[...] = (
        own_gm_ref[...] + norm_back(reduce.by_far[0].astype(F32), x * scale, scale, gain_ref[...])
    ).astype(BF16)
    block_ref[...] = (mixed_ref[...] + outs.total()).astype(BF16)

    owner = owner_of(me)
    next_owner = head_owner((me * dense + dense - 1) // HD)
    for k in range(2 * nz):
        there = (k // 2 != z) | (f != owner + k % 2)
        if k % 2:
            there = there & (next_owner != owner)

        @pl.when(there)
        def _():
            pltpu.make_async_remote_copy(
                gwo_ref.at[0], gwos.at[k], wo_s.at[0], wo_r.at[k], device_id=(z, flip(f, 1)), device_id_type=MESH
            ).wait_recv()

    @pl.when(wanted(f, me))
    def _():
        own_out.wait()

    gwout_ref[...] = sum(gwos[2 * t].astype(F32) for t in range(nz))

    @pl.when(next_owner != owner)
    def _():
        gwout_ref[...] += sum(gwos[2 * t + 1].astype(F32) for t in range(nz))

    def came(d, k):
        dst = (gws.at[0, d], gws.at[1, d], smalls.at[d])[k]
        return pltpu.make_async_remote_copy(
            dst, dst, all_s.at[k, d], all_r.at[k, d], device_id=(d // nf, d % nf), device_id_type=MESH
        )

    def finish(i, _):
        d = (me + i) % count
        came(d, 0).wait_recv()

        @pl.when(two(d % nf))
        def _():
            came(d, 1).wait_recv()

        came(d, 2).wait_recv()
        copies(d, 0).wait_send()

        @pl.when(two(f))
        def _():
            copies(d, 1).wait_send()

        copies(d, 2).wait_send()

        @pl.when(wanted(f, d))
        def _():
            out_copy(d).wait_send()

        return 0

    lax.fori_loop(1, count, finish, 0)
    own_small.wait()
    own_gw[0].wait()

    @pl.when(two(f))
    def _():
        own_gw[1].wait()

    for m in range(8):
        for s in range(SLOTS):
            if real[m * SLOTS + s]:
                h = heads[m * SLOTS + s]
                both = sum(gws[s, t * nf + m].astype(F32) for t in range(nz))
                for c in range(3):
                    gwqkv_ref[:, c * width + h * HD : c * width + (h + 1) * HD] = both[:, c * HD : (c + 1) * HD]
    all_small_ref[...] = smalls[...]
    for i in range(4):
        reduce.core(0, i, part_ref.at[0]).wait_send()
    reduce.end()
    outs.end()


def back(
    gm, wo, w, normed, qkv, attn, lse, cosine, sine, segq, segk, out_part, small, tok, mixed, own_gm, gain, nz, nf
):
    rows, width = tok.shape
    length, count = gm.shape[0], nz * nf
    dense = width // count
    heads, real = head_table(8)
    return pl.pallas_call(
        functools.partial(back_kernel, nz=nz, nf=nf, heads=heads, real=real),
        out_shape=(
            jax.ShapeDtypeStruct((rows, width), BF16),
            jax.ShapeDtypeStruct((rows, width), BF16),
            jax.ShapeDtypeStruct((dense, 3 * width), F32),
            jax.ShapeDtypeStruct((dense, width), F32),
            jax.ShapeDtypeStruct((count, dense, HD), BF16),
        ),
        in_specs=[VMEM] * 17,
        out_specs=(VMEM,) * 5,
        scratch_shapes=[
            pltpu.VMEM((length, 2 * SLOTS * HD), F32),
            pltpu.VMEM((length, 3 * SLOTS * HD), BF16),
            pltpu.VMEM((3 * SLOTS * HD, width), BF16),
            pltpu.VMEM((8, rows, width), BF16),
            pltpu.VMEM((SLOTS, count, dense, 3 * HD), BF16),
            pltpu.VMEM((8, dense, width), BF16),
            pltpu.VMEM((SLOTS, count, dense, 3 * HD), BF16),
            pltpu.VMEM((2 * nz, dense, width), BF16),
            pltpu.VMEM((count, dense, HD), BF16),
            *Reduce.scratch(1, rows, width),
            *Reduce.scratch(nz, rows, width)[1:],
            *pair_of(Reduce.copies(1)),
            *pair_of(Reduce.copies(nz)),
            pltpu.SemaphoreType.DMA((3, count)),
            pltpu.SemaphoreType.DMA((3, count)),
            pltpu.SemaphoreType.DMA((8,)),
            pltpu.SemaphoreType.DMA((2 * nz,)),
            pltpu.SemaphoreType.DMA((4,)),
        ],
        compiler_params=pltpu.CompilerParams(
            collective_id=4, has_side_effects=True, vmem_limit_bytes=60 * 2**20
        ),
        name="back",
    )(
        gm, wo, w, normed, qkv, attn, lse, cosine, sine, segq, segk, out_part,
        small.astype(BF16).reshape(count, dense, HD), tok, mixed, own_gm, gain,
    )


def unpack_kernel(
    pieces_ref, small_ref, wqkv_ref, gwqkv_ref, gain_ref,
    geup_ref, gsup_ref, grouter_ref, ggain_ref,
    *, shared, experts,
):
    nz = pieces_ref.shape[0]
    hidden = pieces_ref.shape[2] // 4
    for t in range(nz):
        for g in range(2):
            for e in range(2):
                at = (2 * g + e) * hidden
                to = (g * nz + t) * hidden
                geup_ref[e, :, to : to + hidden] = pieces_ref[t, :, at : at + hidden].astype(F32)
    count = small_ref.shape[0]
    total = small_ref[0].astype(F32)
    for d in range(count):
        if d:
            total = total + small_ref[d].astype(F32)
        for g in range(2):
            to = (g * count + d) * shared
            gsup_ref[:, to : to + shared] = small_ref[d, :, g * TAIL : g * TAIL + shared].astype(F32)
    grouter_ref[...] = total[:, shared : shared + experts]
    one = jnp.sum(wqkv_ref[...].astype(F32) * gwqkv_ref[...], axis=-1, keepdims=True) / gain_ref[:, :1].astype(F32)
    ggain_ref[...] = jnp.concatenate([one, total[:, HD - 1 :]], axis=1)


def unpack(pieces, small, wqkv, gwqkv, gains, shared, experts):
    nz, up_rows, packed = pieces.shape
    count, dense, _ = small.shape
    return pl.pallas_call(
        functools.partial(unpack_kernel, shared=shared, experts=experts),
        out_shape=(
            jax.ShapeDtypeStruct((2, up_rows, nz * packed // 2), F32),
            jax.ShapeDtypeStruct((dense, 2 * count * shared), F32),
            jax.ShapeDtypeStruct((dense, experts), F32),
            jax.ShapeDtypeStruct((dense, 2), F32),
        ),
        in_specs=[VMEM] * 5,
        out_specs=(VMEM,) * 4,
        compiler_params=pltpu.CompilerParams(vmem_limit_bytes=32 * 2**20),
        name="unpack",
    )(pieces, small, wqkv, gwqkv, gains)


def tables():
    pos = np.arange(SEQ, dtype=np.float32)
    freqs = np.float32(ROPE) ** (-np.arange(HD // 2, dtype=np.float32) * np.float32(2.0 / HD))
    angles = (pos[:, None] * freqs[None, :]).astype(np.float32)
    cosine = np.concatenate([np.cos(angles)] * 2, axis=1).astype(np.float32)
    sine = np.concatenate([-np.sin(angles), np.sin(angles)], axis=1).astype(np.float32)
    return jnp.asarray(cosine), jnp.asarray(sine)


def local_near(
    mesh, tokens, out_grad, segment_ids, expert_ids, attn_gain, ffn_gain, w_qkv, w_out,
    w_router, w_shared_up, w_shared_down, w_expert_up, w_expert_down,
):
    nz, nf = mesh.shape["dp"], mesh.shape["fsdp"]
    rows, width = tokens.shape
    experts = w_router.shape[1]
    hidden, shared = w_expert_down.shape[1], w_shared_down.shape[0]
    f = lax.axis_index("fsdp")
    gains = jnp.stack([attn_gain, ffn_gain], axis=1)
    ids = jnp.concatenate([expert_ids.T, segment_ids[None]], axis=0)
    cosine, sine = tables()
    (
        w, wo, tail, all_gains, marks, own_marks, segq, segk, normed_one, qkv, attn, lse, mixed, normed, plane, all_grad,
        pieces,
    ) = front(
        tokens, w_qkv, w_out, w_router, w_shared_up, gains, ids, cosine, sine, out_grad, w_expert_up, nz, nf, shared
    )
    tail = tail.reshape(width, 2 * TAIL)
    gain_one, gain_two = all_gains[:1], all_gains[1:]
    router = jnp.pad(tail[:, shared : shared + experts], ((0, 0), (TAIL + shared, TAIL - shared - experts)))
    lane = jnp.arange(HD, dtype=jnp.int32) - TAIL - shared
    own = (lane[None, :] == (2 * f + jnp.arange(2, dtype=jnp.int32))[:, None]).astype(F32)
    out_part, seq_gm, grad_mixed, small, gpieces, gedown, gsdown = experts_turn(
        normed, plane, all_grad, marks, own, pieces.reshape(width, 4 * hidden), tail,
        w_expert_down.reshape(2 * hidden, width), w_shared_down, out_grad, mixed, router, own_marks, gain_two, nz, nf,
    )
    block_out, tokens_grad, grad_wqkv, grad_wout, smalls = back(
        seq_gm.reshape(SEQ, width), wo, w, normed_one, qkv, attn, lse, cosine, sine, segq, segk, out_part, small,
        tokens, mixed, grad_mixed, gain_one, nz, nf,
    )
    grad_eup, grad_sup, grad_router, grad_gains = unpack(gpieces, smalls, w_qkv, grad_wqkv, gains, shared, experts)
    return (
        block_out, tokens_grad, grad_gains[:, 0], grad_gains[:, 1], grad_wqkv, grad_wout, grad_router, grad_sup,
        gsdown, grad_eup, gedown.reshape(2, hidden, width),
    )


def local_far(
    mesh, tokens, out_grad, segment_ids, expert_ids, attn_gain, ffn_gain, w_qkv, w_out,
    w_router, w_shared_up, w_shared_down, w_expert_up, w_expert_down,
):
    nz, nf = mesh.shape["dp"], mesh.shape["fsdp"]
    nd = nz * nf
    rows, width = tokens.shape
    group = SEQ // rows
    experts = w_router.shape[1]
    dense = w_qkv.shape[0]
    hidden, shared = w_expert_down.shape[1], w_shared_down.shape[0]
    up_rows = w_expert_up.shape[1]
    both = ("dp", "fsdp")
    groups = None if nf == group else [[a + i for i in range(group)] for a in range(0, nf, group)]
    f = lax.axis_index("fsdp")
    member = lax.rem(f, group)
    heads, real = head_table(group)

    by_head = w_qkv.reshape(dense, 3, HEADS, HD)
    empty = jnp.zeros((dense, 3, HD), BF16)
    cols = jnp.stack([by_head[:, :, h] if r else empty for h, r in zip(heads, real)], axis=0)
    cols = cols.reshape(group, SLOTS, dense, 3 * HD)
    cols = jnp.tile(cols, (nf // group, 1, 1, 1))
    cols = lax.all_to_all(cols, "fsdp", 0, 0, tiled=True)
    w = lax.all_gather(cols, "dp", axis=0, tiled=True).transpose(1, 0, 2, 3).reshape(SLOTS, width, 3 * HD)
    full_out = lax.all_gather(w_out, both, axis=0, tiled=True)
    first = HEADS * member // group
    own_real = (first + jnp.arange(SLOTS) < HEADS * (member + 1) // group).astype(BF16)
    padded = jnp.pad(full_out, ((0, (SLOTS - 1) * HD), (0, 0)))
    wo = lax.dynamic_slice(padded, (first * HD, 0), (SLOTS * HD, width))
    wo = wo * jnp.repeat(own_real, HD)[:, None]
    gains = lax.all_gather(jnp.stack([attn_gain, ffn_gain], axis=1).astype(F32), both, axis=0, tiled=True)
    gain_one, gain_two = gains[:, 0], gains[:, 1]
    router = lax.all_gather(w_router, both, axis=0, tiled=True)
    sup = w_shared_up.reshape(dense, 2, nd, shared).transpose(2, 0, 1, 3).reshape(nd, dense, 2 * shared)
    sup = lax.all_to_all(sup, both, 0, 0, tiled=True).reshape(width, 2, shared)
    eup = w_expert_up.reshape(2, up_rows, 2, nz, hidden).transpose(3, 1, 2, 0, 4)
    eup = lax.all_to_all(eup, "dp", 0, 0, tiled=True).reshape(width, 4 * hidden)
    rest = jnp.zeros((width, TAIL - shared), BF16)
    tail = jnp.concatenate([sup[:, 0], router, rest[:, experts:], sup[:, 1], rest], axis=1)
    chosen = jnp.any(expert_ids[:, :, None] == jnp.arange(experts, dtype=jnp.int32), axis=1)
    at = TAIL + shared
    marks = jnp.pad(chosen.astype(BF16), ((0, 0), (at, HD - experts - at)))
    marks = lax.all_gather(marks, both, axis=0, tiled=True)
    lane = jnp.arange(HD, dtype=jnp.int32)
    own = (lane[None, :] == (at + 2 * f + jnp.arange(2, dtype=jnp.int32))[:, None]).astype(F32)
    cosine, sine = tables()
    seg = lax.all_gather(segment_ids, "fsdp", axis=0, tiled=True, axis_index_groups=groups)
    segq = jnp.broadcast_to(seg[:, None], (SEQ, HD))
    segk = jnp.broadcast_to(seg[None, :], (8, SEQ))

    seq_tokens = lax.all_gather(tokens, "fsdp", axis=0, tiled=True, axis_index_groups=groups)
    part, normed_one, qkv, attn, lse = attn_forward(
        seq_tokens, gain_one[None, :], w, wo, cosine, sine, segq, segk
    )
    projected = lax.psum_scatter(part, "fsdp", scatter_dimension=0, tiled=True, axis_index_groups=groups)
    inputs = tokens.astype(F32)
    mixed = inputs + projected.astype(F32)
    scale_two = rms_scale(mixed)
    normal_two = mixed * scale_two
    normed_two = (normal_two * gain_two).astype(BF16)
    all_normed = lax.all_gather(normed_two, both, axis=0, tiled=True)
    all_grad = lax.all_gather(out_grad, both, axis=0, tiled=True)
    out_part, gx_part, geup, gtail, gedown, gsdown = ffn(
        all_normed, all_grad, marks, own, eup, tail, w_expert_down.reshape(2 * hidden, width), w_shared_down
    )
    gx = lax.psum_scatter(gx_part, both, scatter_dimension=0, tiled=True).astype(F32)
    ffn_out = lax.psum_scatter(out_part, both, scatter_dimension=0, tiled=True).astype(F32)
    block_out = (mixed + ffn_out).astype(BF16)

    logits = jnp.where(chosen, dot(normed_two, router), NEG)
    probs = jax.nn.softmax(logits, axis=-1)
    grad_gates = gx[:, width + at : width + at + experts]
    grad_logits = (
        probs * (grad_gates - jnp.sum(probs * grad_gates, axis=-1, keepdims=True))
    ).astype(BF16)
    grad_router = dot_tn(normed_two, grad_logits)
    grad_normed = gx[:, :width] + dot_nt(grad_logits, router)
    grad_gain_two = jnp.sum(grad_normed * normal_two, axis=0)
    grad_mixed = out_grad.astype(F32) + norm_back(grad_normed, normal_two, scale_two, gain_two)

    seq_gm = lax.all_gather(grad_mixed.astype(BF16), "fsdp", axis=0, tiled=True, axis_index_groups=groups)
    part_back, gw, gwo = attn_backward(
        seq_gm, wo, w, normed_one, qkv, attn, lse, cosine, sine, segq, segk
    )
    grad_normed_one = lax.psum_scatter(
        part_back, "fsdp", scatter_dimension=0, tiled=True, axis_index_groups=groups
    ).astype(F32)
    scale_one = rms_scale(inputs)
    normal_one = inputs * scale_one
    grad_gain_one = jnp.sum(grad_normed_one * normal_one, axis=0)
    tokens_grad = (grad_mixed + norm_back(grad_normed_one, normal_one, scale_one, gain_one)).astype(BF16)

    gw = lax.psum_scatter(gw, "dp", scatter_dimension=1, tiled=True)
    gw = lax.all_to_all(gw.reshape(SLOTS, nf, dense, 3 * HD), "fsdp", 1, 1, tiled=True).astype(F32)
    gw = jnp.sum(gw.reshape(SLOTS, nf // group, group, dense, 3, HD), axis=1)
    picked = [gw[i % SLOTS, i // SLOTS] for i in range(group * SLOTS) if real[i]]
    grad_wqkv = jnp.stack(picked, axis=2).reshape(dense, 3 * width)
    gwo = gwo * jnp.repeat(own_real, HD)[:, None]
    all_gwo = jnp.zeros(((HEADS + SLOTS - 1) * HD, width), BF16)
    all_gwo = lax.dynamic_update_slice(all_gwo, gwo, (first * HD, 0))[: HEADS * HD]
    grad_wout = lax.psum_scatter(all_gwo, both, scatter_dimension=0, tiled=True).astype(F32)
    small = jnp.concatenate([grad_router, grad_gain_one[:, None], grad_gain_two[:, None]], axis=1)
    small = lax.psum_scatter(small, both, scatter_dimension=0, tiled=True)
    gsup = jnp.stack([gtail[:, :shared], gtail[:, TAIL : TAIL + shared]], axis=1)
    gsup = lax.all_to_all(gsup.reshape(nd, dense, 2 * shared).astype(BF16), both, 0, 0, tiled=True)
    grad_sup = gsup.reshape(nd, dense, 2, shared).transpose(1, 2, 0, 3).reshape(dense, 2 * nd * shared).astype(F32)
    geup = lax.all_to_all(geup.reshape(nz, up_rows, 2, 2, hidden), "dp", 0, 0, tiled=True)
    grad_eup = geup.transpose(3, 1, 2, 0, 4).reshape(2, up_rows, 2 * nz * hidden).astype(F32)
    return (
        block_out, tokens_grad, small[:, experts], small[:, experts + 1], grad_wqkv, grad_wout,
        small[:, :experts], grad_sup, gsdown, grad_eup, gedown.reshape(2, hidden, width),
    )


def solution(mesh):
    one, two = P(("dp", "fsdp")), P(("dp", "fsdp"), None)
    three = P("fsdp", "dp", None)

    def local(tokens, *rest):
        near = mesh.shape["fsdp"] == 8 == SEQ // tokens.shape[0] and mesh.shape["dp"] <= 4
        return (local_near if near else local_far)(mesh, tokens, *rest)

    return jax.shard_map(
        local,
        mesh=mesh,
        in_specs=(two, two, one, two, one, one, two, two, two, two, two, three, three),
        out_specs=(two, two, one, one, two, two, two, two, two, three, three),
        check_vma=False,
    )
```

time: 644 us -> 495 us (0.77); the launches traced: 634 us -> 494 us
  Pallas kernels: 593 us -> 474 us
  other arithmetic: 15.5 us -> 4.47 us
  local copies, waits for them, and re-layouts: 24.7 us -> 14.9 us
    pallas_call x7 -> x3, Pallas kernels: 590 us -> 471 us  [the longest x1 171 us: experts_turn(): pl.pallas_call(functools.partial(experts_kernel, nz=nz, hidden=pair // 2,...]
    unnamed x57 -> x28, local copies, waits for them, and re-layouts: 20 us -> 10.1 us
where the time goes in v2:
time: 495 us; the launch traced here: 494 us
  Pallas kernels  474 us (96%)
  local copies, waits for them, and re-layouts  14.9 us (3%)
    pallas_call x1, Pallas kernels, experts_turn(): pl.pallas_call(functools.partial(experts_kernel, nz=nz, hidden=pair // 2,...  171 us
    pallas_call x1, Pallas kernels, front(): pl.pallas_call(functools.partial(front_kernel, nz=nz, nf=nf, hidden=hidde...  167 us
    pallas_call x1, Pallas kernels, back(): pl.pallas_call(functools.partial(back_kernel, nz=nz, nf=nf, heads=heads,...  133 us
    unnamed x28, local copies, waits for them, and re-layouts  10.1 us

profile of v2, /device:TPU:11, one launch (start us, length us, event | category | flops | bytes accessed | tf_op | source)
XLA Modules:
  0.0 494.2 jit_solution(4671738153893007717)
XLA Ops:
  0.7 0.7 pad_maximum_fusion
  1.3 0.6 compare_convert_fusion.own_ref
  2.0 1.3 pad_add_fusion.ids_ref
  3.3 0.7 copy.35.gains_ref.gain_ref
  4.0 1.4 copy.34.router_ref
  5.3 167.0 %front.1 = (bf16[2,1280,384]{2,1,0:T(8,128)(2,1)}, bf16[256,1280]{1,0:T(8,128)(2,1)}, bf16[32,40,128]{2,1,0:T(8,128)(2,1)}, f32[2,1280]{1,0:T(2,128)}, bf16[32,1...) custom-call(bf16[128,1280]{1,0:T(8,128)(2,1)} %tok_ref.3, ...), custom_call_target="tpu_custom_call" | custom-call | tf_op jit(solution)/shard_map/front/pallas_call | solution.py:888
  172.3 1.4 fusion
  173.7 1.1 slice.20
  174.9 0.9 pad.4.router_ref
  175.7 170.9 %experts_turn.1 = (bf16[4,4,128,1280]{3,2,1,0:T(8,128)(2,1)}, bf16[1,8,128,1280]{3,2,1,0:T(8,128)(2,1)}, f32[128,1280]{1,0:T(8,128)}, f32[1280,128]{1,0:T(8,128)...) custom-call(bf16[128,1280]{1,0:T(8,128)(2,1)} %get-tuple-element.44., ...), custom_call_target="tpu_custom_call" | custom-call | tf_op jit(solution)/shard_map/experts_turn/pallas_call | solution.py:1143
  346.6 1.8 convert_element_type.9
  348.5 0.0 copy-start.2
  348.5 0.0 copy-start.3
  348.5 0.0 copy-start.5
  348.5 133.2 %back.1 = (bf16[128,1280]{1,0:T(8,128)(2,1)}, bf16[128,1280]{1,0:T(8,128)(2,1)}, f32[40,3840]{1,0:T(8,128)}, f32[40,1280]{1,0:T(8,128)}, bf16[32,40,128]{2,1,0:T(8,128)(2,1)}) custom-call(bf16[1024,1280]{1,0:T(8,128)(2,1)} %bitcast.11, bf16[256,1280]{1,0:T(8,128)(2,1)} %get-tuple-element.54.wo_ref, bf16[2,1280,384]{2,1,0:T(8,128)(2,1)} %get-tuple-element.55.w_ref, ...), custom_call_target="tpu_custom_call" | custom-call | tf_op jit(solution)/shard_map/back/pallas_call | solution.py:1400
  481.7 0.0 copy-done.2
  481.7 0.0 copy-done.3
  481.7 0.0 copy-done.5
  481.7 0.0 copy-start
  481.7 1.1 copy-done
  482.8 0.0 copy-start.4
  482.8 1.0 copy-done.4
  483.8 0.0 copy-start.7
  483.8 0.0 copy-start.1
  483.8 0.0 copy-start.8
  483.8 3.0 unpack.1
  486.8 0.0 copy-start.6
  486.8 0.7 slice_reduce_fusion
  487.5 0.7 copy.37
  488.2 0.0 copy-start.9
  488.2 1.8 copy.44
  489.9 0.0 copy-done.7
  489.9 0.7 copy.45
  490.6 0.0 copy-done.1
  490.6 0.8 copy.46
  491.5 0.0 copy-done.8
  491.5 0.7 copy.47
  492.2 0.0 copy-done.9
  492.2 0.7 copy.48
  492.8 0.0 copy-done.6
  492.8 1.4 copy.49
  (2 shorter events, 0.0 us)
Async XLA Ops:
  348.5 133.2 %copy-start.2 = (bf16[4,320,896]{2,1,0:T(8,128)(2,1)S(1)}, bf16[4,320,896]{2,1,0:T(8,128)(2,1)}, u32[]{:S(2)}) copy-start(bf16[4,320,896]{2,1,0:T(8,128)(2,1)} %get-tuple-element.67.pieces_ref) | copy-start | bytes 6881284
  348.5 133.2 %copy-start.3 = (bf16[40,3840]{1,0:T(8,128)(2,1)S(1)}, bf16[40,3840]{1,0:T(8,128)(2,1)}, u32[]{:S(2)}) copy-start(bf16[40,3840]{1,0:T(8,128)(2,1)} %wqkv_ref.3) | copy-start | bytes 921604
  348.5 133.2 %copy-start.5 = (bf16[40,2]{1,0:T(8,128)(2,1)S(1)}, bf16[40,2]{1,0:T(8,128)(2,1)}, u32[]{:S(2)}) copy-start(bf16[40,2]{1,0:T(8,128)(2,1)} %copy.35.gains_ref.gain_ref) | copy-start | bytes 484
  481.7 1.1 copy-start
  482.8 1.0 copy-start.4
  483.8 6.1 %copy-start.7 = (bf16[128,1280]{1,0:T(8,128)(2,1)S(1)}, bf16[128,1280]{1,0:T(8,128)(2,1)}, u32[]{:S(2)}) copy-start(bf16[128,1280]{1,0:T(8,128)(2,1)} %get-tuple-element.126) | copy-start | bytes 983044
  483.8 6.9 %copy-start.1 = (f32[40,3840]{1,0:T(8,128)S(1)}, f32[40,3840]{1,0:T(8,128)}, u32[]{:S(2)}) copy-start(f32[40,3840]{1,0:T(8,128)} %get-tuple-element.129.gwqkv_ref) | copy-start | bytes 1843204
  483.8 7.7 %copy-start.8 = (f32[40,1280]{1,0:T(8,128)S(1)}, f32[40,1280]{1,0:T(8,128)}, u32[]{:S(2)}) copy-start(f32[40,1280]{1,0:T(8,128)} %get-tuple-element.130) | copy-start | bytes 614404
  486.8 6.0 %copy-start.6 = (f32[448,1280]{1,0:T(8,128)S(1)}, f32[448,1280]{1,0:T(8,128)}, u32[]{:S(2)}) copy-start(f32[448,1280]{1,0:T(8,128)} %get-tuple-element.76) | copy-start | bytes 6881284
  488.2 4.0 copy-start.9

commit v3 on v2

--- a/solution.py
+++ b/solution.py
@@ -145,7 +145,7 @@
 
 
 def attn_back_block(
-    i, block, gm_ref, wo_ref, qkv_ref, attn_ref, lse_ref, cos_ref, sin_ref, segq_ref, segk_ref, gkv_ref, gqkv_ref
+    i, block, gm, wo_ref, qkv_ref, attn_ref, lse_ref, cos_ref, sin_ref, segq_ref, segk_ref, gkv_ref, gqkv_ref
 ):
     scale = HD**-0.5
     rows = slice(i * block, (i + 1) * block)
@@ -153,7 +153,7 @@
     row_pos = i * block + lax.broadcasted_iota(jnp.int32, (block, keys), 0)
     key_pos = lax.broadcasted_iota(jnp.int32, (block, keys), 1)
     allowed = (key_pos <= row_pos) & (segq_ref[rows, :1] == segk_ref[:1, :keys])
-    grad_attn = dot_nt(gm_ref[rows, :], wo_ref[...]).astype(BF16)
+    grad_attn = dot_nt(gm, wo_ref[...]).astype(BF16)
     for s in range(SLOTS):
         at = 3 * s * HD
         cut = slice(s * HD, (s + 1) * HD)
@@ -195,7 +195,7 @@
     gkv_ref[...] = jnp.zeros_like(gkv_ref)
     for i in range(count):
         attn_back_block(
-            i, block, gm_ref, wo_ref, qkv_ref, attn_ref, lse_ref, cos_ref, sin_ref, segq_ref, segk_ref, gkv_ref, gqkv_ref
+            i, block, gm_ref[i * block : (i + 1) * block, :], wo_ref, qkv_ref, attn_ref, lse_ref, cos_ref, sin_ref, segq_ref, segk_ref, gkv_ref, gqkv_ref
         )
     attn_back_keys(w_ref, cos_ref, sin_ref, gkv_ref, gqkv_ref, wt_ref)
     for i in range(count):
@@ -587,122 +587,103 @@
 
 
 def front_kernel(
-    tok_ref, wqkv_ref, wout_ref, router_ref, sup_ref, gains_ref, ids_ref, cos_ref, sin_ref, og_ref, eup_ref,
-    w_ref, wo_ref, tail_ref, gain_ref, mark_ref, own_mark_ref, segq_ref, segk_ref,
-    normed_ref, qkv_ref, attn_ref, lse_ref, mixed_ref, low_ref, plane_ref, all_grad_ref, pieces_ref,
-    seq, wq, wo_in, all_ids, qpack, tpack, part, wide, pack, *refs, nz, nf, hidden, shared, heads, real,
+    tok_ref, wqkv_ref, wout_ref, router_ref, sup_ref, again_ref, fgain_ref, eids_ref, seg_ref, cos_ref, sin_ref, og_ref,
+    eup_ref,
+    w_out, wo_ref, tail_out, router_out, gain_one_ref, gain_two_ref, mark_out, own_mark_ref, segq_ref, segk_ref,
+    normed_out, qkv_out, attn_out, lse_out, mixed_ref, low_ref, plane_ref, all_grad_ref, pieces_ref,
+    w_ref, tail_ref, mark_ref, normed_ref, qkv_ref, attn_ref, lse_ref, ids_ref, out_sems,
+    seq, wq, wo_in, wz, wzo, all_ids, qpack, tpack, part, wide, pack, *refs, nz, nf, hidden, shared, heads, real,
 ):
     bufs, refs = refs[:4], refs[4:]
-    tok_s, tok_r, all_s, all_r, wo_s, wo_r, rs, rr, gs, gr, xs, xr, es, er, own_sems = refs
+    (
+        tok_s, tok_r, all_s, all_r, q_s, q_r, wo_s, wo_r, zq_s, zq_r, zo_s, zo_r, rs, rr, gs, gr, xs, xr, es, er,
+        own_sems,
+    ) = refs
     z, f = place()
     me, count = z * nf + f, nz * nf
     rows, width = tok_ref.shape
     dense = wqkv_ref.shape[0]
-    experts = router_ref.shape[1]
+    experts = router_ref.shape[0]
     full = shared * count
     greet_all(nz, nf)
 
     toks = (tok_s, tok_r)
     to_near = [send(tok_ref, seq.at[f], toks, i, (z, flip(f, r))) for i, r in enumerate((2, 4, 6))]
     to_core = [send(tok_ref, seq.at[f], toks, 3, (z, flip(f, 1)))]
-    own = [
-        pltpu.make_async_copy(tok_ref, seq.at[f], own_sems.at[0]),
-        pltpu.make_async_copy(ids_ref, all_ids.at[me], own_sems.at[1]),
-        pltpu.make_async_copy(og_ref, all_grad_ref.at[z, f], own_sems.at[2]),
+    own = pltpu.make_async_copy(og_ref, all_grad_ref.at[z, f], own_sems.at[0])
+    own.start()
+    for copy in to_near + to_core:
+        copy.start()
+    seq[f] = tok_ref[...]
+    ids_ref[...] = jnp.concatenate([eids_ref[...], seg_ref[...]], axis=0)
+    all_ids[me] = ids_ref[...]
+    router = router_ref[...].astype(F32).T.astype(BF16)
+    both_gains = jnp.concatenate([again_ref[...], fgain_ref[...]], axis=1)
+
+    def leave(k, src, dst):
+        return pltpu.make_async_copy(src, dst, out_sems.at[k])
+
+    outgoing = [
+        leave(k, src, dst)
+        for k, (src, dst) in enumerate(
+            (
+                (w_ref, w_out), (tail_ref, tail_out), (mark_ref, mark_out), (normed_ref, normed_out),
+                (qkv_ref, qkv_out), (attn_ref, attn_out), (lse_ref, lse_out),
+            )
+        )
     ]
-    for copy in to_near + to_core + own:
+    own.wait()
+    grads = Gather(all_grad_ref, (gs, gr), nz, z, f)
+    grads.first(0, own=True)
+
+    def two(m):
+        return first_head(m + 1) - first_head(m) == 2
+
+    def wanted(m, block):
+        low, high = out_blocks(m, dense)
+        return (low <= block) & (block <= high)
+
+    low, high = out_blocks(f, dense)
+
+    def piece(j):
+        return lax.rem(z - away(j, nz) + nz, nz) if j else z
+
+    def along(src, dst, sems, j):
+        return send(src, dst.at[z], sems, j, (lax.rem(z + away(j, nz), nz), f))
+
+    zq = [None] + [along(wqkv_ref, wz, (zq_s, zq_r), j) for j in range(1, nz)]
+    zo = [None] + [along(wout_ref, wzo, (zo_s, zo_r), j) for j in range(1, nz)]
+    for copy in zq[1:] + zo[1:]:
         copy.start()
 
-    for m in range(8):
-        for s in range(SLOTS):
-            h = heads[m * SLOTS + s]
-            if real[m * SLOTS + s]:
-                qpack[m, s] = jnp.concatenate(
-                    [wqkv_ref[:, c * width + h * HD : c * width + (h + 1) * HD] for c in range(3)], axis=1
-                )
     pad = jnp.zeros((dense, TAIL - shared - experts), BF16)
     pad_two = jnp.zeros((dense, TAIL - shared - 2), BF16)
     for d in range(count):
         tpack[d] = jnp.concatenate(
             [
-                sup_ref[:, d * shared : (d + 1) * shared], router_ref[...], pad,
-                sup_ref[:, full + d * shared : full + (d + 1) * shared], gains_ref[...], pad_two,
+                sup_ref[:, d * shared : (d + 1) * shared], router, pad,
+                sup_ref[:, full + d * shared : full + (d + 1) * shared], both_gains, pad_two,
             ],
             axis=1,
         )
 
-    def two(m):
-        return first_head(m + 1) - first_head(m) == 2
-
     def copies(d, k):
-        src, dst = (
-            (qpack.at[d % nf, 0], wq.at[0, me]),
-            (qpack.at[d % nf, 1], wq.at[1, me]),
-            (tpack.at[d], tail_ref.at[me]),
-            (ids_ref, all_ids.at[me]),
-        )[k]
+        src, dst = ((tpack.at[d], tail_ref.at[me]), (ids_ref, all_ids.at[me]))[k]
         return pltpu.make_async_remote_copy(
             src, dst, all_s.at[k, d], all_r.at[k, me], device_id=(d // nf, d % nf), device_id_type=MESH
         )
 
     def came(d, k):
-        dst = (wq.at[0, d], wq.at[1, d], tail_ref.at[d], all_ids.at[d])[k]
+        dst = (tail_ref.at[d], all_ids.at[d])[k]
         return pltpu.make_async_remote_copy(
             dst, dst, all_s.at[k, d], all_r.at[k, d], device_id=(d // nf, d % nf), device_id_type=MESH
         )
 
-    def out_copy(d):
-        first, _ = out_blocks(d % nf, dense)
-        return pltpu.make_async_remote_copy(
-            wout_ref, wo_in.at[me - first], wo_s.at[d], wo_r.at[me - first],
-            device_id=(d // nf, d % nf), device_id_type=MESH,
-        )
-
-    def wanted(d, block):
-        low, high = out_blocks(d % nf, dense)
-        return (low <= block) & (block <= high)
-
     def start(i, _):
         d = (me + i) % count
         copies(d, 0).start()
-
-        @pl.when(two(d % nf))
-        def _():
-            copies(d, 1).start()
-
-        copies(d, 2).start()
-        copies(d, 3).start()
+        copies(d, 1).start()
         return 0
-
-    lax.fori_loop(1, count, start, 0)
-
-    def start_out(i, _):
-        d = (me + i) % count
-
-        @pl.when(wanted(d, me))
-        def _():
-            out_copy(d).start()
-
-        return 0
-
-    lax.fori_loop(1, count, start_out, 0)
-    own_packs = [
-        pltpu.make_async_copy(qpack.at[f, 0], wq.at[0, me], own_sems.at[3]),
-        pltpu.make_async_copy(tpack.at[me], tail_ref.at[me], own_sems.at[4]),
-    ]
-    for copy in own_packs:
-        copy.start()
-    own_two = pltpu.make_async_copy(qpack.at[f, 1], wq.at[1, me], own_sems.at[5])
-    low, high = out_blocks(f, dense)
-    own_out = pltpu.make_async_copy(wout_ref, wo_in.at[me - low], own_sems.at[6])
-
-    @pl.when(two(f))
-    def _():
-        own_two.start()
-
-    @pl.when(wanted(me, me))
-    def _():
-        own_out.start()
 
     whole = nz * hidden
     for t in range(nz):
@@ -714,49 +695,105 @@
             ],
             axis=1,
         )
+    tail_ref[me] = tpack[me]
+    lax.fori_loop(1, count, start, 0)
+
+    def q_copy(j, m, s):
+        return pltpu.make_async_remote_copy(
+            qpack.at[j, m, s], wq.at[s, piece(j) * nf + f], q_s.at[j, m, s], q_r.at[j, f, s],
+            device_id=(z, m), device_id_type=MESH,
+        )
+
+    def q_came(j, m, s):
+        dst = wq.at[s, piece(j) * nf + m]
+        return pltpu.make_async_remote_copy(
+            dst, dst, q_s.at[j, m, s], q_r.at[j, m, s], device_id=(z, m), device_id_type=MESH
+        )
+
+    def q_own(j, s):
+        wq[s, piece(j) * nf + f] = qpack[j, f, s]
+
+    def q_each(act, m):
+        act(0)
+
+        @pl.when(two(m))
+        def _():
+            act(1)
+
+    def q_send(j):
+        ref = wz.at[piece(j)] if j else wqkv_ref
+        for m in range(8):
+            for s in range(SLOTS):
+                h = heads[m * SLOTS + s]
+                if real[m * SLOTS + s]:
+                    qpack[j, m, s] = jnp.concatenate(
+                        [ref[:, c * width + h * HD : c * width + (h + 1) * HD] for c in range(3)], axis=1
+                    )
+
+        def go(i, _):
+            m = (f + i) % nf
+            q_each(lambda s: q_copy(j, m, s).start(), m)
+            return 0
+
+        lax.fori_loop(1, nf, go, 0)
+        q_each(lambda s: q_own(j, s), f)
+
+    grads.second(0)
     for i, r in enumerate((2, 4, 6)):
         to_near[i].wait_recv()
         slot = seq.at[flip(f, r)]
         copy = send(slot, slot, toks, 4 + i, (z, flip(f, 1)))
         copy.start()
         to_core.append(copy)
+    q_send(0)
+    grads.third(0)
+    for copy in zq[1:]:
+        copy.wait_send()
+    for j in range(1, nz):
+        grads.by_z(j).start()
+    for j in range(1, nz):
+        zq[j].wait_recv()
+        q_send(j)
 
     def arrive(i, _):
         d = (me + i) % count
         came(d, 0).wait_recv()
-
-        @pl.when(two(f))
-        def _():
-            came(d, 1).wait_recv()
-
-        came(d, 2).wait_recv()
-        came(d, 3).wait_recv()
+        came(d, 1).wait_recv()
         return 0
 
     lax.fori_loop(1, count, arrive, 0)
-    for copy in own + own_packs:
-        copy.wait()
-
-    @pl.when(two(f))
-    def _():
-        own_two.wait()
-
+
+    def q_arrive(i, _):
+        m = (f + i) % nf
+        for j in range(nz):
+            q_each(lambda s: q_came(j, m, s).wait_recv(), f)
+        return 0
+
+    lax.fori_loop(1, nf, q_arrive, 0)
     for copy in to_core:
         copy.wait_recv()
 
-    grads = Gather(all_grad_ref, (gs, gr), nz, z, f)
-    grads.along_z(1)
-    grads.first(0, own=True)
-
     w_ref[0] = wq[0].reshape(width, 3 * HD)
     w_ref[1] = jnp.where(two(f), wq[1].astype(F32), 0.0).reshape(width, 3 * HD).astype(BF16)
-    gain_ref[...] = tail_ref[...].reshape(width, 2 * TAIL)[:, TAIL + shared : TAIL + shared + 2].astype(F32).T
+    outgoing[0].start()
+    outgoing[1].start()
+    tails = tail_ref[...].reshape(width, 2 * TAIL)
+    gains = tails[:, TAIL + shared : TAIL + shared + 2].astype(F32).T
+    gain_one_ref[...] = gains[0:1]
+    gain_two_ref[...] = gains[1:2]
+    router_out[...] = jnp.concatenate(
+        [
+            jnp.zeros((width, TAIL + shared), BF16), tails[:, shared : shared + experts],
+            jnp.zeros((width, TAIL - shared - experts), BF16),
+        ],
+        axis=1,
+    )
     for m in range(8):
         ids = all_ids[z * nf + m]
         segk_ref[:, m * rows : (m + 1) * rows] = jnp.broadcast_to(ids[-1:], (8, rows))
         segq_ref[m * rows : (m + 1) * rows, :] = jnp.broadcast_to(ids.T[:, -1:], (rows, HD))
     block = 256
-    gain_one = gain_ref[0:1, :]
+    gain_one = gain_one_ref[...]
 
     def project(i, _):
         x = seq[pl.ds(i * (block // rows), block // rows)].reshape(block, width)
@@ -764,63 +801,101 @@
         return 0
 
     lax.fori_loop(0, 8 * rows // block, project, 0)
-    grads.second(0)
-    grads.along_z(2)
+    outgoing[3].start()
+    outgoing[4].start()
+    def out_block(j):
+        return piece(j) * nf + f
+
+    def out_src(j):
+        return wzo.at[piece(j)] if j else wout_ref
+
+    def out_copy(j, m):
+        first, _ = out_blocks(m, dense)
+        slot = out_block(j) - first
+        return pltpu.make_async_remote_copy(
+            out_src(j), wo_in.at[slot], wo_s.at[j, m], wo_r.at[slot], device_id=(z, m), device_id_type=MESH
+        )
+
+    def out_own(j):
+        wo_in[out_block(j) - low] = wzo[piece(j)] if j else wout_ref[...]
+
+    def out_each(act, act_own):
+        for j in range(nz):
+
+            def one(i, _):
+                m = (f + i) % nf
+
+                @pl.when(wanted(m, out_block(j)))
+                def _():
+                    act(j, m)
+
+                return 0
+
+            lax.fori_loop(1, nf, one, 0)
+
+            @pl.when(wanted(f, out_block(j)))
+            def _():
+                act_own(j)
+
+    for j in range(1, nz):
+        zo[j].wait()
+    out_each(lambda j, m: out_copy(j, m).start(), out_own)
+
+    reduce = Reduce(bufs, (rs, rr), 1, z, f)
+    for i in range(8 * rows // block):
+        attn_block(i, block, segq_ref, segk_ref, qkv_ref, attn_ref, lse_ref)
+
+    outgoing[5].start()
+    outgoing[6].start()
 
     def arrive_out(j, _):
-        @pl.when((low + j <= high) & (low + j != me))
+        @pl.when((low + j <= high) & (lax.rem(low + j, nf) != f))
         def _():
             pltpu.make_async_remote_copy(
-                wo_in.at[j], wo_in.at[j], wo_s.at[j], wo_r.at[j], device_id=(z, flip(f, 1)), device_id_type=MESH
+                wo_in.at[j], wo_in.at[j], wo_s.at[0, j], wo_r.at[j], device_id=(z, flip(f, 1)), device_id_type=MESH
             ).wait_recv()
 
         return 0
 
     lax.fori_loop(0, wo_in.shape[0], arrive_out, 0)
-
-    @pl.when(wanted(me, me))
-    def _():
-        own_out.wait()
-
     wide[...] = wo_in[...].astype(F32).reshape(wide.shape)
     offset = pl.multiple_of(first_head(f) * HD - low * dense, 8)
     wo_ref[:HD, :] = wide[pl.ds(offset, HD), :].astype(BF16)
     wo_ref[HD:, :] = jnp.where(two(f), wide[pl.ds(offset + HD, HD), :], 0.0).astype(BF16)
-    reduce = Reduce(bufs, (rs, rr), 1, z, f)
     for i in range(8 * rows // block):
-        outs = attn_block(i, block, segq_ref, segk_ref, qkv_ref, attn_ref, lse_ref)
         at = i * (block // rows)
-        part[at : at + block // rows] = dot(outs, wo_ref[...]).astype(BF16).reshape(block // rows, rows, width)
-        if i == 1:
-            grads.third(0)
+        part[at : at + block // rows] = (
+            dot(attn_ref[i * block : (i + 1) * block, :], wo_ref[...]).astype(BF16).reshape(block // rows, rows, width)
+        )
     for i in range(4):
         reduce.core(0, i, part.at[flip(f, 1 | 2 * i)]).start()
-    for i in range(4):
-        reduce.core(0, i, None).wait_recv()
-        reduce.by_core[0, i] = reduce.by_core[0, i] + part[flip(f, 2 * i)]
-    reduce.send_near(0)
-    grads.along_z(3)
-    reduce.far(0)
-    reduce.along_z(0)
-    mixed = tok_ref[...].astype(F32) + reduce.by_far[0].astype(F32)
-    mixed_ref[...] = mixed
-    low_ref[...] = (mixed * rms_scale(mixed) * gain_ref[1:2, :]).astype(BF16)
-    near_own = pltpu.make_async_copy(low_ref, plane_ref.at[0, f], own_sems.at[7])
-    near_own.start()
-    near = Gather(plane_ref, (xs, xr), 1, z, f)
-    near_own.wait()
-    near.first(0, own=True)
-
     ups = []
     for j in range(1, nz):
         there = lax.rem(z + j, nz)
         copy = send(pack.at[there], pieces_ref.at[z], (es, er), j, (there, f))
         copy.start()
         ups.append(copy)
-    ups.append(pltpu.make_async_copy(pack.at[z], pieces_ref.at[z], own_sems.at[8]))
+    ups.append(pltpu.make_async_copy(pack.at[z], pieces_ref.at[z], own_sems.at[2]))
     ups[-1].start()
-
+    for i in range(4):
+        reduce.core(0, i, None).wait_recv()
+        reduce.by_core[0, i] = reduce.by_core[0, i] + part[flip(f, 2 * i)]
+    reduce.send_near(0)
+    reduce.far(0)
+    reduce.along_z(0)
+    mixed = tok_ref[...].astype(F32) + reduce.by_far[0].astype(F32)
+    mixed_ref[...] = mixed
+    low_ref[...] = (mixed * rms_scale(mixed) * gain_two_ref[...]).astype(BF16)
+    near_own = pltpu.make_async_copy(low_ref, plane_ref.at[0, f], own_sems.at[1])
+    near_own.start()
+    near = Gather(plane_ref, (xs, xr), 1, z, f)
+    near_own.wait()
+    near.first(0, own=True)
+    for j in range(1, nz):
+        grads.first(j)
     near.second(0)
+    for j in range(1, nz):
+        grads.second(j)
     lane = lax.broadcasted_iota(jnp.int32, (rows, HD), 1) - TAIL - shared
 
     def mark(d, _):
@@ -838,12 +913,9 @@
         return 0
 
     lax.fori_loop(0, count, mark, 0)
+    outgoing[2].start()
     near.third(0)
     for j in range(1, nz):
-        grads.first(j)
-        grads.second(j)
-        if j + 3 <= nz:
-            grads.along_z(j + 3)
         grads.third(j)
     for j in range(nz):
         grads.fourth(j)
@@ -852,33 +924,33 @@
     def left(i, _):
         d = (me + i) % count
         copies(d, 0).wait_send()
-
-        @pl.when(two(d % nf))
-        def _():
-            copies(d, 1).wait_send()
-
-        copies(d, 2).wait_send()
-        copies(d, 3).wait_send()
-
-        @pl.when(wanted(d, me))
-        def _():
-            out_copy(d).wait_send()
-
+        copies(d, 1).wait_send()
         return 0
 
     lax.fori_loop(1, count, left, 0)
+
+    def q_left(i, _):
+        m = (f + i) % nf
+        for j in range(nz):
+            q_each(lambda s: q_copy(j, m, s).wait_send(), m)
+        return 0
+
+    lax.fori_loop(1, nf, q_left, 0)
+    out_each(lambda j, m: out_copy(j, m).wait_send(), lambda j: None)
     for copy in to_near + to_core:
         copy.wait_send()
     for i in range(4):
         reduce.core(0, i, part.at[0]).wait_send()
     reduce.end()
+    for j in range(1, nz):
+        grads.by_z(j).wait_send()
     grads.end()
     near.end()
-    for copy in ups:
+    for copy in ups + outgoing:
         copy.wait()
 
 
-def front(tok, wqkv, wout, router, sup, gains, ids, cosine, sine, og, eup, nz, nf, shared):
+def front(tok, wqkv, wout, router, sup, again, fgain, eids, seg, cosine, sine, og, eup, nz, nf, shared):
     rows, width = tok.shape
     dense, count = wqkv.shape[0], nz * nf
     length = 8 * rows
@@ -891,7 +963,9 @@
             shape((SLOTS, width, 3 * HD), BF16),
             shape((SLOTS * HD, width), BF16),
             shape((count, dense, 2 * TAIL), BF16),
-            shape((2, width), F32),
+            shape((width, HD), BF16),
+            shape((1, width), F32),
+            shape((1, width), F32),
             shape((count, rows, HD), BF16),
             shape((rows, HD), F32),
             shape((length, HD), jnp.int32),
@@ -906,35 +980,50 @@
             shape((nz, 8, rows, width), BF16),
             shape((nz, up_rows, 4 * hidden), BF16),
         ),
-        in_specs=[VMEM] * 9 + [ANY, VMEM],
-        out_specs=(VMEM,) * 14 + (ANY,) * 3,
+        in_specs=[VMEM] * 13,
+        out_specs=(ANY, VMEM, ANY, VMEM, VMEM, VMEM, ANY, VMEM, VMEM, VMEM) + (ANY,) * 4 + (VMEM,) * 2 + (ANY,) * 3,
         scratch_shapes=[
+            pltpu.VMEM((SLOTS, width, 3 * HD), BF16),
+            pltpu.VMEM((count, dense, 2 * TAIL), BF16),
+            pltpu.VMEM((count, rows, HD), BF16),
+            pltpu.VMEM((length, width), BF16),
+            pltpu.VMEM((length, 3 * SLOTS * HD), BF16),
+            pltpu.VMEM((length, SLOTS * HD), BF16),
+            pltpu.VMEM((length, SLOTS * HD), F32),
+            pltpu.VMEM((eids.shape[0] + 1, rows), jnp.int32),
+            pltpu.SemaphoreType.DMA((7,)),
             pltpu.VMEM((8, rows, width), BF16),
             pltpu.VMEM((SLOTS, count, dense, 3 * HD), BF16),
             pltpu.VMEM((8, dense, width), BF16),
-            pltpu.VMEM((count, *ids.shape), jnp.int32),
-            pltpu.VMEM((8, SLOTS, dense, 3 * HD), BF16),
+            pltpu.VMEM((nz, dense, 3 * width), BF16),
+            pltpu.VMEM((nz, dense, width), BF16),
+            pltpu.VMEM((count, eids.shape[0] + 1, rows), jnp.int32),
+            pltpu.VMEM((nz, 8, SLOTS, dense, 3 * HD), BF16),
             pltpu.VMEM((count, dense, 2 * TAIL), BF16),
             pltpu.VMEM((8, rows, width), BF16),
             pltpu.VMEM((8 * dense, width), F32),
             pltpu.VMEM((nz, up_rows, 4 * hidden), BF16),
             *Reduce.scratch(1, rows, width),
             *pair_of(7),
-            pltpu.SemaphoreType.DMA((4, count)),
-            pltpu.SemaphoreType.DMA((4, count)),
-            pltpu.SemaphoreType.DMA((count,)),
+            pltpu.SemaphoreType.DMA((2, count)),
+            pltpu.SemaphoreType.DMA((2, count)),
+            pltpu.SemaphoreType.DMA((nz, 8, SLOTS)),
+            pltpu.SemaphoreType.DMA((nz, 8, SLOTS)),
+            pltpu.SemaphoreType.DMA((nz, 8)),
             pltpu.SemaphoreType.DMA((8,)),
+            *pair_of(nz),
+            *pair_of(nz),
             *pair_of(Reduce.copies(1)),
             *pair_of(Gather.copies(nz)),
             *pair_of(Gather.copies(1)),
             *pair_of(nz),
-            pltpu.SemaphoreType.DMA((9,)),
+            pltpu.SemaphoreType.DMA((3,)),
         ],
         compiler_params=pltpu.CompilerParams(
             collective_id=1, has_side_effects=True, vmem_limit_bytes=58 * 2**20
         ),
         name="front",
-    )(tok, wqkv, wout, router, sup, gains, ids, cosine, sine, og, eup)
+    )(tok, wqkv, wout, router, sup, again, fgain, eids, seg, cosine, sine, og, eup)
 
 
 def route_grads(gx, og, mixed, normed, router, marks, gain):
@@ -960,11 +1049,12 @@
 def experts_kernel(
     normed_ref, plane_ref, all_grad_ref, mark_ref, own_ref, eup_ref, tail_ref, edown_ref, sdown_ref,
     og_ref, mixed_ref, router_ref, own_mark_ref, gain_ref,
-    out_ref, seq_ref, gm_ref, small_ref, pieces_ref, gedown_ref, gsdown_ref, all_normed_ref,
+    out_any, low_ref, gm_ref, small_ref, geup_ref, gedown_ref, gsdown_ref, all_normed_ref,
+    out_ref,
     up_ref, upt_ref, down_ref, downt_ref, gup_ref, gdown_ref,
-    xt, gt, mt, px, po, low, *refs, nz, hidden, shared,
+    xt, gt, mt, px, po, *refs, nz, hidden, shared,
 ):
-    bufs, (tile_sems, rs, rr, os_, or_, xs, xr, gs, gr, es, er, own_sems) = refs[:4], refs[4:]
+    bufs, (tile_sems, rs, rr, os_, or_, xs, xr, own_sems) = refs[:4], refs[4:]
     z, f = place()
     rows, width = mixed_ref.shape
     half = down_ref.shape[0]
@@ -1087,50 +1177,33 @@
     lax.fori_loop(0, 4 * nz, tile, 0)
     up_ref[:, : 2 * pair] = jnp.concatenate([gup_ref[:, :pair], gup_ref[:, half : half + pair]], axis=1).astype(BF16)
     up_rows = width // nz
-
-    def ups(j):
-        there = lax.rem(z + j, nz)
-        src = up_ref.at[pl.ds(pl.multiple_of(there * up_rows, up_rows), up_rows), pl.ds(0, 2 * pair)]
-        if j == 0:
-            return pltpu.make_async_copy(src, pieces_ref.at[z], own_sems.at[1])
-        return send(src, pieces_ref.at[z], (es, er), j, (there, f))
-
-    for j in (1, nz - 1):
-        ups(j).start()
-    own_down = pltpu.make_async_copy(gdown_ref.at[pl.ds(0, pair)], gedown_ref, own_sems.at[2])
-    own_down.start()
-    ups(0).start()
+    ends = [
+        pltpu.make_async_copy(up_ref.at[pl.ds(p * up_rows, up_rows), pl.ds(0, 2 * pair)], geup_ref.at[p], own_sems.at[p])
+        for p in range(nz)
+    ]
+    ends.append(pltpu.make_async_copy(gdown_ref.at[pl.ds(0, pair)], gedown_ref, own_sems.at[nz]))
+    ends.append(pltpu.make_async_copy(out_ref, out_any, own_sems.at[nz + 1]))
+    for copy in ends:
+        copy.start()
     reduce.far(nz - 1)
     gtail = jnp.concatenate([gup_ref[:, half - TAIL : half], gup_ref[:, 2 * half - TAIL :]], axis=1)
     gsdown_ref[...] = gdown_ref[half - TAIL : half - TAIL + shared, :]
     reduce.along_z(nz - 1)
-    for j in range(2, nz - 1):
-        ups(j).start()
     grad_mixed, small = route_grads(
         reduce.total(), og_ref[...], mixed_ref[...], normed_ref[...], router_ref[...], own_mark_ref[...], gain_ref[...]
     )
     gm_ref[...] = grad_mixed
-    low[...] = grad_mixed.astype(BF16)
-    own = pltpu.make_async_copy(low, seq_ref.at[0, f], own_sems.at[3])
-    own.start()
-    turned = Gather(seq_ref, (gs, gr), 1, z, f)
-    own.wait()
-    turned.first(0, own=True)
-    small_ref[...] = small + gtail
-    turned.second(0)
-    turned.third(0)
-    turned.fourth(0)
+    low_ref[...] = grad_mixed.astype(BF16)
+    small_ref[...] = (small + gtail).astype(BF16)
     for k in range(4):
         reduce.core(nz - 1, k, px.at[k]).wait_send()
         outs.core(nz - 1, k, po.at[k]).wait_send()
-    own_down.wait()
-    for j in range(nz):
-        ups(j).wait()
+    for copy in ends:
+        copy.wait()
     for j in range(4, nz + 1):
         gather.along_z(j)
     gather.end(1)
     reduce.end()
-    turned.end()
 
 
 def experts_turn(
@@ -1144,17 +1217,18 @@
         functools.partial(experts_kernel, nz=nz, hidden=pair // 2, shared=shared),
         out_shape=(
             jax.ShapeDtypeStruct((nz, 4, rows, width), BF16),
-            jax.ShapeDtypeStruct((1, 8, rows, width), BF16),
+            jax.ShapeDtypeStruct((rows, width), BF16),
             jax.ShapeDtypeStruct((rows, width), F32),
-            jax.ShapeDtypeStruct((width, HD), F32),
+            jax.ShapeDtypeStruct((width, HD), BF16),
             jax.ShapeDtypeStruct((nz, width // nz, 2 * pair), BF16),
             jax.ShapeDtypeStruct((pair, width), F32),
             jax.ShapeDtypeStruct((shared, width), F32),
             jax.ShapeDtypeStruct((nz, 8, rows, width), BF16),
         ),
         in_specs=[VMEM, ANY, ANY, ANY] + [VMEM] * 10,
-        out_specs=(VMEM, ANY, VMEM, VMEM, ANY, ANY, VMEM, ANY),
+        out_specs=(ANY, VMEM, VMEM, VMEM, ANY, ANY, VMEM, ANY),
         scratch_shapes=[
+            pltpu.VMEM((nz, 4, rows, width), BF16),
             pltpu.VMEM((width, 2 * half), BF16),
             pltpu.VMEM((2 * half, width), BF16),
             pltpu.VMEM((half, width), BF16),
@@ -1166,15 +1240,12 @@
             pltpu.VMEM((2, 2, rows, HD), BF16),
             pltpu.VMEM((8, rows, wide), BF16),
             pltpu.VMEM((8, rows, width), BF16),
-            pltpu.VMEM((rows, width), BF16),
             *Reduce.scratch(nz, rows, wide),
             pltpu.SemaphoreType.DMA((2, 6)),
             *pair_of(Reduce.copies(nz)),
             *pair_of(Reduce.copies(nz)),
             *pair_of(Gather.copies(nz)),
-            *pair_of(Gather.copies(1)),
-            *pair_of(nz),
-            pltpu.SemaphoreType.DMA((4,)),
+            pltpu.SemaphoreType.DMA((nz + 2,)),
         ],
         compiler_params=pltpu.CompilerParams(
             collective_id=3, has_side_effects=True, vmem_limit_bytes=60 * 2**20
@@ -1186,22 +1257,51 @@
 
 
 def back_kernel(
-    gm_ref, wo_ref, w_ref, normed_ref, qkv_ref, attn_ref, lse_ref, cos_ref, sin_ref, segq_ref, segk_ref,
+    low_ref, geup_ref, *refs, nz, nf, heads, real,
+):
+    sources, refs = refs[:11], refs[11:]
+    (wo_ref, w_ref, normed_ref, qkv_ref, attn_ref, lse_ref, cos_ref, sin_ref, segq_ref, segk_ref, out_ref), refs = (
+        refs[-12:-1],
+        refs[:-12] + refs[-1:],
+    )
+    back_body(sources, low_ref, geup_ref, wo_ref, w_ref, normed_ref, qkv_ref, attn_ref, lse_ref, cos_ref, sin_ref,
+              segq_ref, segk_ref, out_ref, *refs, nz=nz, nf=nf, heads=heads, real=real)
+
+
+def back_body(
+    sources, low_ref, geup_ref, wo_ref, w_ref, normed_ref, qkv_ref, attn_ref, lse_ref, cos_ref, sin_ref, segq_ref, segk_ref,
     out_ref, small_ref, tok_ref, mixed_ref, own_gm_ref, gain_ref,
-    block_ref, gtok_ref, gwqkv_ref, gwout_ref, all_small_ref,
-    gkv_ref, gqkv_ref, wt_ref, part_ref, gw_ref, gwo_ref, gws, gwos, smalls, *refs, nz, nf, heads, real,
+    block_ref, gtok_ref, gwqkv_ref, gwout_ref, all_small_ref, pieces_ref,
+    seq, gkv_ref, gqkv_ref, wt_ref, part_ref, gw_ref, gwo_ref, gws, gwos, smalls, *refs, nz, nf, heads, real,
 ):
     bufs, refs = refs[:7], refs[7:]
-    rs, rr, os_, or_, all_s, all_r, wo_s, wo_r, own_sems = refs
+    rs, rr, os_, or_, all_s, all_r, wo_s, wo_r, gs, gr, es, er, own_sems, in_sems = refs
+    local = (wo_ref, w_ref, normed_ref, qkv_ref, attn_ref, lse_ref, cos_ref, sin_ref, segq_ref, segk_ref, out_ref)
+    loads = [pltpu.make_async_copy(src, dst, in_sems.at[k]) for k, (src, dst) in enumerate(zip(sources, local))]
+    for copy in loads:
+        copy.start()
     z, f = place()
     me, count = z * nf + f, nz * nf
     dense = gw_ref.shape[2]
     rows, width = tok_ref.shape
-    length = gm_ref.shape[0]
+    length = 8 * rows
     greet_all(nz, nf)
+    seq[0, f] = low_ref[...]
+    turned = Gather(seq, (gs, gr), 1, z, f)
+    turned.first(0, own=True)
+    ups = []
+    for j in range(1, nz):
+        there = lax.rem(z + j, nz)
+        ups.append(send(geup_ref.at[there], pieces_ref.at[z], (es, er), j, (there, f)))
+    ups.append(pltpu.make_async_copy(geup_ref.at[z], pieces_ref.at[z], own_sems.at[0]))
+    for copy in ups:
+        copy.start()
+    turned.second(0)
     outs = Reduce([out_ref, *bufs[4:]], (os_, or_), nz, z, f)
     order = list(range(1, nz)) + [0]
+    loads[10].wait()
     outs.send_near(order[0])
+    turned.third(0)
 
     def two(m):
         return first_head(m + 1) - first_head(m) == 2
@@ -1229,12 +1329,15 @@
             device_id=(d // nf, d % nf), device_id_type=MESH,
         )
 
+    for copy in loads[:10]:
+        copy.wait()
+    turned.fourth(0)
     spare = gwo_ref.shape[0] * dense
     wide = up_to(spare, HD)
     shift = first_head(f) * HD - low * dense
     moved = jnp.concatenate([attn_ref[...].astype(F32), jnp.zeros((length, wide - SLOTS * HD), F32)], axis=1)
     moved = pltpu.roll(moved, shift, 1).astype(BF16)
-    gwo_ref[...] = dot_tn(moved, gm_ref[...])[:spare].reshape(gwo_ref.shape).astype(BF16)
+    gwo_ref[...] = dot_tn(moved, seq[0].reshape(length, width))[:spare].reshape(gwo_ref.shape).astype(BF16)
 
     def start_small(i, _):
         d = (me + i) % count
@@ -1248,19 +1351,17 @@
 
     lax.fori_loop(1, count, start_small, 0)
     own_slot = 2 * z + f - owner_of(me)
-    own_out = pltpu.make_async_copy(gwo_ref.at[me - low], gwos.at[own_slot], own_sems.at[0])
-    own_small = pltpu.make_async_copy(small_ref.at[me], smalls.at[me], own_sems.at[1])
-    own_small.start()
+    smalls[me] = small_ref[me]
 
     @pl.when(wanted(f, me))
     def _():
-        own_out.start()
+        gwos[own_slot] = gwo_ref[me - low]
 
     gkv_ref[...] = jnp.zeros_like(gkv_ref)
     block = 256
     for i in range(length // block):
         attn_back_block(
-            i, block, gm_ref, wo_ref, qkv_ref, attn_ref, lse_ref, cos_ref, sin_ref, segq_ref, segk_ref, gkv_ref, gqkv_ref
+            i, block, seq[0, i * block // rows : (i + 1) * block // rows].reshape(block, width), wo_ref, qkv_ref, attn_ref, lse_ref, cos_ref, sin_ref, segq_ref, segk_ref, gkv_ref, gqkv_ref
         )
         if i + 1 < nz:
             outs.send_near(order[i + 1])
@@ -1280,8 +1381,6 @@
     for i in range(4):
         reduce.core(0, i, part_ref.at[flip(f, 1 | 2 * i)]).start()
 
-    own_gw = [pltpu.make_async_copy(gw_ref.at[s, me], gws.at[s, me], own_sems.at[2 + s]) for s in range(SLOTS)]
-
     def weights(s):
         value = dot_tn(normed_ref[...], gqkv_ref[:, s * step : (s + 1) * step])
         gw_ref[s] = value.reshape(count, dense, step).astype(BF16)
@@ -1291,7 +1390,7 @@
             return 0
 
         lax.fori_loop(1, count, start, 0)
-        own_gw[s].start()
+        gws[s, me] = gw_ref[s, me]
 
     weights(0)
     for i in range(4):
@@ -1329,10 +1428,6 @@
                 gwo_ref.at[0], gwos.at[k], wo_s.at[0], wo_r.at[k], device_id=(z, flip(f, 1)), device_id_type=MESH
             ).wait_recv()
 
-    @pl.when(wanted(f, me))
-    def _():
-        own_out.wait()
-
     gwout_ref[...] = sum(gwos[2 * t].astype(F32) for t in range(nz))
 
     @pl.when(next_owner != owner)
@@ -1369,13 +1464,6 @@
         return 0
 
     lax.fori_loop(1, count, finish, 0)
-    own_small.wait()
-    own_gw[0].wait()
-
-    @pl.when(two(f))
-    def _():
-        own_gw[1].wait()
-
     for m in range(8):
         for s in range(SLOTS):
             if real[m * SLOTS + s]:
@@ -1388,13 +1476,16 @@
         reduce.core(0, i, part_ref.at[0]).wait_send()
     reduce.end()
     outs.end()
+    turned.end()
+    for copy in ups:
+        copy.wait()
 
 
 def back(
-    gm, wo, w, normed, qkv, attn, lse, cosine, sine, segq, segk, out_part, small, tok, mixed, own_gm, gain, nz, nf
+    low, geup, wo, w, normed, qkv, attn, lse, cosine, sine, segq, segk, out_part, small, tok, mixed, own_gm, gain, nz, nf
 ):
     rows, width = tok.shape
-    length, count = gm.shape[0], nz * nf
+    length, count = 8 * rows, nz * nf
     dense = width // count
     heads, real = head_table(8)
     return pl.pallas_call(
@@ -1405,10 +1496,12 @@
             jax.ShapeDtypeStruct((dense, 3 * width), F32),
             jax.ShapeDtypeStruct((dense, width), F32),
             jax.ShapeDtypeStruct((count, dense, HD), BF16),
+            jax.ShapeDtypeStruct(geup.shape, BF16),
         ),
-        in_specs=[VMEM] * 17,
-        out_specs=(VMEM,) * 5,
+        in_specs=[VMEM] + [ANY] * 12 + [VMEM] * 5,
+        out_specs=(VMEM,) * 5 + (ANY,),
         scratch_shapes=[
+            pltpu.VMEM((1, 8, rows, width), BF16),
             pltpu.VMEM((length, 2 * SLOTS * HD), F32),
             pltpu.VMEM((length, 3 * SLOTS * HD), BF16),
             pltpu.VMEM((3 * SLOTS * HD, width), BF16),
@@ -1426,23 +1519,32 @@
             pltpu.SemaphoreType.DMA((3, count)),
             pltpu.SemaphoreType.DMA((8,)),
             pltpu.SemaphoreType.DMA((2 * nz,)),
-            pltpu.SemaphoreType.DMA((4,)),
+            *pair_of(Gather.copies(1)),
+            *pair_of(nz),
+            pltpu.SemaphoreType.DMA((1,)),
+            *[pltpu.VMEM(a.shape, a.dtype) for a in (wo, w, normed, qkv, attn, lse, cosine, sine, segq, segk, out_part)],
+            pltpu.SemaphoreType.DMA((11,)),
         ],
         compiler_params=pltpu.CompilerParams(
             collective_id=4, has_side_effects=True, vmem_limit_bytes=60 * 2**20
         ),
         name="back",
     )(
-        gm, wo, w, normed, qkv, attn, lse, cosine, sine, segq, segk, out_part,
-        small.astype(BF16).reshape(count, dense, HD), tok, mixed, own_gm, gain,
+        low, geup, wo, w, normed, qkv, attn, lse, cosine, sine, segq, segk, out_part,
+        small.reshape(count, dense, HD), tok, mixed, own_gm, gain,
     )
 
 
 def unpack_kernel(
-    pieces_ref, small_ref, wqkv_ref, gwqkv_ref, gain_ref,
-    geup_ref, gsup_ref, grouter_ref, ggain_ref,
+    pieces_ref, small_ref, wqkv_ref, gwqkv_ref, gain_ref, block_in, tok_in, wout_in, edown_in, sdown_in,
+    geup_ref, gsup_ref, grouter_ref, gone_ref, gtwo_ref, block_ref, tok_ref, gqkv_ref, wout_ref, edown_ref, sdown_ref,
     *, shared, experts,
 ):
+    for src, dst in (
+        (block_in, block_ref), (tok_in, tok_ref), (gwqkv_ref, gqkv_ref), (wout_in, wout_ref), (edown_in, edown_ref),
+        (sdown_in, sdown_ref),
+    ):
+        dst[...] = src[...]
     nz = pieces_ref.shape[0]
     hidden = pieces_ref.shape[2] // 4
     for t in range(nz):
@@ -1459,12 +1561,13 @@
         for g in range(2):
             to = (g * count + d) * shared
             gsup_ref[:, to : to + shared] = small_ref[d, :, g * TAIL : g * TAIL + shared].astype(F32)
-    grouter_ref[...] = total[:, shared : shared + experts]
-    one = jnp.sum(wqkv_ref[...].astype(F32) * gwqkv_ref[...], axis=-1, keepdims=True) / gain_ref[:, :1].astype(F32)
-    ggain_ref[...] = jnp.concatenate([one, total[:, HD - 1 :]], axis=1)
-
-
-def unpack(pieces, small, wqkv, gwqkv, gains, shared, experts):
+    grouter_ref[...] = total[:, shared : shared + experts].T
+    one = jnp.sum(wqkv_ref[...].astype(F32) * gwqkv_ref[...], axis=-1, keepdims=True) / gain_ref[...].astype(F32)
+    gone_ref[...] = one.T
+    gtwo_ref[...] = total[:, HD - 1 :].T
+
+
+def unpack(pieces, small, wqkv, gwqkv, gain, rest, shared, experts):
     nz, up_rows, packed = pieces.shape
     count, dense, _ = small.shape
     return pl.pallas_call(
@@ -1472,14 +1575,16 @@
         out_shape=(
             jax.ShapeDtypeStruct((2, up_rows, nz * packed // 2), F32),
             jax.ShapeDtypeStruct((dense, 2 * count * shared), F32),
-            jax.ShapeDtypeStruct((dense, experts), F32),
-            jax.ShapeDtypeStruct((dense, 2), F32),
+            jax.ShapeDtypeStruct((experts, dense), F32),
+            jax.ShapeDtypeStruct((1, dense), F32),
+            jax.ShapeDtypeStruct((1, dense), F32),
+            *[jax.ShapeDtypeStruct(a.shape, a.dtype) for a in (*rest[:2], gwqkv, *rest[2:])],
         ),
-        in_specs=[VMEM] * 5,
-        out_specs=(VMEM,) * 4,
-        compiler_params=pltpu.CompilerParams(vmem_limit_bytes=32 * 2**20),
+        in_specs=[VMEM] * 10,
+        out_specs=(VMEM,) * 11,
+        compiler_params=pltpu.CompilerParams(vmem_limit_bytes=40 * 2**20),
         name="unpack",
-    )(pieces, small, wqkv, gwqkv, gains)
+    )(pieces, small, wqkv, gwqkv, gain, *rest)
 
 
 def tables():
@@ -1500,31 +1605,33 @@
     experts = w_router.shape[1]
     hidden, shared = w_expert_down.shape[1], w_shared_down.shape[0]
     f = lax.axis_index("fsdp")
-    gains = jnp.stack([attn_gain, ffn_gain], axis=1)
-    ids = jnp.concatenate([expert_ids.T, segment_ids[None]], axis=0)
     cosine, sine = tables()
     (
-        w, wo, tail, all_gains, marks, own_marks, segq, segk, normed_one, qkv, attn, lse, mixed, normed, plane, all_grad,
-        pieces,
+        w, wo, tail, router, gain_one, gain_two, marks, own_marks, segq, segk, normed_one, qkv, attn, lse, mixed, normed,
+        plane, all_grad, pieces,
     ) = front(
-        tokens, w_qkv, w_out, w_router, w_shared_up, gains, ids, cosine, sine, out_grad, w_expert_up, nz, nf, shared
+        tokens, w_qkv, w_out, w_router.T, w_shared_up, attn_gain[:, None], ffn_gain[:, None], expert_ids.T,
+        segment_ids[None], cosine, sine, out_grad, w_expert_up, nz, nf, shared,
     )
     tail = tail.reshape(width, 2 * TAIL)
-    gain_one, gain_two = all_gains[:1], all_gains[1:]
-    router = jnp.pad(tail[:, shared : shared + experts], ((0, 0), (TAIL + shared, TAIL - shared - experts)))
     lane = jnp.arange(HD, dtype=jnp.int32) - TAIL - shared
     own = (lane[None, :] == (2 * f + jnp.arange(2, dtype=jnp.int32))[:, None]).astype(F32)
-    out_part, seq_gm, grad_mixed, small, gpieces, gedown, gsdown = experts_turn(
+    out_part, low, grad_mixed, small, geup, gedown, gsdown = experts_turn(
         normed, plane, all_grad, marks, own, pieces.reshape(width, 4 * hidden), tail,
         w_expert_down.reshape(2 * hidden, width), w_shared_down, out_grad, mixed, router, own_marks, gain_two, nz, nf,
     )
-    block_out, tokens_grad, grad_wqkv, grad_wout, smalls = back(
-        seq_gm.reshape(SEQ, width), wo, w, normed_one, qkv, attn, lse, cosine, sine, segq, segk, out_part, small,
+    block_out, tokens_grad, grad_wqkv, grad_wout, smalls, gpieces = back(
+        low, geup, wo, w, normed_one, qkv, attn, lse, cosine, sine, segq, segk, out_part, small,
         tokens, mixed, grad_mixed, gain_one, nz, nf,
     )
-    grad_eup, grad_sup, grad_router, grad_gains = unpack(gpieces, smalls, w_qkv, grad_wqkv, gains, shared, experts)
+    (
+        grad_eup, grad_sup, grad_router, grad_one, grad_two, block_out, tokens_grad, grad_wqkv, grad_wout, gedown, gsdown,
+    ) = unpack(
+        gpieces, smalls, w_qkv, grad_wqkv, attn_gain[:, None], (block_out, tokens_grad, grad_wout, gedown, gsdown),
+        shared, experts,
+    )
     return (
-        block_out, tokens_grad, grad_gains[:, 0], grad_gains[:, 1], grad_wqkv, grad_wout, grad_router, grad_sup,
+        block_out, tokens_grad, grad_one[0], grad_two[0], grad_wqkv, grad_wout, grad_router.T, grad_sup,
         gsdown, grad_eup, gedown.reshape(2, hidden, width),
     )
 

time: 495 us -> 457 us (0.923)
  Pallas kernels: 474 us -> 444 us
  local copies, waits for them, and re-layouts: 14.9 us -> 9.27 us
    pallas_call x1, Pallas kernels: 171 us -> 126 us  [experts_turn(): pl.pallas_call(functools.partial(experts_kernel, nz=nz, hidden=pair // 2,...]
    pallas_call x1, Pallas kernels: 133 us -> 160 us  [back(): pl.pallas_call(functools.partial(back_kernel, nz=nz, nf=nf, heads=heads,...]
    pallas_call x1, Pallas kernels: 167 us -> 153 us  [front(): pl.pallas_call(functools.partial(front_kernel, nz=nz, nf=nf, hidden=hidde...]
    unnamed x28 -> x20, local copies, waits for them, and re-layouts: 10.1 us -> 6.58 us
where the time goes in v3:
time: 457 us; the launch traced here: 455 us
  Pallas kernels  444 us (97%)
  local copies, waits for them, and re-layouts  9.27 us (2%)
    pallas_call x1, Pallas kernels, back(): pl.pallas_call(functools.partial(back_kernel, nz=nz, nf=nf, heads=heads,...  160 us
    pallas_call x1, Pallas kernels, front(): pl.pallas_call(functools.partial(front_kernel, nz=nz, nf=nf, hidden=hidde...  153 us
    pallas_call x1, Pallas kernels, experts_turn(): pl.pallas_call(functools.partial(experts_kernel, nz=nz, hidden=pair // 2,...  126 us

profile of v3, /device:TPU:11, one launch (start us, length us, event | category | flops | bytes accessed | tf_op | source)
XLA Modules:
  0.0 455.0 jit_solution(8069222149078627340)
XLA Ops:
  0.7 0.6 compare_convert_fusion.own_ref
  1.3 1.3 copy.26.again_ref.gain_ref
  2.6 1.3 copy.27.fgain_ref
  4.0 153.4 %front.1 = (bf16[2,1280,384]{2,1,0:T(8,128)(2,1)}, bf16[256,1280]{1,0:T(8,128)(2,1)}, bf16[32,40,128]{2,1,0:T(8,128)(2,1)}, bf16[1280,128]{1,0:T(8,128)(2,1)}, f...) custom-call(bf16[128,1280]{1,0:T(8,128)(2,1)} %refs_12_.1, ...), custom_call_target="tpu_custom_call" | custom-call | tf_op jit(solution)/shard_map/front/pallas_call | solution.py:960
  157.4 126.3 %experts_turn.1 = (bf16[4,4,128,1280]{3,2,1,0:T(8,128)(2,1)}, bf16[128,1280]{1,0:T(8,128)(2,1)}, f32[128,1280]{1,0:T(8,128)}, bf16[1280,128]{1,0:T(8,128)(2,1)},...) custom-call(bf16[128,1280]{1,0:T(8,128)(2,1)} %get-tuple-element.54., ...), custom_call_target="tpu_custom_call" | custom-call | tf_op jit(solution)/shard_map/experts_turn/pallas_call | solution.py:1216
  283.7 0.0 copy-start
  283.7 0.0 copy-start.2
  283.7 0.0 copy-start.8
  283.8 0.0 copy-start.9
  283.8 160.3 %back.1 = (bf16[128,1280]{1,0:T(8,128)(2,1)}, bf16[128,1280]{1,0:T(8,128)(2,1)}, f32[40,3840]{1,0:T(8,128)}, f32[40,1280]{1,0:T(8,128)}, bf16[32,40,128]{2,1,0:T(8,128)(2,1)}, /*index=5*/bf16[4,320,896]{2,1,0:T(8,128)(2,1)}) custom-call(bf16[128,1280]{1,0:T(8,128)(2,1)} %get-tuple-element.64.low_ref, bf16[4,320,896]{2,1,0:T(8,128)(2,1)} %get-tuple-element.65.geup_ref, ...), custom_call_target="tpu_custom_call" | custom-call | tf_op jit(solution)/shard_map/back/pallas_call | solution.py:1491
  444.1 0.0 copy-done
  444.1 0.0 copy-done.2
  444.1 0.0 copy-done.8
  444.1 0.0 copy-done.9
  444.2 0.0 copy-start.1
  444.2 1.6 copy-done.1
  445.8 0.0 copy-start.3
  445.8 1.1 copy-done.3
  446.9 0.0 copy-start.4
  446.9 1.0 copy-done.4
  447.8 0.0 copy-start.5
  447.8 1.0 copy-done.5
  448.8 0.0 copy-start.6
  448.8 1.0 copy-done.6
  449.8 0.0 copy-start.7
  449.8 0.9 copy-done.7
  450.7 4.3 unpack.1
  (2 shorter events, 0.0 us)
Async XLA Ops:
  283.7 160.4 %copy-start = (f32[448,1280]{1,0:T(8,128)S(1)}, f32[448,1280]{1,0:T(8,128)}, u32[]{:S(2)}) copy-start(f32[448,1280]{1,0:T(8,128)} %get-tuple-element.84.edown_in) | copy-start | bytes 6881284
  283.7 160.4 %copy-start.2 = (bf16[40,3840]{1,0:T(8,128)(2,1)S(1)}, bf16[40,3840]{1,0:T(8,128)(2,1)}, u32[]{:S(2)}) copy-start(bf16[40,3840]{1,0:T(8,128)(2,1)} %wqkv_ref.3) | copy-start | bytes 921604
  283.7 160.4 %copy-start.8 = (f32[28,1280]{1,0:T(8,128)S(1)}, f32[28,1280]{1,0:T(8,128)}, u32[]{:S(2)}) copy-start(f32[28,1280]{1,0:T(8,128)} %get-tuple-element.85.sdown_in) | copy-start | bytes 430084
  283.8 160.4 %copy-start.9 = (bf16[40,1]{1,0:T(8,128)(2,1)S(1)}, bf16[40,1]{1,0:T(8,128)(2,1)}, u32[]{:S(2)}) copy-start(bf16[40,1]{1,0:T(8,128)(2,1)} %copy.26.again_ref.gain_ref) | copy-start | bytes 244
  444.2 1.6 copy-start.1
  445.8 1.1 copy-start.3
  446.9 1.0 copy-start.4
  447.8 1.0 copy-start.5
  448.8 1.0 copy-start.6
  449.8 0.9 copy-start.7

commit v4 on v3

--- a/solution.py
+++ b/solution.py
@@ -403,6 +403,10 @@
     return jnp.where(j < 2, j, jnp.where(j == 2, nz - 1, j - 1))
 
 
+def spot(ref, piece, f):
+    return ref.at[piece, f // 4, f // 2 % 2, f % 2] if len(ref.shape) == 6 else ref.at[piece, f]
+
+
 class Gather:
     @staticmethod
     def copies(nz):
@@ -413,7 +417,7 @@
 
     def slot(self, j, r, h=None):
         piece = lax.rem(self.z - away(j, self.nz) + self.nz, self.nz) if self.nz > 1 else 0
-        ref = self.buf.at[piece, flip(self.f, r)]
+        ref = spot(self.buf, piece, flip(self.f, r))
         return ref if h is None else ref.at[pl.ds(*halves(self.buf.shape[-2])[h])]
 
     def here(self, j, r, h, index, device):
@@ -618,7 +622,7 @@
     ids_ref[...] = jnp.concatenate([eids_ref[...], seg_ref[...]], axis=0)
     all_ids[me] = ids_ref[...]
     router = router_ref[...].astype(F32).T.astype(BF16)
-    both_gains = jnp.concatenate([again_ref[...], fgain_ref[...]], axis=1)
+    both_gains = jnp.concatenate([again_ref[...].astype(F32).T, fgain_ref[...].astype(F32).T], axis=1).astype(BF16)
 
     def leave(k, src, dst):
         return pltpu.make_async_copy(src, dst, out_sems.at[k])
@@ -1052,7 +1056,7 @@
     out_any, low_ref, gm_ref, small_ref, geup_ref, gedown_ref, gsdown_ref, all_normed_ref,
     out_ref,
     up_ref, upt_ref, down_ref, downt_ref, gup_ref, gdown_ref,
-    xt, gt, mt, px, po, *refs, nz, hidden, shared,
+    xt, gt, px, po, *refs, nz, hidden, shared,
 ):
     bufs, (tile_sems, rs, rr, os_, or_, xs, xr, own_sems) = refs[:4], refs[4:]
     z, f = place()
@@ -1060,7 +1064,7 @@
     half = down_ref.shape[0]
     pair = 2 * hidden
     greet(near_devices(z, f) + z_devices(z, f, nz))
-    own = pltpu.make_async_copy(normed_ref, all_normed_ref.at[z, f], own_sems.at[0])
+    own = pltpu.make_async_copy(normed_ref, spot(all_normed_ref, z, f), own_sems.at[0])
     own.start()
     gather = Gather(all_normed_ref, (xs, xr), nz, z, f)
     reduce = Reduce(bufs, (rs, rr), nz, z, f)
@@ -1074,27 +1078,26 @@
     if nz > 1:
         gather.first(1)
 
+    def where(i):
+        j, t = i // 4, i % 4
+        base = f + (1 - 2 * (f % 2)) * (1 - t // 2) + (4 - 8 * (f // 4 % 2)) * (t % 2)
+        return lax.rem(z - away(j, nz) + nz, nz), base // 4, base % 2
+
     def loads(i, rows_ref=all_normed_ref):
-        j, t, slot = i // 4, i % 4, i % 2
-        piece = lax.rem(z - away(j, nz) + nz, nz)
-        base = f + (1 - 2 * (f % 2)) * (1 - t // 2) + (4 - 8 * (f // 4 % 2)) * (t % 2)
-        copies = []
-        for b in range(2):
-            block = flip(base, 2 * b)
-            there = piece if rows_ref is all_normed_ref else 0
-            copies += [
-                pltpu.make_async_copy(rows_ref.at[there, block], xt.at[slot, b], tile_sems.at[slot, b]),
-                pltpu.make_async_copy(all_grad_ref.at[piece, block], gt.at[slot, b], tile_sems.at[slot, 2 + b]),
-                pltpu.make_async_copy(mark_ref.at[piece, block], mt.at[slot, b], tile_sems.at[slot, 4 + b]),
-            ]
-        return copies
+        piece, y, core = where(i)
+        there = piece if rows_ref is all_normed_ref else 0
+        slot = i % 2
+        return [
+            pltpu.make_async_copy(rows_ref.at[there, y, :, core], xt.at[slot], tile_sems.at[slot, 0]),
+            pltpu.make_async_copy(all_grad_ref.at[piece, y, :, core], gt.at[slot], tile_sems.at[slot, 1]),
+        ]
 
     for copy in loads(0, plane_ref):
         copy.start()
     last = 4 * nz - 1
 
     def tile(i, _):
-        j, t, slot = i // 4, i % 4, i % 2
+        j, t = i // 4, i % 4
         more = j < nz - 1
 
         @pl.when((t == 0) & more)
@@ -1136,14 +1139,17 @@
             for copy in loads(i + 1):
                 copy.start()
 
-        x = xt[slot].reshape(2 * rows, width)
-        g = gt[slot].reshape(2 * rows, width)
+        piece, y, core = where(i)
+        marks = jnp.concatenate([mark_ref[piece, 4 * y + core], mark_ref[piece, 4 * y + 2 + core]], axis=0)
+        x, g = xt[i % 2].reshape(2 * rows, width), gt[i % 2].reshape(2 * rows, width)
         out, gx, grad_pre, acts = ffn_rows(
-            x, g, mt[slot].reshape(2 * rows, HD), own_ref[...], up_ref, upt_ref, down_ref, downt_ref, hidden, shared
-        )
-        at = pl.ds(2 * t, 2)
-        po[at] = out.reshape(2, rows, width)
-        px[at] = gx.reshape(2, rows, width + HD)
+            x, g, marks, own_ref[...], up_ref, upt_ref, down_ref, downt_ref, hidden, shared
+        )
+        x_at = f // 2 % 2
+        for b in range(2):
+            at = 2 * t + (1 - x_at if b else x_at)
+            po[at] = out[b * rows : (b + 1) * rows]
+            px[at] = gx[b * rows : (b + 1) * rows]
         gup_ref[...] += dot_tn(x, grad_pre)
         gdown_ref[...] += dot_tn(acts, g)
 
@@ -1223,9 +1229,9 @@
             jax.ShapeDtypeStruct((nz, width // nz, 2 * pair), BF16),
             jax.ShapeDtypeStruct((pair, width), F32),
             jax.ShapeDtypeStruct((shared, width), F32),
-            jax.ShapeDtypeStruct((nz, 8, rows, width), BF16),
+            jax.ShapeDtypeStruct((nz, 2, 2, 2, rows, width), BF16),
         ),
-        in_specs=[VMEM, ANY, ANY, ANY] + [VMEM] * 10,
+        in_specs=[VMEM, ANY, ANY, VMEM] + [VMEM] * 10,
         out_specs=(ANY, VMEM, VMEM, VMEM, ANY, ANY, VMEM, ANY),
         scratch_shapes=[
             pltpu.VMEM((nz, 4, rows, width), BF16),
@@ -1237,11 +1243,10 @@
             pltpu.VMEM((half, width), F32),
             pltpu.VMEM((2, 2, rows, width), BF16),
             pltpu.VMEM((2, 2, rows, width), BF16),
-            pltpu.VMEM((2, 2, rows, HD), BF16),
             pltpu.VMEM((8, rows, wide), BF16),
             pltpu.VMEM((8, rows, width), BF16),
             *Reduce.scratch(nz, rows, wide),
-            pltpu.SemaphoreType.DMA((2, 6)),
+            pltpu.SemaphoreType.DMA((2, 2)),
             *pair_of(Reduce.copies(nz)),
             *pair_of(Reduce.copies(nz)),
             *pair_of(Gather.copies(nz)),
@@ -1252,7 +1257,8 @@
         ),
         name="experts_turn",
     )(
-        normed, plane, all_grad, marks.reshape(nz, 8, rows, HD), own, eup, tail, edown, sdown, og, mixed, router, own_marks, gain
+        normed, plane.reshape(1, 2, 2, 2, rows, width), all_grad.reshape(nz, 2, 2, 2, rows, width),
+        marks.reshape(nz, 8, rows, HD), own, eup, tail, edown, sdown, og, mixed, router, own_marks, gain
     )[:7]
 
 
@@ -1272,10 +1278,10 @@
     sources, low_ref, geup_ref, wo_ref, w_ref, normed_ref, qkv_ref, attn_ref, lse_ref, cos_ref, sin_ref, segq_ref, segk_ref,
     out_ref, small_ref, tok_ref, mixed_ref, own_gm_ref, gain_ref,
     block_ref, gtok_ref, gwqkv_ref, gwout_ref, all_small_ref, pieces_ref,
-    seq, gkv_ref, gqkv_ref, wt_ref, part_ref, gw_ref, gwo_ref, gws, gwos, smalls, *refs, nz, nf, heads, real,
+    seq, gkv_ref, gqkv_ref, wt_ref, part_ref, gw_ref, gwo_ref, gq, gob, gpk, gz, smalls, *refs, nz, nf, heads, real,
 ):
     bufs, refs = refs[:7], refs[7:]
-    rs, rr, os_, or_, all_s, all_r, wo_s, wo_r, gs, gr, es, er, own_sems, in_sems = refs
+    rs, rr, os_, or_, all_s, all_r, q_s, q_r, wo_s, wo_r, zs, zr, gs, gr, es, er, own_sems, in_sems = refs
     local = (wo_ref, w_ref, normed_ref, qkv_ref, attn_ref, lse_ref, cos_ref, sin_ref, segq_ref, segk_ref, out_ref)
     loads = [pltpu.make_async_copy(src, dst, in_sems.at[k]) for k, (src, dst) in enumerate(zip(sources, local))]
     for copy in loads:
@@ -1306,27 +1312,38 @@
     def two(m):
         return first_head(m + 1) - first_head(m) == 2
 
-    def copies(d, k):
-        device = (d // nf, d % nf)
-        src, dst = ((gw_ref.at[0, d], gws.at[0, me]), (gw_ref.at[1, d], gws.at[1, me]), (small_ref.at[d], smalls.at[me]))[k]
+    def small_copy(d):
         return pltpu.make_async_remote_copy(
-            src, dst, all_s.at[k, d], all_r.at[k, me], device_id=device, device_id_type=MESH
-        )
-
-    def wanted(m, block):
-        low, high = out_blocks(m, dense)
-        return (low <= block) & (block <= high)
+            small_ref.at[d], smalls.at[me], all_s.at[d], all_r.at[me], device_id=(d // nf, d % nf), device_id_type=MESH
+        )
+
+    def small_came(d):
+        return pltpu.make_async_remote_copy(
+            smalls.at[d], smalls.at[d], all_s.at[d], all_r.at[d], device_id=(d // nf, d % nf), device_id_type=MESH
+        )
+
+    def q_copy(p, m, s):
+        return pltpu.make_async_remote_copy(
+            gw_ref.at[s, p * nf + m], gq.at[p, f, s], q_s.at[p, m, s], q_r.at[p, f, s],
+            device_id=(z, m), device_id_type=MESH,
+        )
+
+    def q_came(p, m, s):
+        dst = gq.at[p, m, s]
+        return pltpu.make_async_remote_copy(
+            dst, dst, q_s.at[p, m, s], q_r.at[p, m, s], device_id=(z, m), device_id_type=MESH
+        )
 
     def owner_of(block):
         return head_owner(block * dense // HD)
 
-    low, _ = out_blocks(f, dense)
-
-    def out_copy(d):
-        k = 2 * z + f - owner_of(d)
+    low, high = out_blocks(f, dense)
+
+    def out_copy(i):
+        d = low + i
+        k = 2 * (d // nf) + f - owner_of(d)
         return pltpu.make_async_remote_copy(
-            gwo_ref.at[d - low], gwos.at[k], wo_s.at[d - low], wo_r.at[k],
-            device_id=(d // nf, d % nf), device_id_type=MESH,
+            gwo_ref.at[i], gob.at[k], wo_s.at[i], wo_r.at[k], device_id=(z, d % nf), device_id_type=MESH
         )
 
     for copy in loads[:10]:
@@ -1340,23 +1357,26 @@
     gwo_ref[...] = dot_tn(moved, seq[0].reshape(length, width))[:spare].reshape(gwo_ref.shape).astype(BF16)
 
     def start_small(i, _):
-        d = (me + i) % count
-        copies(d, 2).start()
-
-        @pl.when(wanted(f, d))
-        def _():
-            out_copy(d).start()
-
+        small_copy((me + i) % count).start()
         return 0
 
     lax.fori_loop(1, count, start_small, 0)
-    own_slot = 2 * z + f - owner_of(me)
     smalls[me] = small_ref[me]
 
-    @pl.when(wanted(f, me))
-    def _():
-        gwos[own_slot] = gwo_ref[me - low]
-
+    def start_out(i, _):
+        d = low + i
+
+        @pl.when((d <= high) & (d % nf != f))
+        def _():
+            out_copy(i).start()
+
+        @pl.when((d <= high) & (d % nf == f))
+        def _():
+            gob[2 * (d // nf) + f - owner_of(d)] = gwo_ref[i]
+
+        return 0
+
+    lax.fori_loop(0, gwo_ref.shape[0], start_out, 0)
     gkv_ref[...] = jnp.zeros_like(gkv_ref)
     block = 256
     for i in range(length // block):
@@ -1386,11 +1406,13 @@
         gw_ref[s] = value.reshape(count, dense, step).astype(BF16)
 
         def start(i, _):
-            copies((me + i) % count, s).start()
+            for p in range(nz):
+                q_copy(p, (f + i) % nf, s).start()
             return 0
 
-        lax.fori_loop(1, count, start, 0)
-        gws[s, me] = gw_ref[s, me]
+        lax.fori_loop(1, nf, start, 0)
+        for p in range(nz):
+            gq[p, f, s] = gw_ref[s, p * nf + f]
 
     weights(0)
     for i in range(4):
@@ -1402,11 +1424,61 @@
     def _():
         weights(1)
 
+    reduce.far(0)
+
+    def q_arrive(i, _):
+        m = (f + i) % nf
+        for p in range(nz):
+            q_came(p, m, 0).wait_recv()
+
+        @pl.when(two(m))
+        def _():
+            for p in range(nz):
+                q_came(p, m, 1).wait_recv()
+
+        return 0
+
+    lax.fori_loop(1, nf, q_arrive, 0)
+
+    def arrive_out(k, _):
+        d = (k // 2) * nf + f
+        source = owner_of(d) + k % 2
+        last = head_owner((d * dense + dense - 1) // HD)
+
+        @pl.when((source <= last) & (source != f))
+        def _():
+            pltpu.make_async_remote_copy(
+                gob.at[k], gob.at[k], wo_s.at[0], wo_r.at[k], device_id=(z, flip(f, 1)), device_id_type=MESH
+            ).wait_recv()
+
+        return 0
+
+    lax.fori_loop(0, 2 * nz, arrive_out, 0)
+    for p in range(nz):
+        for m in range(8):
+            for s in range(SLOTS):
+                if real[m * SLOTS + s]:
+                    at = heads[m * SLOTS + s] * HD
+                    for c in range(3):
+                        gpk[p, :, c * width + at : c * width + at + HD] = gq[p, m, s, :, c * HD : (c + 1) * HD]
+        d = p * nf + f
+        gpk[p, :, 3 * width :] = gob[2 * p]
+
+        @pl.when(head_owner((d * dense + dense - 1) // HD) != owner_of(d))
+        def _():
+            gpk[p, :, 3 * width :] = gob[2 * p] + gob[2 * p + 1]
+
+    alongs = []
+    for j in range(1, nz):
+        there = lax.rem(z + j, nz)
+        copy = send(gpk.at[there], gz.at[z], (zs, zr), j, (there, f))
+        copy.start()
+        alongs.append(copy)
+    gz[z] = gpk[z]
     for k in range(length // block, nz):
         outs.far(order[k])
     for k in range(length // block - 1, nz):
         outs.along_z(order[k])
-    reduce.far(0)
     reduce.along_z(0)
     x = tok_ref[...].astype(F32)
     scale = rms_scale(x)
@@ -1415,62 +1487,40 @@
     ).astype(BF16)
     block_ref[...] = (mixed_ref[...] + outs.total()).astype(BF16)
 
-    owner = owner_of(me)
-    next_owner = head_owner((me * dense + dense - 1) // HD)
-    for k in range(2 * nz):
-        there = (k // 2 != z) | (f != owner + k % 2)
-        if k % 2:
-            there = there & (next_owner != owner)
-
-        @pl.when(there)
-        def _():
-            pltpu.make_async_remote_copy(
-                gwo_ref.at[0], gwos.at[k], wo_s.at[0], wo_r.at[k], device_id=(z, flip(f, 1)), device_id_type=MESH
-            ).wait_recv()
-
-    gwout_ref[...] = sum(gwos[2 * t].astype(F32) for t in range(nz))
-
-    @pl.when(next_owner != owner)
-    def _():
-        gwout_ref[...] += sum(gwos[2 * t + 1].astype(F32) for t in range(nz))
-
-    def came(d, k):
-        dst = (gws.at[0, d], gws.at[1, d], smalls.at[d])[k]
-        return pltpu.make_async_remote_copy(
-            dst, dst, all_s.at[k, d], all_r.at[k, d], device_id=(d // nf, d % nf), device_id_type=MESH
-        )
-
     def finish(i, _):
         d = (me + i) % count
-        came(d, 0).wait_recv()
-
-        @pl.when(two(d % nf))
-        def _():
-            came(d, 1).wait_recv()
-
-        came(d, 2).wait_recv()
-        copies(d, 0).wait_send()
+        small_came(d).wait_recv()
+        small_copy(d).wait_send()
+        return 0
+
+    lax.fori_loop(1, count, finish, 0)
+
+    def q_left(i, _):
+        m = (f + i) % nf
+        for p in range(nz):
+            q_copy(p, m, 0).wait_send()
 
         @pl.when(two(f))
         def _():
-            copies(d, 1).wait_send()
-
-        copies(d, 2).wait_send()
-
-        @pl.when(wanted(f, d))
-        def _():
-            out_copy(d).wait_send()
+            for p in range(nz):
+                q_copy(p, m, 1).wait_send()
 
         return 0
 
-    lax.fori_loop(1, count, finish, 0)
-    for m in range(8):
-        for s in range(SLOTS):
-            if real[m * SLOTS + s]:
-                h = heads[m * SLOTS + s]
-                both = sum(gws[s, t * nf + m].astype(F32) for t in range(nz))
-                for c in range(3):
-                    gwqkv_ref[:, c * width + h * HD : c * width + (h + 1) * HD] = both[:, c * HD : (c + 1) * HD]
+    lax.fori_loop(1, nf, q_left, 0)
+
+    def out_left(i, _):
+        @pl.when((low + i <= high) & ((low + i) % nf != f))
+        def _():
+            out_copy(i).wait_send()
+
+        return 0
+
+    lax.fori_loop(0, gwo_ref.shape[0], out_left, 0)
+    for copy in alongs:
+        copy.wait()
+    gwqkv_ref[...] = sum(gz[p, :, : 3 * width].astype(F32) for p in range(nz))
+    gwout_ref[...] = sum(gz[p, :, 3 * width :].astype(F32) for p in range(nz))
     all_small_ref[...] = smalls[...]
     for i in range(4):
         reduce.core(0, i, part_ref.at[0]).wait_send()
@@ -1508,17 +1558,21 @@
             pltpu.VMEM((8, rows, width), BF16),
             pltpu.VMEM((SLOTS, count, dense, 3 * HD), BF16),
             pltpu.VMEM((8, dense, width), BF16),
-            pltpu.VMEM((SLOTS, count, dense, 3 * HD), BF16),
+            pltpu.VMEM((nz, 8, SLOTS, dense, 3 * HD), BF16),
             pltpu.VMEM((2 * nz, dense, width), BF16),
+            pltpu.VMEM((nz, dense, 4 * width), BF16),
+            pltpu.VMEM((nz, dense, 4 * width), BF16),
             pltpu.VMEM((count, dense, HD), BF16),
             *Reduce.scratch(1, rows, width),
             *Reduce.scratch(nz, rows, width)[1:],
             *pair_of(Reduce.copies(1)),
             *pair_of(Reduce.copies(nz)),
-            pltpu.SemaphoreType.DMA((3, count)),
-            pltpu.SemaphoreType.DMA((3, count)),
+            *pair_of(count),
+            pltpu.SemaphoreType.DMA((nz, 8, SLOTS)),
+            pltpu.SemaphoreType.DMA((nz, 8, SLOTS)),
             pltpu.SemaphoreType.DMA((8,)),
             pltpu.SemaphoreType.DMA((2 * nz,)),
+            *pair_of(nz),
             *pair_of(Gather.copies(1)),
             *pair_of(nz),
             pltpu.SemaphoreType.DMA((1,)),
@@ -1562,7 +1616,7 @@
             to = (g * count + d) * shared
             gsup_ref[:, to : to + shared] = small_ref[d, :, g * TAIL : g * TAIL + shared].astype(F32)
     grouter_ref[...] = total[:, shared : shared + experts].T
-    one = jnp.sum(wqkv_ref[...].astype(F32) * gwqkv_ref[...], axis=-1, keepdims=True) / gain_ref[...].astype(F32)
+    one = jnp.sum(wqkv_ref[...].astype(F32) * gwqkv_ref[...], axis=-1, keepdims=True) / gain_ref[...].astype(F32).T
     gone_ref[...] = one.T
     gtwo_ref[...] = total[:, HD - 1 :].T
 
@@ -1610,7 +1664,7 @@
         w, wo, tail, router, gain_one, gain_two, marks, own_marks, segq, segk, normed_one, qkv, attn, lse, mixed, normed,
         plane, all_grad, pieces,
     ) = front(
-        tokens, w_qkv, w_out, w_router.T, w_shared_up, attn_gain[:, None], ffn_gain[:, None], expert_ids.T,
+        tokens, w_qkv, w_out, w_router.T, w_shared_up, attn_gain[None], ffn_gain[None], expert_ids.T,
         segment_ids[None], cosine, sine, out_grad, w_expert_up, nz, nf, shared,
     )
     tail = tail.reshape(width, 2 * TAIL)
@@ -1627,7 +1681,7 @@
     (
         grad_eup, grad_sup, grad_router, grad_one, grad_two, block_out, tokens_grad, grad_wqkv, grad_wout, gedown, gsdown,
     ) = unpack(
-        gpieces, smalls, w_qkv, grad_wqkv, attn_gain[:, None], (block_out, tokens_grad, grad_wout, gedown, gsdown),
+        gpieces, smalls, w_qkv, grad_wqkv, attn_gain[None], (block_out, tokens_grad, grad_wout, gedown, gsdown),
         shared, experts,
     )
     return (

time: 457 us -> 440 us (0.963)
  Pallas kernels: 444 us -> 428 us
    pallas_call x1, Pallas kernels: 160 us -> 141 us  [back(): pl.pallas_call(functools.partial(back_kernel, nz=nz, nf=nf, heads=heads,...]
where the time goes in v4:
time: 440 us; the launch traced here: 436 us
  Pallas kernels  428 us (97%)
  local copies, waits for them, and re-layouts  6.58 us (1%)
    pallas_call x1, Pallas kernels, front(): pl.pallas_call(functools.partial(front_kernel, nz=nz, nf=nf, hidden=hidde...  153 us
    pallas_call x1, Pallas kernels, back(): pl.pallas_call(functools.partial(back_kernel, nz=nz, nf=nf, heads=heads,...  141 us
    pallas_call x1, Pallas kernels, experts_turn(): pl.pallas_call(functools.partial(experts_kernel, nz=nz, hidden=pair // 2,...  130 us

profile of v4, /device:TPU:11, one launch (start us, length us, event | category | flops | bytes accessed | tf_op | source)
XLA Modules:
  0.0 436.3 jit_solution(11661427971280853157)
XLA Ops:
  0.7 0.6 compare_convert_fusion.own_ref
  1.3 153.4 %front.1 = (bf16[2,1280,384]{2,1,0:T(8,128)(2,1)}, bf16[256,1280]{1,0:T(8,128)(2,1)}, bf16[32,40,128]{2,1,0:T(8,128)(2,1)}, bf16[1280,128]{1,0:T(8,128)(2,1)}, f...) custom-call(bf16[128,1280]{1,0:T(8,128)(2,1)} %refs_12_.1, ...), custom_call_target="tpu_custom_call" | custom-call | tf_op jit(solution)/shard_map/front/pallas_call | solution.py:964
  154.7 129.7 %experts_turn.1 = (bf16[4,4,128,1280]{3,2,1,0:T(8,128)(2,1)}, bf16[128,1280]{1,0:T(8,128)(2,1)}, f32[128,1280]{1,0:T(8,128)}, bf16[1280,128]{1,0:T(8,128)(2,1)},...) custom-call(bf16[128,1280]{1,0:T(8,128)(2,1)} %get-tuple-element.54., ...), custom_call_target="tpu_custom_call" | custom-call | tf_op jit(solution)/shard_map/experts_turn/pallas_call | solution.py:1222
  284.4 0.0 copy-start
  284.4 0.0 copy-start.2
  284.5 0.0 copy-start.8
  284.5 0.0 copy-start.9
  284.5 140.9 %back.1 = (bf16[128,1280]{1,0:T(8,128)(2,1)}, bf16[128,1280]{1,0:T(8,128)(2,1)}, f32[40,3840]{1,0:T(8,128)}, f32[40,1280]{1,0:T(8,128)}, bf16[32,40,128]{2,1,0:T(8,128)(2,1)}, /*index=5*/bf16[4,320,896]{2,1,0:T(8,128)(2,1)}) custom-call(bf16[128,1280]{1,0:T(8,128)(2,1)} %get-tuple-element.64.low_ref, bf16[4,320,896]{2,1,0:T(8,128)(2,1)} %get-tuple-element.65.geup_ref, ...), custom_call_target="tpu_custom_call" | custom-call | tf_op jit(solution)/shard_map/back/pallas_call | solution.py:1541
  425.4 0.0 copy-done
  425.4 0.0 copy-done.2
  425.4 0.0 copy-done.8
  425.4 0.0 copy-done.9
  425.4 0.0 copy-start.1
  425.4 1.6 copy-done.1
  427.1 0.0 copy-start.3
  427.1 1.1 copy-done.3
  428.1 0.0 copy-start.4
  428.1 1.0 copy-done.4
  429.1 0.0 copy-start.5
  429.1 1.0 copy-done.5
  430.1 0.0 copy-start.6
  430.1 1.0 copy-done.6
  431.0 0.0 copy-start.7
  431.0 0.9 copy-done.7
  432.0 4.3 unpack.1
  (2 shorter events, 0.0 us)
Async XLA Ops:
  284.4 140.9 %copy-start = (f32[448,1280]{1,0:T(8,128)S(1)}, f32[448,1280]{1,0:T(8,128)}, u32[]{:S(2)}) copy-start(f32[448,1280]{1,0:T(8,128)} %get-tuple-element.84.edown_in) | copy-start | bytes 6881284
  284.4 140.9 %copy-start.2 = (bf16[40,3840]{1,0:T(8,128)(2,1)S(1)}, bf16[40,3840]{1,0:T(8,128)(2,1)}, u32[]{:S(2)}) copy-start(bf16[40,3840]{1,0:T(8,128)(2,1)} %wqkv_ref.3) | copy-start | bytes 921604
  284.5 140.9 %copy-start.8 = (f32[28,1280]{1,0:T(8,128)S(1)}, f32[28,1280]{1,0:T(8,128)}, u32[]{:S(2)}) copy-start(f32[28,1280]{1,0:T(8,128)} %get-tuple-element.85.sdown_in) | copy-start | bytes 430084
  284.5 140.9 %copy-start.9 = (bf16[40]{0:T(256)(128)(2,1)S(1)}, bf16[40]{0:T(256)(128)(2,1)}, u32[]{:S(2)}) copy-start(bf16[40]{0:T(256)(128)(2,1)} %param.19) | copy-start | bytes 244
  425.4 1.6 copy-start.1
  427.1 1.1 copy-start.3
  428.1 1.0 copy-start.4
  429.1 1.0 copy-start.5
  430.1 1.0 copy-start.6
  431.0 0.9 copy-start.7

commit v5 on v4

--- a/solution.py
+++ b/solution.py
@@ -1385,11 +1385,11 @@
         )
         if i + 1 < nz:
             outs.send_near(order[i + 1])
-        if i < nz:
-            outs.far(order[i])
-        if 0 < i <= nz:
-            outs.along_z(order[i - 1])
     attn_back_keys(w_ref, cos_ref, sin_ref, gkv_ref, gqkv_ref, wt_ref)
+    if nz > 0:
+        outs.far(order[0])
+    if nz > 1:
+        outs.far(order[1])
     step = 3 * HD
     reduce = Reduce(bufs[:4], (rs, rr), 1, z, f)
     for i in range(length // block):
@@ -1400,6 +1400,10 @@
         )
     for i in range(4):
         reduce.core(0, i, part_ref.at[flip(f, 1 | 2 * i)]).start()
+    if nz > 2:
+        outs.far(order[2])
+    if nz > 3:
+        outs.far(order[3])
 
     def weights(s):
         value = dot_tn(normed_ref[...], gqkv_ref[:, s * step : (s + 1) * step])
@@ -1419,12 +1423,20 @@
         reduce.core(0, i, None).wait_recv()
         reduce.by_core[0, i] = reduce.by_core[0, i] + part_ref[flip(f, 2 * i)]
     reduce.send_near(0)
+    if nz > 0:
+        outs.along_z(order[0])
+    if nz > 1:
+        outs.along_z(order[1])
 
     @pl.when(two(f))
     def _():
         weights(1)
 
+    if nz > 2:
+        outs.along_z(order[2])
     reduce.far(0)
+    if nz > 3:
+        outs.along_z(order[3])
 
     def q_arrive(i, _):
         m = (f + i) % nf
@@ -1475,10 +1487,6 @@
         copy.start()
         alongs.append(copy)
     gz[z] = gpk[z]
-    for k in range(length // block, nz):
-        outs.far(order[k])
-    for k in range(length // block - 1, nz):
-        outs.along_z(order[k])
     reduce.along_z(0)
     x = tok_ref[...].astype(F32)
     scale = rms_scale(x)
@@ -1636,7 +1644,7 @@
         ),
         in_specs=[VMEM] * 10,
         out_specs=(VMEM,) * 11,
-        compiler_params=pltpu.CompilerParams(vmem_limit_bytes=40 * 2**20),
+        compiler_params=pltpu.CompilerParams(vmem_limit_bytes=60 * 2**20),
         name="unpack",
     )(pieces, small, wqkv, gwqkv, gain, *rest)
 

time: 440 us -> 434 us (0.986)
  local copies, waits for them, and re-layouts: 6.58 us -> 0 us
    unnamed x20 -> x0, local copies, waits for them, and re-layouts: 6.58 us -> none
where the time goes in v5:
time: 434 us; the launch traced here: 430 us
  Pallas kernels  428 us (99%)
    pallas_call x1, Pallas kernels, front(): pl.pallas_call(functools.partial(front_kernel, nz=nz, nf=nf, hidden=hidde...  153 us
    pallas_call x1, Pallas kernels, back(): pl.pallas_call(functools.partial(back_kernel, nz=nz, nf=nf, heads=heads,...  138 us
    pallas_call x1, Pallas kernels, experts_turn(): pl.pallas_call(functools.partial(experts_kernel, nz=nz, hidden=pair // 2,...  130 us

profile of v5, /device:TPU:11, one launch (start us, length us, event | category | flops | bytes accessed | tf_op | source)
XLA Modules:
  0.0 429.7 jit_solution(3889317649153068381)
XLA Ops:
  0.7 0.6 compare_convert_fusion.own_ref
  1.3 153.4 %front.1 = (bf16[2,1280,384]{2,1,0:T(8,128)(2,1)}, bf16[256,1280]{1,0:T(8,128)(2,1)}, bf16[32,40,128]{2,1,0:T(8,128)(2,1)}, bf16[1280,128]{1,0:T(8,128)(2,1)}, f...) custom-call(bf16[128,1280]{1,0:T(8,128)(2,1)} %refs_12_.1, ...), custom_call_target="tpu_custom_call" | custom-call | tf_op jit(solution)/shard_map/front/pallas_call | solution.py:964
  154.7 129.8 %experts_turn.1 = (bf16[4,4,128,1280]{3,2,1,0:T(8,128)(2,1)}, bf16[128,1280]{1,0:T(8,128)(2,1)}, f32[128,1280]{1,0:T(8,128)}, bf16[1280,128]{1,0:T(8,128)(2,1)},...) custom-call(bf16[128,1280]{1,0:T(8,128)(2,1)} %get-tuple-element.54., ...), custom_call_target="tpu_custom_call" | custom-call | tf_op jit(solution)/shard_map/experts_turn/pallas_call | solution.py:1222
  284.5 137.9 %back.1 = (bf16[128,1280]{1,0:T(8,128)(2,1)}, bf16[128,1280]{1,0:T(8,128)(2,1)}, f32[40,3840]{1,0:T(8,128)}, f32[40,1280]{1,0:T(8,128)}, bf16[32,40,128]{2,1,0:T(8,128)(2,1)}, /*index=5*/bf16[4,320,896]{2,1,0:T(8,128)(2,1)}) custom-call(bf16[128,1280]{1,0:T(8,128)(2,1)} %get-tuple-element.64.low_ref, bf16[4,320,896]{2,1,0:T(8,128)(2,1)} %get-tuple-element.65.geup_ref, ...), custom_call_target="tpu_custom_call" | custom-call | tf_op jit(solution)/shard_map/back/pallas_call | solution.py:1549
  422.4 7.4 %unpack.1 = (f32[2,320,1792]{2,1,0:T(8,128)}, f32[40,1792]{1,0:T(8,128)}, f32[16,40]{1,0:T(8,128)}, f32[1,40]{1,0:T(1,128)}, f32[1,40]{1,0:T(1,128)}, /*index=5*...) custom-call(bf16[4,320,896]{2,1,0:T(8,128)(2,1)} %get-tuple-element., ...), custom_call_target="tpu_custom_call" | custom-call | tf_op jit(solution)/shard_map/unpack/pallas_call | solution.py:1635
  (2 shorter events, 0.0 us)

commit v6 on v5

--- a/solution.py
+++ b/solution.py
@@ -412,7 +412,8 @@
     def copies(nz):
         return 11 * nz
 
-    def __init__(self, buf, sems, nz, z, f):
+    def __init__(self, buf, sems, nz, z, f, own=None):
+        self.own = own
         self.buf, self.sems, self.nz, self.z, self.f = buf, sems, nz, z, f
 
     def slot(self, j, r, h=None):
@@ -422,11 +423,15 @@
 
     def here(self, j, r, h, index, device):
         ref = self.slot(j, r, h)
-        return send(ref, ref, self.sems, index, device)
+        src = ref
+        if self.own is not None and isinstance(j, int) and j == 0 and r == 0:
+            src = self.own if h is None else self.own.at[pl.ds(*halves(self.own.shape[-2])[h])]
+        return send(src, ref, self.sems, index, device)
 
     def by_z(self, j):
         own = self.slot(0, 0)
-        return send(own, own, self.sems, j, (lax.rem(self.z + away(j, self.nz), self.nz), self.f))
+        src = own if self.own is None else self.own
+        return send(src, own, self.sems, j, (lax.rem(self.z + away(j, self.nz), self.nz), self.f))
 
     def near(self, j, h):
         return self.here(j, 0, h, self.nz + 2 * j + h, (self.z, flip(self.f, ORDER[h][0])))
@@ -591,11 +596,11 @@
 
 
 def front_kernel(
-    tok_ref, wqkv_ref, wout_ref, router_ref, sup_ref, again_ref, fgain_ref, eids_ref, seg_ref, cos_ref, sin_ref, og_ref,
-    eup_ref,
+    tok_ref, wqkv_ref, wout_ref, router_ref, sup_ref, again_ref, fgain_ref, eids_ref, seg_ref, cos_in, sin_in, og_ref,
+    eup_in,
     w_out, wo_ref, tail_out, router_out, gain_one_ref, gain_two_ref, mark_out, own_mark_ref, segq_ref, segk_ref,
     normed_out, qkv_out, attn_out, lse_out, mixed_ref, low_ref, plane_ref, all_grad_ref, pieces_ref,
-    w_ref, tail_ref, mark_ref, normed_ref, qkv_ref, attn_ref, lse_ref, ids_ref, out_sems,
+    w_ref, tail_ref, mark_ref, normed_ref, qkv_ref, attn_ref, lse_ref, ids_ref, cos_ref, sin_ref, eup_ref, out_sems,
     seq, wq, wo_in, wz, wzo, all_ids, qpack, tpack, part, wide, pack, *refs, nz, nf, hidden, shared, heads, real,
 ):
     bufs, refs = refs[:4], refs[4:]
@@ -609,6 +614,12 @@
     dense = wqkv_ref.shape[0]
     experts = router_ref.shape[0]
     full = shared * count
+    loads = [
+        pltpu.make_async_copy(src, dst, out_sems.at[7 + k])
+        for k, (src, dst) in enumerate(((eup_in, eup_ref), (cos_in, cos_ref), (sin_in, sin_ref)))
+    ]
+    for copy in loads:
+        copy.start()
     greet_all(nz, nf)
 
     toks = (tok_s, tok_r)
@@ -690,6 +701,8 @@
         return 0
 
     whole = nz * hidden
+    for copy in loads:
+        copy.wait()
     for t in range(nz):
         pack[t] = jnp.concatenate(
             [
@@ -892,8 +905,7 @@
     low_ref[...] = (mixed * rms_scale(mixed) * gain_two_ref[...]).astype(BF16)
     near_own = pltpu.make_async_copy(low_ref, plane_ref.at[0, f], own_sems.at[1])
     near_own.start()
-    near = Gather(plane_ref, (xs, xr), 1, z, f)
-    near_own.wait()
+    near = Gather(plane_ref, (xs, xr), 1, z, f, own=low_ref)
     near.first(0, own=True)
     for j in range(1, nz):
         grads.first(j)
@@ -950,7 +962,7 @@
         grads.by_z(j).wait_send()
     grads.end()
     near.end()
-    for copy in ups + outgoing:
+    for copy in ups + outgoing + [near_own]:
         copy.wait()
 
 
@@ -984,7 +996,7 @@
             shape((nz, 8, rows, width), BF16),
             shape((nz, up_rows, 4 * hidden), BF16),
         ),
-        in_specs=[VMEM] * 13,
+        in_specs=[VMEM] * 9 + [ANY] * 2 + [VMEM, ANY],
         out_specs=(ANY, VMEM, ANY, VMEM, VMEM, VMEM, ANY, VMEM, VMEM, VMEM) + (ANY,) * 4 + (VMEM,) * 2 + (ANY,) * 3,
         scratch_shapes=[
             pltpu.VMEM((SLOTS, width, 3 * HD), BF16),
@@ -995,7 +1007,10 @@
             pltpu.VMEM((length, SLOTS * HD), BF16),
             pltpu.VMEM((length, SLOTS * HD), F32),
             pltpu.VMEM((eids.shape[0] + 1, rows), jnp.int32),
-            pltpu.SemaphoreType.DMA((7,)),
+            pltpu.VMEM(cosine.shape, F32),
+            pltpu.VMEM(sine.shape, F32),
+            pltpu.VMEM(eup.shape, BF16),
+            pltpu.SemaphoreType.DMA((10,)),
             pltpu.VMEM((8, rows, width), BF16),
             pltpu.VMEM((SLOTS, count, dense, 3 * HD), BF16),
             pltpu.VMEM((8, dense, width), BF16),
@@ -1051,26 +1066,31 @@
 
 
 def experts_kernel(
-    normed_ref, plane_ref, all_grad_ref, mark_ref, own_ref, eup_ref, tail_ref, edown_ref, sdown_ref,
+    normed_ref, plane_ref, all_grad_ref, mark_in, own_ref, eup_in, tail_ref, edown_in, sdown_ref,
     og_ref, mixed_ref, router_ref, own_mark_ref, gain_ref,
     out_any, low_ref, gm_ref, small_ref, geup_ref, gedown_ref, gsdown_ref, all_normed_ref,
     out_ref,
     up_ref, upt_ref, down_ref, downt_ref, gup_ref, gdown_ref,
-    xt, gt, px, po, *refs, nz, hidden, shared,
+    xt, gt, px, po, mark_ref, eup_ref, edown_ref, *refs, nz, hidden, shared,
 ):
     bufs, (tile_sems, rs, rr, os_, or_, xs, xr, own_sems) = refs[:4], refs[4:]
     z, f = place()
     rows, width = mixed_ref.shape
     half = down_ref.shape[0]
     pair = 2 * hidden
+    starts = [
+        pltpu.make_async_copy(src, dst, own_sems.at[k])
+        for k, (src, dst) in enumerate(((eup_in, eup_ref), (edown_in, edown_ref), (mark_in, mark_ref)))
+    ]
+    for copy in starts:
+        copy.start()
     greet(near_devices(z, f) + z_devices(z, f, nz))
-    own = pltpu.make_async_copy(normed_ref, spot(all_normed_ref, z, f), own_sems.at[0])
-    own.start()
-    gather = Gather(all_normed_ref, (xs, xr), nz, z, f)
+    gather = Gather(all_normed_ref, (xs, xr), nz, z, f, own=normed_ref)
+    gather.along_z(1)
     reduce = Reduce(bufs, (rs, rr), nz, z, f)
     outs = Reduce([out_ref, out_ref, out_ref, out_ref], (os_, or_), nz, z, f)
-    own.wait()
-    gather.along_z(1)
+    for copy in starts:
+        copy.wait()
     ffn_weights(eup_ref, tail_ref, edown_ref, sdown_ref, up_ref, upt_ref, down_ref, downt_ref)
     gup_ref[...] = jnp.zeros_like(gup_ref)
     gdown_ref[...] = jnp.zeros_like(gdown_ref)
@@ -1231,7 +1251,7 @@
             jax.ShapeDtypeStruct((shared, width), F32),
             jax.ShapeDtypeStruct((nz, 2, 2, 2, rows, width), BF16),
         ),
-        in_specs=[VMEM, ANY, ANY, VMEM] + [VMEM] * 10,
+        in_specs=[VMEM, ANY, ANY, ANY, VMEM, ANY, VMEM, ANY] + [VMEM] * 6,
         out_specs=(ANY, VMEM, VMEM, VMEM, ANY, ANY, VMEM, ANY),
         scratch_shapes=[
             pltpu.VMEM((nz, 4, rows, width), BF16),
@@ -1245,12 +1265,15 @@
             pltpu.VMEM((2, 2, rows, width), BF16),
             pltpu.VMEM((8, rows, wide), BF16),
             pltpu.VMEM((8, rows, width), BF16),
+            pltpu.VMEM((nz, 8, rows, HD), BF16),
+            pltpu.VMEM(eup.shape, BF16),
+            pltpu.VMEM(edown.shape, BF16),
             *Reduce.scratch(nz, rows, wide),
             pltpu.SemaphoreType.DMA((2, 2)),
             *pair_of(Reduce.copies(nz)),
             *pair_of(Reduce.copies(nz)),
             *pair_of(Gather.copies(nz)),
-            pltpu.SemaphoreType.DMA((nz + 2,)),
+            pltpu.SemaphoreType.DMA((nz + 3,)),
         ],
         compiler_params=pltpu.CompilerParams(
             collective_id=3, has_side_effects=True, vmem_limit_bytes=60 * 2**20

time: 434 us -> 432 us (level)
  no operation moved by 1% of the time
where the time goes in v6:
time: 432 us; the launch traced here: 427 us
  Pallas kernels  426 us (99%)
    pallas_call x1, Pallas kernels, front(): pl.pallas_call(functools.partial(front_kernel, nz=nz, nf=nf, hidden=hidde...  151 us
    pallas_call x1, Pallas kernels, back(): pl.pallas_call(functools.partial(back_kernel, nz=nz, nf=nf, heads=heads,...  139 us
    pallas_call x1, Pallas kernels, experts_turn(): pl.pallas_call(functools.partial(experts_kernel, nz=nz, hidden=pair // 2,...  128 us

profile of v6, /device:TPU:11, one launch (start us, length us, event | category | flops | bytes accessed | tf_op | source)
XLA Modules:
  0.0 427.3 jit_solution(7825234548654166535)
XLA Ops:
  0.7 0.6 compare_convert_fusion.own_ref
  1.3 151.5 %front.1 = (bf16[2,1280,384]{2,1,0:T(8,128)(2,1)}, bf16[256,1280]{1,0:T(8,128)(2,1)}, bf16[32,40,128]{2,1,0:T(8,128)(2,1)}, bf16[1280,128]{1,0:T(8,128)(2,1)}, f...) custom-call(bf16[128,1280]{1,0:T(8,128)(2,1)} %refs_12_.1, ...), custom_call_target="tpu_custom_call" | custom-call | tf_op jit(solution)/shard_map/front/pallas_call | solution.py:976
  152.8 128.4 %experts_turn.1 = (bf16[4,4,128,1280]{3,2,1,0:T(8,128)(2,1)}, bf16[128,1280]{1,0:T(8,128)(2,1)}, f32[128,1280]{1,0:T(8,128)}, bf16[1280,128]{1,0:T(8,128)(2,1)},...) custom-call(bf16[128,1280]{1,0:T(8,128)(2,1)} %get-tuple-element.54., ...), custom_call_target="tpu_custom_call" | custom-call | tf_op jit(solution)/shard_map/experts_turn/pallas_call | solution.py:1242
  281.2 138.7 %back.1 = (bf16[128,1280]{1,0:T(8,128)(2,1)}, bf16[128,1280]{1,0:T(8,128)(2,1)}, f32[40,3840]{1,0:T(8,128)}, f32[40,1280]{1,0:T(8,128)}, bf16[32,40,128]{2,1,0:T(8,128)(2,1)}, /*index=5*/bf16[4,320,896]{2,1,0:T(8,128)(2,1)}) custom-call(bf16[128,1280]{1,0:T(8,128)(2,1)} %get-tuple-element.64.low_ref, bf16[4,320,896]{2,1,0:T(8,128)(2,1)} %get-tuple-element.65.geup_ref, ...), custom_call_target="tpu_custom_call" | custom-call | tf_op jit(solution)/shard_map/back/pallas_call | solution.py:1572
  419.9 7.4 %unpack.1 = (f32[2,320,1792]{2,1,0:T(8,128)}, f32[40,1792]{1,0:T(8,128)}, f32[16,40]{1,0:T(8,128)}, f32[1,40]{1,0:T(1,128)}, f32[1,40]{1,0:T(1,128)}, /*index=5*...) custom-call(bf16[4,320,896]{2,1,0:T(8,128)(2,1)} %get-tuple-element., ...), custom_call_target="tpu_custom_call" | custom-call | tf_op jit(solution)/shard_map/unpack/pallas_call | solution.py:1658
  (2 shorter events, 0.0 us)
